TPU v7x, 256 devices: a whole 4x4x8 slice. The times are simulated.
256 devices in a mesh: cache: 16 (over x, y), heads: 16 (over z, core).
Axes of the slice: x: 4, y: 4, z: 8, core: 2. Of those that a mesh axis runs over, the one named last changes fastest.
Arguments:
- hidden: bfloat16 [3072, 8192], P('cache'), may hold values from -6 to 6
- norm_gain: bfloat16 [8192], replicated, may hold values from 0.099609375 to 1.8984375
- q_weight: bfloat16 [8192, 8192], P('cache', 'heads'), may hold values from -0.0625 to 0.0625
- q_bias: bfloat16 [8192], P('heads'), may hold values from -4 to 4
- kv_weight: bfloat16 [8192, 2048], P('cache'), may hold values from -0.0625 to 0.0625
- kv_bias: bfloat16 [2048], replicated, may hold values from -4 to 4
- out_weight: bfloat16 [8192, 8192], P('heads', 'cache'), may hold values from -0.0625 to 0.0625
- kv_store: bfloat16 [128, 16, 512, 256], P('cache', 'heads'), as said below
- stretch_place: int32 [128], replicated, may hold values from 0 to 127, as said below
- req_stretches: int32 [16, 8], replicated, may hold values from 0 to 127, as said below
- rec_rows: int32 [16, 8, 24], replicated, may hold values from 0 to 511, as said below
Outputs:
- attn_out: bfloat16 [3072, 8192], P('cache', 'heads')
- new_store: bfloat16 [128, 16, 512, 256], P('cache', 'heads')
Inputs may be any that keep to these rules, and one draw needn't show every extreme that they name: `req_stretches`: each stretch stands in exactly one request; among the stretches of one request at most 2 have the same owner, and in every request some owner has exactly 2. `stretch_place`: A permutation of the slots; each owner holds 8 stretches. `rec_rows`: distinct and increasing within each stretch. `kv_store`: entries g and g2 of the second dimension are equal when g // 2 == g2 // 2.
All inputs are finite; a program needn't handle non-finite values.
Results may differ from a plain program's by a relative error of at most 0.023.
The roundings to bfloat16 on the way count: a program that leaves them out, or rounds other values in their place, can miss the bound.
Values may be sent and summed in bfloat16 or wider, within the bound.
A program may use at most 128 MiB of HBM per device.

v0:
```python
import math

import jax
import jax.numpy as jnp
from jax import lax
from jax.sharding import PartitionSpec as P


def rms_norm(hidden, norm_gain):
    values = hidden.astype(jnp.float32)
    factor = lax.rsqrt(jnp.mean(values * values, axis=-1, keepdims=True) + 1e-06)
    return (values * factor * norm_gain.astype(jnp.float32)).astype(jnp.bfloat16)


def shards(
    hidden,
    norm_gain,
    q_weight,
    q_bias,
    kv_weight,
    kv_bias,
    out_weight,
    kv_store,
    stretch_place,
    req_stretches,
    rec_rows,
):
    owners = lax.axis_size("cache")
    self_index = lax.axis_index("cache")
    head_count = lax.axis_size("heads")
    head_index = lax.axis_index("heads")
    rows_dev = hidden.shape[0]
    stretch_count = kv_store.shape[0]
    kv_width = kv_store.shape[3]
    head_dim = kv_width // 2
    per_stretch = rec_rows.shape[2]
    capacity = (stretch_count + owners - 1) // owners + 1
    query_width = q_weight.shape[1]
    heads_here = query_width // head_dim
    kv_heads = kv_weight.shape[1] // kv_width
    shared = head_count // kv_heads
    kv_head = head_index // shared
    kv_columns = lax.dynamic_slice_in_dim(kv_weight, kv_head * kv_width, kv_width, 1)
    kv_bias_here = lax.dynamic_slice_in_dim(kv_bias, kv_head * kv_width, kv_width, 0)
    normed = rms_norm(hidden, norm_gain)
    slices = lax.all_to_all(normed, "cache", split_axis=1, concat_axis=0, tiled=True)
    mixed = lax.psum_scatter(
        jnp.concatenate(
            [
                jnp.dot(slices, q_weight, preferred_element_type=jnp.float32),
                jnp.dot(slices, kv_columns, preferred_element_type=jnp.float32),
            ],
            axis=1,
        ),
        "cache",
        scatter_dimension=0,
        tiled=True,
    )
    q_mixed = mixed[:, :query_width]
    kv_mixed = mixed[:, query_width:]
    queries = (q_mixed + q_bias.astype(jnp.float32)).astype(jnp.bfloat16)
    fresh = (kv_mixed + kv_bias_here.astype(jnp.float32)).astype(jnp.bfloat16)
    fresh_blocks = fresh.reshape(stretch_count, per_stretch, kv_width)
    places = stretch_place[req_stretches]
    owner_of = places // stretch_count
    slot_of = places % stretch_count
    same_owner = owner_of[:, :, None] == owner_of[:, None, :]
    earlier = jnp.arange(stretch_count)[None, :] < jnp.arange(stretch_count)[:, None]
    rank_of = jnp.sum(same_owner & earlier[None], axis=2)
    mine = owner_of == self_index
    picked = mine[:, :, None] & (rank_of[:, :, None] == jnp.arange(capacity)[None, None, :])
    send_slot = jnp.sum(picked.astype(jnp.int32) * slot_of[:, :, None], axis=1)
    valid = jnp.any(picked, axis=1)
    outgoing = kv_store[send_slot, 0]
    outgoing = jnp.where(valid[:, :, None, None], outgoing, jnp.zeros_like(outgoing))
    received = lax.all_to_all(outgoing, "cache", split_axis=0, concat_axis=0, tiled=True)
    my_owner = lax.dynamic_index_in_dim(owner_of, self_index, 0, keepdims=False)
    my_rank = lax.dynamic_index_in_dim(rank_of, self_index, 0, keepdims=False)
    my_rows = lax.dynamic_index_in_dim(rec_rows, self_index, 0, keepdims=False)
    flat_received = received.reshape(owners * capacity, received.shape[2], kv_width)
    blocks = flat_received[my_owner * capacity + my_rank]
    blocks = blocks.at[jnp.arange(stretch_count)[:, None], my_rows].set(fresh_blocks)
    stretch_len = blocks.shape[1]
    keyvals = blocks.reshape(stretch_count * stretch_len, kv_width)
    query_heads = queries.reshape(rows_dev, heads_here, head_dim)
    scores = jnp.einsum(
        "qjd,kd->jqk", query_heads, keyvals[:, :head_dim], preferred_element_type=jnp.float32
    ) / math.sqrt(head_dim)
    query_pos = (jnp.arange(stretch_count)[:, None] * stretch_len + my_rows).reshape(rows_dev)
    key_pos = jnp.arange(stretch_count * stretch_len)
    allowed = key_pos[None, :] <= query_pos[:, None]
    scores = jnp.where(allowed[None], scores, -jnp.inf)
    highest = jnp.max(scores, axis=-1, keepdims=True)
    expon = jnp.exp(scores - highest)
    weights = (expon / jnp.sum(expon, axis=-1, keepdims=True)).astype(jnp.bfloat16)
    context = jnp.einsum(
        "jqk,kd->qjd", weights, keyvals[:, head_dim:], preferred_element_type=jnp.float32
    ).astype(jnp.bfloat16)
    context = context.reshape(rows_dev, query_width)
    partial_terms = jnp.dot(
        context,
        lax.all_gather(out_weight, "cache", axis=1, tiled=True),
        preferred_element_type=jnp.float32,
    )
    attn_out = lax.psum_scatter(
        partial_terms.astype(jnp.bfloat16), "heads", scatter_dimension=1, tiled=True
    )
    outbound = jnp.zeros((owners, capacity, per_stretch, kv_width), jnp.bfloat16)
    outbound = outbound.at[my_owner, my_rank].set(fresh_blocks)
    inbound = lax.all_to_all(outbound, "cache", split_axis=0, concat_axis=0, tiled=True)
    send_rows = jnp.sum(picked.astype(jnp.int32)[:, :, :, None] * rec_rows[:, :, None, :], axis=1)
    target_slot = jnp.where(valid, send_slot, stretch_count)
    store_local = kv_store[:, 0]
    store_local = store_local.at[target_slot[:, :, None], send_rows].set(inbound, mode="drop")
    new_store = store_local[:, None]
    return (attn_out, new_store)


def solution(mesh):
    placed = (
        P("cache", None),
        P(),
        P("cache", "heads"),
        P("heads"),
        P("cache", None),
        P(),
        P("heads", "cache"),
        P("cache", "heads", None, None),
        P(),
        P(),
        P(),
    )
    return jax.shard_map(
        shards,
        mesh=mesh,
        in_specs=placed,
        out_specs=(P("cache", "heads"), P("cache", "heads", None, None)),
        check_vma=False,
    )
```

profile of v0, /device:TPU:34, one launch (start us, length us, event | category | flops | bytes accessed | tf_op | source)
XLA Modules:
  0.0 509.5 jit_solution(14210031023383556534)
XLA Ops:
  7.2 3.2 copy.131
  10.4 0.7 convert_element_type.46
  11.1 0.7 fusion.2
  11.8 0.9 fusion.4
  12.7 2.0 copy.126
  14.7 7.5 %all-to-all-start.1 = ((bf16[192,16,512]{2,0,1:T(8,128)(2,1)}), bf16[192,16,512]{2,0,1:T(8,128)(2,1)}, u32[]{:S(2)}, u32[]{:S(2)}) async-start(bf16[192,16,512]{2,0,1:T(8,128)(2,1)} %bitcast.81), calls=%async_computation.1 | async-start | bytes 6291456 | tf_op jit(solution)/shard_map/all_to_all | solution.py:46
  22.2 41.2 %all-to-all-done.1 = bf16[192,16,512]{2,0,1:T(8,128)(2,1)} async-done(((bf16[192,16,512]{2,0,1:T(8,128)(2,1)}), bf16[192,16,512]{2,0,1:T(8,128)(2,1)}, u32[]{:S(2)}, u32[]{:S(2)}) %all-to-all-start.1) | async-done | bytes 3145760 | tf_op jit(solution)/shard_map/all_to_all | solution.py:46
  63.4 6.4 %fusion.38 = f32[3072,512]{0,1:T(8,128)} fusion(bf16[3072,512]{1,0:T(8,128)(2,1)} %bitcast.6, bf16[512,512]{1,0:T(8,128)(2,1)S(1)} %copy-done.5), kind=kOutput, calls=%fused_computation.99 | convolution fusion | flops 1610612736 | bytes 9961472 | tf_op jit(solution)/shard_map/dot_general | solution.py:50
  69.8 2.9 fusion.12
  72.7 7.6 %pad_maximum_fusion = f32[3072,768]{0,1:T(8,128)} fusion(f32[3072,256]{0,1:T(8,128)S(1)} %fusion.12, f32[3072,512]{0,1:T(8,128)} %fusion.38), kind=kLoop, calls=%fused_computation.12 | loop fusion | flops 2359296 | bytes 18874368 | tf_op jit(solution)/shard_map/concatenate | solution.py:48
  80.3 9.6 %copy.113 = f32[3072,768]{1,0:T(8,128)} copy(f32[3072,768]{0,1:T(8,128)} %pad_maximum_fusion) | data formatting | bytes 18874368
  90.9 1.2 gather_fusion
  92.8 6.5 %gather_fusion.1 = bf16[32,512,256]{2,1,0:T(8,128)(2,1)} fusion(bf16[8,1,512,256]{3,2,1,0:T(8,128)(2,1)} %copy.131, s32[32]{0:T(128)S(1)} %reshape.308), kind=kCustom, calls=%fused_computation.1 | custom fusion | bytes 16777472 | tf_op jit(solution)/shard_map/gather | solution.py:74
  99.3 7.2 %broadcast_select_fusion = bf16[16,2,512,256]{3,2,1,0:T(8,128)(2,1)} fusion(bf16[16,2,512,256]{3,2,1,0:T(8,128)(2,1)} %bitcast.80, pred[16,2]{1,0:T(8,128)(4,1)S(1)} %copy.103), kind=kLoop, calls=%fused_computation.13 | loop fusion | flops 4194304 | bytes 16777248 | tf_op jit(solution)/shard_map/jit(_where)/select_n | solution.py:75
  106.5 9.3 %all-to-all-start = ((bf16[16,2,512,256]{3,2,1,0:T(8,128)(2,1)}), bf16[16,2,512,256]{3,2,1,0:T(8,128)(2,1)}, u32[]{:S(2)}, u32[]{:S(2)}) async-start(bf16[16,2,512,256]{3,2,1,0:T(8,128)(2,1)} %broadcast_select_fusion), calls=%async_computation | async-start | bytes 16777216 | tf_op jit(solution)/shard_map/all_to_all | solution.py:76
  116.7 0.8 dynamic-slice_convert_fusion
  118.0 115.0 %all-to-all-done = bf16[16,2,512,256]{3,2,1,0:T(8,128)(2,1)} async-done(((bf16[16,2,512,256]{3,2,1,0:T(8,128)(2,1)}), bf16[16,2,512,256]{3,2,1,0:T(8,128)(2,1)}, u32[]{:S(2)}, u32[]{:S(2)}) %all-to-all-start) | async-done | bytes 8388640 | tf_op jit(solution)/shard_map/all_to_all | solution.py:76
  233.0 5.7 %gather_fusion.2 = bf16[8,512,256]{2,1,0:T(8,128)(2,1)} fusion(bf16[32,512,256]{2,1,0:T(8,128)(2,1)} %bitcast.2, s32[1024]{0:T(1024)S(1)} %pad_clamp_fusion), kind=kCustom, calls=%fused_computation.2 | custom fusion | bytes 4194336 | tf_op jit(solution)/shard_map/gather | solution.py:81
  238.8 74.2 %reduce-scatter.7.cloned.1.call-done = f32[192,768]{1,0:T(8,128)} async-done(((f32[3072,768]{1,0:T(8,128)}), f32[192,768]{1,0:T(8,128)}) %reduce-scatter.7.cloned.1.call-update) | async-done | bytes 589840 | tf_op jit(solution)/shard_map/reduce_scatter | solution.py:47
  313.0 1.0 slice.31
  314.2 0.9 fusion.16
  315.2 21.5 %scatter_fusion = bf16[8,512,256]{2,1,0:T(8,128)(2,1)} fusion(bf16[8,512,256]{2,1,0:T(8,128)(2,1)} %gather_fusion.2, s32[192]{0:T(256)S(1)} %reshape.322, bf16[192,256]{1,0:T(8,128)(2,1)S(1)} %fusion.16), kind=kCustom, calls=%fused_computation.3 | custom fusion | bytes 296448 | tf_op jit(solution)/shard_map/scatter | solution.py:82
  336.9 7.5 %fusion.11 = f32[4096,192,4]{0,1,2:T(8,128)} fusion(bf16[192,4,128]{0,2,1:T(8,128)(2,1)S(1)} %bitcast.86, bf16[4096,256]{1,0:T(8,128)(2,1)} %bitcast.83), kind=kOutput, calls=%fused_computation.28 | convolution fusion | flops 805306368 | bytes 13828096 | tf_op jit(solution)/shard_map/qjd,kd->jqk/dot_general | solution.py:86
  344.4 17.3 %fusion.37 = (f32[4,192]{1,0:T(4,128)S(1)}, f32[4,192,4096]{2,1,0:T(8,128)}) fusion(f32[4096,192,4]{0,1,2:T(8,128)} %fusion.11, pred[192,4096]{1,0:T(8,128)(4,1)S(1)} %iota_compare_fusion), kind=kOutput, calls=%fused_computation.98 | output fusion | flops 18878464 | bytes 25955328 | tf_op jit(solution)/shard_map/sub | solution.py:94
  361.7 6.4 %fusion.10 = bf16[4,24,8,128]{3,2,1,0:T(8,128)(2,1)S(1)} fusion(f32[4,192,4096]{2,1,0:T(8,128)} %get-tuple-element.11, f32[4,192]{1,0:T(4,128)S(1)} %get-tuple-element.10, bf16[4096,256]{1,0:T(8,128)(2,1)S(1)} %bitcast.84), kind=kOutput, calls=%fused_computation.26 | convolution fusion | flops 811696128 | bytes 13832192 | tf_op jit(solution)/shard_map/jqk,kd->qjd/dot_general | solution.py:96
  368.2 30.2 %all-gather.2.cloned.1.call-done = bf16[512,8192]{1,0:T(8,128)(2,1)} async-done(((bf16[512,512]{1,0:T(8,128)(2,1)}), bf16[512,8192]{1,0:T(8,128)(2,1)}) %all-gather.2.cloned.1.call-update) | async-done | bytes 8388624 | tf_op jit(solution)/shard_map/all_gather | solution.py:102
  398.4 7.0 %convolution_convert_fusion = bf16[192,8192]{1,0:T(8,128)(2,1)} fusion(bf16[512,8192]{1,0:T(8,128)(2,1)} %all-gather.2.cloned.1.call-done, bf16[4,24,8,128]{3,2,1,0:T(8,128)(2,1)S(1)} %fusion.10), kind=kOutput, calls=%fused_computation.10 | convolution fusion | flops 1612185600 | bytes 11730944 | tf_op jit(solution)/shard_map/dot_general | solution.py:100
  405.5 0.8 broadcast_in_dim.36
  406.2 2.0 scatter_fusion.1
  408.3 5.7 %all-to-all-start.2 = ((bf16[16,2,24,256]{3,2,1,0:T(8,128)(2,1)}), bf16[16,2,24,256]{3,2,1,0:T(8,128)(2,1)S(1)}, u32[]{:S(2)}, u32[]{:S(2)}) async-start(bf16[16,2,24,256]{3,2,1,0:T(8,128)(2,1)} %scatter_fusion.1), calls=%async_computation.3 | async-start | bytes 786432 | tf_op jit(solution)/shard_map/all_to_all | solution.py:110
  414.4 6.8 %all-to-all-done.2 = bf16[16,2,24,256]{3,2,1,0:T(8,128)(2,1)S(1)} async-done(((bf16[16,2,24,256]{3,2,1,0:T(8,128)(2,1)}), bf16[16,2,24,256]{3,2,1,0:T(8,128)(2,1)S(1)}, u32[]{:S(2)}, u32[]{:S(2)}) %all-to-all-start.2) | async-done | bytes 393248 | tf_op jit(solution)/shard_map/all_to_all | solution.py:110
  421.2 81.7 %scatter_fusion.2 = bf16[8,512,256]{2,1,0:T(8,128)(2,1)} fusion(bf16[8,512,256]{2,1,0:T(8,128)(2,1)} %bitcast.78, s32[768]{0:T(1024)S(1)} %reshape.334, bf16[768,256]{1,0:T(8,128)(2,1)S(1)} %bitcast.85), kind=kCustom, calls=%fused_computation.5 | custom fusion | bytes 1185792 | tf_op jit(solution)/shard_map/scatter | solution.py:114
  (63 shorter events, 3.7 us)
Async XLA Ops:
  7.2 62.6 %copy-start = (bf16[512,2048]{1,0:T(8,128)(2,1)S(1)}, bf16[512,2048]{1,0:T(8,128)(2,1)}, u32[]{:S(2)}) copy-start(bf16[512,2048]{1,0:T(8,128)(2,1)} %param.15) | copy-start | bytes 6291460
  7.2 3.9 copy-start.3
  12.7 50.7 %copy-start.5 = (bf16[512,512]{1,0:T(8,128)(2,1)S(1)}, bf16[512,512]{1,0:T(8,128)(2,1)}, u32[]{:S(2)}) copy-start(bf16[512,512]{1,0:T(8,128)(2,1)} %param.13) | copy-start | bytes 1572868
  14.7 48.7 %all-to-all-start.1 = ((bf16[192,16,512]{2,0,1:T(8,128)(2,1)}), bf16[192,16,512]{2,0,1:T(8,128)(2,1)}, u32[]{:S(2)}, u32[]{:S(2)}) async-start(bf16[192,16,512]{2,0,1:T(8,128)(2,1)} %bitcast.81), calls=%async_computation.1 | async-start | bytes 6291456 | tf_op jit(solution)/shard_map/all_to_all | solution.py:46
  22.2 290.8 %reduce-scatter.7.cloned.1.call-start = ((), (), s32[]{:S(2)}) async-start(), calls=%async_computation.7 | async-start | bytes 10027008 | tf_op jit(solution)/shard_map/reduce_scatter | solution.py:47
  89.9 0.8 copy-start.7
  89.9 1.0 copy-start.2
  89.9 308.5 %all-gather.2.cloned.1.call-start = ((), (), s32[]{:S(2)}) async-start(), calls=%async_computation.5 | async-start | bytes 8912896 | tf_op jit(solution)/shard_map/all_gather | solution.py:102
  106.5 9.6 %copy-start.6 = (s32[16,8,24]{2,1,0:T(8,128)S(1)}, s32[16,8,24]{2,1,0:T(8,128)}, u32[]{:S(2)}) copy-start(s32[16,8,24]{2,1,0:T(8,128)} %param.21) | copy-start | bytes 36868
  106.5 9.7 %copy-start.8 = (bf16[512]{0:T(512)(128)(2,1)S(1)}, bf16[512]{0:T(512)(128)(2,1)}, u32[]{:S(2)}) copy-start(bf16[512]{0:T(512)(128)(2,1)} %param.14) | copy-start | bytes 3076
  106.5 126.5 %all-to-all-start = ((bf16[16,2,512,256]{3,2,1,0:T(8,128)(2,1)}), bf16[16,2,512,256]{3,2,1,0:T(8,128)(2,1)}, u32[]{:S(2)}, u32[]{:S(2)}) async-start(bf16[16,2,512,256]{3,2,1,0:T(8,128)(2,1)} %broadcast_select_fusion), calls=%async_computation | async-start | bytes 16777216 | tf_op jit(solution)/shard_map/all_to_all | solution.py:76
  115.8 387.1 %reduce-scatter.5.cloned.1.call-start = ((), (), s32[]{:S(2)}) async-start(), calls=%async_computation.6 | async-start | bytes 3342336 | tf_op jit(solution)/shard_map/reduce_scatter | solution.py:105
  344.4 17.3 %copy-start.4 = (bf16[8,512,256]{2,1,0:T(8,128)(2,1)S(1)}, bf16[8,512,256]{2,1,0:T(8,128)(2,1)}, u32[]{:S(2)}) copy-start(bf16[8,512,256]{2,1,0:T(8,128)(2,1)} %scatter_fusion) | copy-start | bytes 6291460
  398.4 104.5 %copy-start.1 = (bf16[512,2048]{1,0:T(8,128)(2,1)S(1)}, bf16[512,2048]{1,0:T(8,128)(2,1)}, u32[]{:S(2)}) copy-start(bf16[512,2048]{1,0:T(8,128)(2,1)} %param.15) | copy-start | bytes 6291460
  408.3 13.0 %all-to-all-start.2 = ((bf16[16,2,24,256]{3,2,1,0:T(8,128)(2,1)}), bf16[16,2,24,256]{3,2,1,0:T(8,128)(2,1)S(1)}, u32[]{:S(2)}, u32[]{:S(2)}) async-start(bf16[16,2,24,256]{3,2,1,0:T(8,128)(2,1)} %scatter_fusion.1), calls=%async_computation.3 | async-start | bytes 786432 | tf_op jit(solution)/shard_map/all_to_all | solution.py:110
Sparse Core Ops, SparseCore 0:
  90.1 222.9 reduce-scatter.6
  315.7 82.6 all-gather.1
  405.6 57.3 reduce-scatter.4
where the time goes:
time: 515 us; the launch traced here: 509 us
  waiting for transfers between devices  268 us (52%)
  local copies, waits for them, and re-layouts  137 us (27%)
  other arithmetic  37.2 us (7%)
  matrix products  30.3 us (6%)
  starting transfers between devices  22.8 us (4%)
  between operations  14 us (3%)
    all_to_all x1, waiting for transfers between devices, shards(): lax.all_to_all(outgoing, 'cache', split_axis=0, concat_axis=0, tiled=True)  115 us
    scatter x1, local copies, waits for them, and re-layouts, shards(): store_local.at[target_slot[:, :, None], send_rows].set(inbound, mode='drop')  81.7 us
    reduce_scatter x1, waiting for transfers between devices, shards(): lax.psum_scatter(jnp.concatenate([jnp.dot(slices, q_weight, preferred_ele...  74.2 us
    all_to_all x1, waiting for transfers between devices, shards(): lax.all_to_all(normed, 'cache', split_axis=1, concat_axis=0, tiled=True)  41.2 us
    all_gather x1, waiting for transfers between devices, shards(): lax.all_gather(out_weight, 'cache', axis=1, tiled=True)  30.2 us
    scatter x1, local copies, waits for them, and re-layouts, shards(): blocks.at[jnp.arange(stretch_count)[:, None], my_rows].set(fresh_blocks)  21.5 us
    sub x1, other arithmetic, shards(): expon = jnp.exp(scores - highest)  17.3 us
    unnamed x21, local copies, waits for them, and re-layouts  13.1 us
  transfers between devices with their start and end apart: 6, of which 5 were waited for; matrix products, arithmetic and copies ran while one was open for 32% of the time, Pallas kernels for 0%

commit v1 on v0

v1 whole, which is shorter than its diff:
```python
import functools
import math

import jax
import jax.numpy as jnp
from jax import lax
from jax.experimental import pallas as pl
from jax.experimental.pallas import tpu as pltpu
from jax.sharding import PartitionSpec as P

MESH = pl.DeviceIdType.MESH
SIDE = 4
BF16 = jnp.bfloat16
F32 = jnp.float32
PAD = 32


def remote(src, dst, send_sem, recv_sem, device):
    return pltpu.make_async_remote_copy(
        src_ref=src, dst_ref=dst, send_sem=send_sem, recv_sem=recv_sem, device_id=device, device_id_type=MESH
    )


def gather_project(
    place_ref, hid_hbm, gain_ref, qw_hbm, kvw_hbm, qb_ref, kvb_ref, store_hbm,
    q_ref, fresh_ref, blocks_hbm,
    hid, nrm, w, acc, hop_in, hop_out, qs, fpad,
    loc, w_send, w_recv, h1_send, h1_recv, h2_send, h2_recv, x_send, x_recv,
):
    me = lax.axis_index("cache")
    head = lax.axis_index("heads")
    core = lax.rem(head, 2)
    partner = (me, head + 1 - 2 * core)
    x, y = me // SIDE, lax.rem(me, SIDE)
    owners = SIDE * SIDE
    rows = hid.shape[0]
    depth, width = w.shape[1], w.shape[2]
    unit, half = depth // 4, depth // 2
    q_cols = qw_hbm.shape[1]
    hd = width - q_cols

    def at(dx, dy):
        return lax.rem(x + dx, SIDE) * SIDE + lax.rem(y + dy, SIDE)

    own_q = pltpu.make_async_copy(qw_hbm, w.at[me, :, 0:q_cols], loc.at[0])
    own_kv = pltpu.make_async_copy(
        kvw_hbm.at[:, pl.ds(pl.multiple_of(head * hd, hd), hd)], w.at[me, :, q_cols:width], loc.at[1]
    )
    own_hid = pltpu.make_async_copy(hid_hbm, hid, loc.at[2])
    own_hop = pltpu.make_async_copy(store_hbm.at[:, me, core], hop_in.at[pl.ds(me * 8, 8)], loc.at[3])
    own_q.start()
    own_kv.start()
    own_hop.start()
    own_hid.start()

    barrier = pltpu.get_barrier_semaphore()

    @pl.loop(1, owners)
    def _(o):
        pl.semaphore_signal(barrier, inc=1, device_id=(lax.rem(me + o, owners), head), device_id_type=MESH)

    pl.semaphore_signal(barrier, inc=1, device_id=partner, device_id_type=MESH)
    pl.semaphore_wait(barrier, owners)

    def hop1(o):
        to = lax.rem(me + o, owners)
        return remote(
            store_hbm.at[:, to, core], hop_in.at[pl.ds(me * 8, 8)], h1_send.at[o], h1_recv.at[me], (to, head)
        )

    def hop1_from(o):
        src = lax.rem(me + owners - o, owners)
        return remote(
            store_hbm.at[:, src, core], hop_in.at[pl.ds(src * 8, 8)], h1_send.at[o], h1_recv.at[src], (src, head)
        )

    def hop2(o):
        to = lax.rem(me + o, owners)
        return remote(hop_out.at[to], blocks_hbm.at[:, me, core], h2_send.at[o], h2_recv.at[me], (to, head))

    def hop2_from(o):
        src = lax.rem(me + owners - o, owners)
        return remote(hop_out.at[src], blocks_hbm.at[:, src, core], h2_send.at[o], h2_recv.at[src], (src, head))

    @pl.loop(1, owners)
    def _(o):
        hop1(o).start()

    own_q.wait()
    own_kv.wait()

    sends = []

    def piece(c, u):
        return w.at[c, pl.ds(u * unit, unit)]

    def send(c, u, dx, dy):
        copy = remote(piece(c, u), piece(c, u), w_send.at[len(sends)], w_recv.at[c, u], (at(dx, dy), head))
        copy.start()
        sends.append(copy)

    def arrived(c, u):
        remote(piece(c, u), piece(c, u), w_send.at[0], w_recv.at[c, u], (at(1, 0), head)).wait_recv()

    L, O, R = SIDE - 1, 2, 1

    def first(axis, d):
        return at(d, 0) if axis == 0 else at(0, d)

    def go(c, u, axis, d):
        send(c, u, d if axis == 0 else 0, d if axis == 1 else 0)

    for u in (0, 1):
        for axis in (0, 1):
            for d in (R, L):
                go(me, 2 * axis + u, axis, d)

    own_hid.wait()
    tall = 16

    @pl.loop(0, rows // tall)
    def _(i):
        lines = pl.ds(pl.multiple_of(i * tall, tall), tall)
        total = jnp.zeros((tall, 1), F32)
        for c in range(owners):
            v = hid[lines, c * depth : (c + 1) * depth].astype(F32)
            total += jnp.sum(v * v, axis=-1, keepdims=True)
        factor = lax.rsqrt(total / (owners * depth) + 1e-06)
        for c in range(owners):
            v = hid[lines, c * depth : (c + 1) * depth].astype(F32)
            g = gain_ref[:, c * depth : (c + 1) * depth].astype(F32)
            nrm[c, lines, :] = (v * factor * g).astype(BF16)

    acc[...] = jnp.zeros_like(acc)

    def multiply(c, axis):
        lo = axis * half
        acc[...] += jnp.dot(nrm[c, :, lo : lo + half], w[c, lo : lo + half, :], preferred_element_type=F32)

    for axis in (0, 1):
        arrived(first(axis, L), 2 * axis)
        go(first(axis, L), 2 * axis, axis, R)
        arrived(first(axis, R), 2 * axis + 1)
        go(first(axis, R), 2 * axis + 1, axis, L)
    for axis in (0, 1):
        for u in (0, 1):
            for d in (R, L):
                go(me, 2 * axis + u, 1 - axis, d)

    own_hop.wait()

    @pl.loop(1, owners)
    def _(o):
        hop1_from(o).wait_recv()

    @pl.loop(0, owners)
    def _(i):
        for r in range(8):
            hop_out[i, r] = hop_in[place_ref[i * 8 + r]]

    @pl.loop(1, owners)
    def _(o):
        hop2(o).start()

    own_out = pltpu.make_async_copy(hop_out.at[me], blocks_hbm.at[:, me, core], loc.at[4])
    own_out.start()

    for axis in (0, 1):
        arrived(first(axis, L), 2 * axis + 1)
        arrived(first(axis, R), 2 * axis)
        for s in (L, R):
            for u in (0, 1):
                for d in (R, L):
                    go(first(axis, s), 2 * axis + u, 1 - axis, d)
    for axis in (0, 1):
        arrived(first(axis, O), 2 * axis)
        arrived(first(axis, O), 2 * axis + 1)
        for u in (0, 1):
            for d in (R, L):
                go(first(axis, O), 2 * axis + u, 1 - axis, d)

    @pl.loop(0, SIDE)
    def _(i):
        multiply(at(i, 0), 0)
        multiply(at(0, i), 1)

    def second(axis, s, d):
        return at(s, d) if axis == 0 else at(d, s)

    def core_swap(which):
        return remote(
            blocks_hbm.at[:, :, which], blocks_hbm.at[:, :, which], x_send.at[0], x_recv.at[0], partner
        )

    for n, s in enumerate((0, L, R, O)):
        for axis in (0, 1):
            arrived(second(axis, s, L), 2 * axis)
            go(second(axis, s, L), 2 * axis, 1 - axis, R)
            arrived(second(axis, s, R), 2 * axis + 1)
            go(second(axis, s, R), 2 * axis + 1, 1 - axis, L)
        for axis in (0, 1):
            arrived(second(axis, s, L), 2 * axis + 1)
            arrived(second(axis, s, R), 2 * axis)
            arrived(second(axis, s, O), 2 * axis)
            arrived(second(axis, s, O), 2 * axis + 1)

        @pl.loop(1, SIDE)
        def _(i):
            multiply(second(0, s, i), 0)
            multiply(second(1, s, i), 1)

        if n == 2:
            own_out.wait()

            @pl.loop(1, owners)
            def _(o):
                hop2_from(o).wait_recv()

            core_swap(core).start()

    per = rows // 8
    heads = q_cols // hd
    bias = qb_ref[...].astype(F32)
    kv_bias = kvb_ref[:, pl.ds(pl.multiple_of(head * hd, hd), hd)].astype(F32)
    for r in range(8):
        lines = slice(per * r, per * (r + 1))
        for j in range(heads):
            at_row = (r * heads + j) * per
            qs[at_row : at_row + per, :] = acc[lines, j * hd : (j + 1) * hd] + bias[:, j * hd : (j + 1) * hd]
        fpad[r * PAD : r * PAD + per, :] = acc[lines, q_cols:width] + kv_bias
        fpad[r * PAD + per : (r + 1) * PAD, :] = jnp.zeros((PAD - per, hd), F32)
    fresh_ref[core] = fpad[...].astype(BF16)
    swap = remote(fresh_ref.at[core], fresh_ref.at[core], x_send.at[1], x_recv.at[1], partner)
    swap.start()
    q_ref[...] = qs[...].astype(BF16)

    core_swap(1 - core).wait_recv()
    remote(fresh_ref.at[1 - core], fresh_ref.at[1 - core], x_send.at[1], x_recv.at[1], partner).wait_recv()
    swap.wait_send()
    core_swap(core).wait_send()
    for copy in sends:
        copy.wait_send()

    @pl.loop(1, owners)
    def _(o):
        hop1(o).wait_send()
        hop2(o).wait_send()


def attend(q_ref, fresh_ref, blocks_ref, row_ref, pos_ref, ctx_ref, ks, vs, sc, top, low, out, flat):
    stretches, length = blocks_ref.shape[0], blocks_ref.shape[1]
    hd = q_ref.shape[1]
    total = q_ref.shape[0]
    group = total // stretches
    heads = ctx_ref.shape[1] // hd
    per = group // heads
    scale = math.log2(math.e) / math.sqrt(hd)
    ones = jnp.ones((PAD, hd), BF16)
    for r in range(stretches):
        hit = lax.broadcasted_iota(jnp.int32, (length, PAD), 0) == row_ref[r : r + 1, :]
        lines = slice(r * PAD, (r + 1) * PAD)
        table = jnp.concatenate([fresh_ref[0, lines, :], fresh_ref[1, lines, :], ones], axis=1)
        new = jnp.dot(hit.astype(F32).astype(BF16), table, preferred_element_type=F32)
        there = new[:, 2 * hd :] > 0.5
        ks[r] = jnp.where(there, new[:, :hd], blocks_ref[r, :, :hd].astype(F32)).astype(BF16)
        vs[r] = jnp.where(there, new[:, hd : 2 * hd], blocks_ref[r, :, hd:].astype(F32)).astype(BF16)
    top[...] = jnp.full_like(top, -jnp.inf)
    low[...] = jnp.zeros_like(low)
    out[...] = jnp.zeros_like(out)

    def fold(a, op):
        parts = [a[:, i * hd : (i + 1) * hd] for i in range(length // hd)]
        while len(parts) > 1:
            parts = [op(parts[i], parts[i + 1]) for i in range(0, len(parts), 2)]
        return parts[0]

    for s in range(stretches):
        scores = lax.dot_general(
            q_ref[s * group :, :], ks[s], (((1,), (1,)), ((), ())), preferred_element_type=F32
        )
        key = lax.broadcasted_iota(jnp.int32, (group, length), 1)
        first = jnp.where(key <= pos_ref[s * group : (s + 1) * group, :], scores[:group], -jnp.inf)
        sc[s, s * group : (s + 1) * group, :] = first
        top[s * group : (s + 1) * group, :] = jnp.maximum(
            top[s * group : (s + 1) * group, :], fold(first, jnp.maximum)
        )
        if s + 1 < stretches:
            sc[s, (s + 1) * group :, :] = scores[group:]
            top[(s + 1) * group :, :] = jnp.maximum(top[(s + 1) * group :, :], fold(scores[group:], jnp.maximum))
    top[...] = jnp.broadcast_to(jnp.max(top[...], axis=1, keepdims=True), top.shape)
    for s in range(stretches):
        here = slice(s * group, total)
        peak = top[here, :]
        expon = jnp.concatenate(
            [jnp.exp2((sc[s, here, i * hd : (i + 1) * hd] - peak) * scale) for i in range(length // hd)], axis=1
        )
        low[here, :] += fold(expon, jnp.add)
        out[here, :] += jnp.dot(expon.astype(BF16), vs[s], preferred_element_type=F32)
    out[...] = out[...] / jnp.sum(low[...], axis=1, keepdims=True)
    for r in range(stretches):
        for j in range(heads):
            at_row = (r * heads + j) * per
            flat[r * per : (r + 1) * per, j * hd : (j + 1) * hd] = out[at_row : at_row + per, :]
    ctx_ref[...] = flat[...].astype(BF16)


def project_out(
    slot_ref, pick_ref, ctx_ref, w_hbm, fresh_ref,
    out_ref, back_ref,
    w, pair_out, pair_in, own, r_out, l_out, r_in, l_in, f_out, f_in,
    w_sem, p_send, p_recv, r_send, r_recv, l_send, l_recv, f_send, f_recv, b_send, b_recv,
):
    me = lax.axis_index("cache")
    head = lax.axis_index("heads")
    owners = lax.axis_size("cache")
    ring = lax.axis_size("heads") // 2
    core = lax.rem(head, 2)
    z = head // 2
    partner = (me, head + 1 - 2 * core)
    right = (me, lax.rem(z + 1, ring) * 2 + core)
    left = (me, lax.rem(z + ring - 1, ring) * 2 + core)
    rows = ctx_ref.shape[0]
    hrow = rows // 2
    order = (4, 3, -3, 2, -2, 1, -1, 0)

    def column(n, parity):
        return lax.rem(z + order[n] + ring, ring) * 2 + parity

    def fetch(n, which):
        block = column(n, 1 - core if which == 0 else core)
        return pltpu.make_async_copy(w_hbm.at[block], w.at[2 * n + which], w_sem.at[2 * n + which])

    for n in range(len(order)):
        for which in (0, 1):
            fetch(n, which).start()

    barrier = pltpu.get_barrier_semaphore()

    @pl.loop(1, owners)
    def _(o):
        pl.semaphore_signal(barrier, inc=1, device_id=(lax.rem(me + o, owners), head), device_id_type=MESH)

    for peer in (partner, left, right):
        pl.semaphore_signal(barrier, inc=1, device_id=peer, device_id_type=MESH)
    pl.semaphore_wait(barrier, owners + 2)

    @pl.loop(0, owners)
    def _(o):
        for m in range(2):
            f_out[2 * o + m] = fresh_ref[core, slot_ref[2 * o + m]]

    def give(o):
        to = lax.rem(me + o, owners)
        return remote(
            f_out.at[pl.ds(2 * to, 2)], f_in.at[pl.ds(2 * me, 2)], f_send.at[o], f_recv.at[me], (to, head)
        )

    def take(o):
        src = lax.rem(me + owners - o, owners)
        return remote(
            f_out.at[pl.ds(2 * src, 2)], f_in.at[pl.ds(2 * src, 2)], f_send.at[o], f_recv.at[src], (src, head)
        )

    @pl.loop(1, owners)
    def _(o):
        give(o).start()

    for m in range(2):
        f_in[2 * me + m] = f_out[2 * me + m]

    def pair(n):
        return remote(pair_out.at[n], pair_in.at[n], p_send.at[n], p_recv.at[n], partner)

    for n in range(len(order)):
        fetch(n, 0).wait()
        pair_out[n] = jnp.dot(ctx_ref[...], w[2 * n], preferred_element_type=F32).astype(BF16)
        pair(n).start()
        fetch(n, 1).wait()
        own[n] = jnp.dot(ctx_ref[...], w[2 * n + 1], preferred_element_type=F32).astype(BF16)

    def lines(part):
        return slice(part * hrow, (part + 1) * hrow)

    def total(n, part):
        return own[n, lines(part), :].astype(F32) + pair_in[n, lines(part), :].astype(F32)

    def ring_copy(step, part, out, into, send_sem, recv_sem, to):
        return remote(
            out.at[step, pl.ds(part * hrow, hrow)],
            into.at[step, pl.ds(part * hrow, hrow)],
            send_sem.at[step, part],
            recv_sem.at[step, part],
            to,
        )

    def rightward(step, part):
        return ring_copy(step, part, r_out, r_in, r_send, r_recv, right)

    def leftward(step, part):
        return ring_copy(step, part, l_out, l_in, l_send, l_recv, left)

    pair(0).wait_recv()
    r_out[0, lines(0), :] = total(0, 0).astype(BF16)
    rightward(0, 0).start()
    l_out[0, lines(1), :] = total(0, 1).astype(BF16)
    leftward(0, 1).start()
    for step in (1, 2, 3):
        n_right, n_left = 2 * step - 1, 2 * step
        pair(n_right).wait_recv()
        pair(n_left).wait_recv()
        parts = ((1, 0), (0, 1)) if step == 1 else ((0, 1), (1, 0))
        for right_part, left_part in zip(*parts):
            value = total(n_right, right_part)
            if step > 1 or right_part == 0:
                rightward(step - 1, right_part).wait_recv()
                value += r_in[step - 1, lines(right_part), :].astype(F32)
            r_out[step, lines(right_part), :] = value.astype(BF16)
            rightward(step, right_part).start()
            value = total(n_left, left_part)
            if step > 1 or left_part == 1:
                leftward(step - 1, left_part).wait_recv()
                value += l_in[step - 1, lines(left_part), :].astype(F32)
            l_out[step, lines(left_part), :] = value.astype(BF16)
            leftward(step, left_part).start()

    @pl.loop(1, owners)
    def _(o):
        take(o).wait_recv()

    for s in range(back_ref.shape[1]):
        back_ref[core, s] = f_in[pick_ref[s]]
    swap = remote(back_ref.at[core], back_ref.at[core], b_send.at[0], b_recv.at[0], partner)
    swap.start()

    pair(7).wait_recv()
    for part in (0, 1):
        rightward(3, part).wait_recv()
        leftward(3, part).wait_recv()
        value = total(7, part) + r_in[3, lines(part), :].astype(F32) + l_in[3, lines(part), :].astype(F32)
        out_ref[lines(part), :] = value.astype(BF16)

    remote(back_ref.at[1 - core], back_ref.at[1 - core], b_send.at[0], b_recv.at[0], partner).wait_recv()
    swap.wait_send()
    for n in range(len(order)):
        pair(n).wait_send()
    rightward(0, 0).wait_send()
    leftward(0, 1).wait_send()
    for step in (1, 2, 3):
        for part in (0, 1):
            rightward(step, part).wait_send()
            leftward(step, part).wait_send()

    @pl.loop(1, owners)
    def _(o):
        give(o).wait_send()


def write_back(store_ref, back_ref, row_ref, new_ref):
    length, hd = store_ref.shape[2], back_ref.shape[3]
    hit = lax.broadcasted_iota(jnp.int32, (length, PAD), 0) == row_ref[0]
    table = jnp.concatenate([back_ref[0, 0], back_ref[1, 0], jnp.ones((PAD, hd), BF16)], axis=1)
    new = jnp.dot(hit.astype(F32).astype(BF16), table, preferred_element_type=F32)
    there = new[:, 2 * hd :] > 0.5
    for part in (0, 1):
        lanes = slice(part * hd, (part + 1) * hd)
        new_ref[0, 0, :, lanes] = jnp.where(there, new[:, lanes], store_ref[0, 0, :, lanes].astype(F32)).astype(BF16)


def whole(shape=None):
    return pl.BlockSpec(memory_space=pltpu.VMEM)


def shards(
    hidden, norm_gain, q_weight, q_bias, kv_weight, kv_bias, out_weight, kv_store, stretch_place, req_stretches, rec_rows
):
    owners = lax.axis_size("cache")
    me = lax.axis_index("cache")
    rows, width = hidden.shape
    stretches, _, length, kv_width = kv_store.shape
    hd = kv_width // 2
    per = rec_rows.shape[2]
    depth, q_cols = q_weight.shape
    heads = q_cols // hd
    vmem = pl.BlockSpec(memory_space=pltpu.VMEM)
    smem = pl.BlockSpec(memory_space=pltpu.SMEM)
    hbm = pl.BlockSpec(memory_space=pl.ANY)
    dma = pltpu.SemaphoreType.DMA

    out_blocks = lax.all_gather(out_weight, "cache", axis=0, tiled=False)

    places = stretch_place[req_stretches]
    owner_of = places // stretches
    earlier = jnp.arange(stretches)[None, :] < jnp.arange(stretches)[:, None]
    rank_of = jnp.sum((owner_of[:, :, None] == owner_of[:, None, :]) & earlier[None], axis=2).astype(jnp.int32)
    pair_of = owner_of * 2 + rank_of
    my_pair = lax.dynamic_index_in_dim(pair_of, me, 0, keepdims=False)
    order = jnp.arange(stretches, dtype=jnp.int32)
    slot_r = jnp.sum((my_pair[None, :] == jnp.arange(2 * owners)[:, None]) * order[None, :], axis=1).astype(jnp.int32)
    flat_places = places.reshape(-1)
    mine = flat_places[None, :] == (me * stretches + order)[:, None]
    source = jnp.arange(owners)[:, None] * 2 + rank_of
    pick = jnp.sum(mine * source.reshape(1, -1), axis=1).astype(jnp.int32)
    slot_rows = jnp.sum(mine[:, :, None] * rec_rows.reshape(1, -1, per), axis=1).astype(jnp.int32)
    slot_rows = jnp.pad(slot_rows, ((0, 0), (0, PAD - per)), constant_values=-1)
    my_rows = lax.dynamic_index_in_dim(rec_rows, me, 0, keepdims=False)
    pad_rows = jnp.pad(my_rows, ((0, 0), (0, PAD - per)), constant_values=-1)
    row_pos = jnp.broadcast_to(my_rows[:, None, :], (stretches, heads, per)).reshape(rows * heads, 1)

    store = kv_store.reshape(stretches, owners, 2, length // (2 * owners), kv_width)
    piece = length // (2 * owners)

    queries, fresh, blocks = pl.pallas_call(
        gather_project,
        out_shape=(
            jax.ShapeDtypeStruct((rows * heads, hd), BF16),
            jax.ShapeDtypeStruct((2, stretches * PAD, hd), BF16),
            jax.ShapeDtypeStruct((stretches, owners, 2, piece, kv_width), BF16),
        ),
        in_specs=[smem, hbm, vmem, hbm, hbm, vmem, vmem, hbm],
        out_specs=(vmem, vmem, hbm),
        scratch_shapes=[
            pltpu.VMEM((rows, width), BF16),
            pltpu.VMEM((owners, rows, depth), BF16),
            pltpu.VMEM((owners, depth, q_cols + hd), BF16),
            pltpu.VMEM((rows, q_cols + hd), F32),
            pltpu.VMEM((owners * stretches, piece, kv_width), BF16),
            pltpu.VMEM((owners, stretches, piece, kv_width), BF16),
            pltpu.VMEM((rows * heads, hd), F32),
            pltpu.VMEM((stretches * PAD, hd), F32),
            dma((5,)),
            dma((60,)),
            dma((owners, 4)),
            dma((owners,)),
            dma((owners,)),
            dma((owners,)),
            dma((owners,)),
            dma((2,)),
            dma((2,)),
        ],
        compiler_params=pltpu.CompilerParams(collective_id=0, has_side_effects=True, vmem_limit_bytes=48 << 20),
        name="gather_project",
    )(
        flat_places, hidden, norm_gain.reshape(1, -1), q_weight, kv_weight,
        q_bias.reshape(1, -1), kv_bias.reshape(1, -1), store,
    )
    blocks = blocks.reshape(stretches, length, kv_width)

    context = pl.pallas_call(
        attend,
        out_shape=jax.ShapeDtypeStruct((rows, q_cols), BF16),
        in_specs=[vmem] * 5,
        out_specs=vmem,
        scratch_shapes=[
            pltpu.VMEM((stretches, length, hd), BF16),
            pltpu.VMEM((stretches, length, hd), BF16),
            pltpu.VMEM((stretches, rows * heads, length), F32),
            pltpu.VMEM((rows * heads, hd), F32),
            pltpu.VMEM((rows * heads, hd), F32),
            pltpu.VMEM((rows * heads, hd), F32),
            pltpu.VMEM((rows, q_cols), F32),
        ],
        compiler_params=pltpu.CompilerParams(vmem_limit_bytes=48 << 20),
        name="attend",
    )(queries, fresh, blocks, pad_rows, row_pos)

    ring = 8
    attn_out, back = pl.pallas_call(
        project_out,
        out_shape=(
            jax.ShapeDtypeStruct((rows, q_cols), BF16),
            jax.ShapeDtypeStruct((2, stretches, PAD, hd), BF16),
        ),
        in_specs=[smem, smem, vmem, hbm, vmem],
        out_specs=(vmem, vmem),
        scratch_shapes=[
            pltpu.VMEM((2 * ring, depth, q_cols), BF16),
            pltpu.VMEM((ring, rows, q_cols), BF16),
            pltpu.VMEM((ring, rows, q_cols), BF16),
            pltpu.VMEM((ring, rows, q_cols), BF16),
            pltpu.VMEM((4, rows, q_cols), BF16),
            pltpu.VMEM((4, rows, q_cols), BF16),
            pltpu.VMEM((4, rows, q_cols), BF16),
            pltpu.VMEM((4, rows, q_cols), BF16),
            pltpu.VMEM((2 * owners, PAD, hd), BF16),
            pltpu.VMEM((2 * owners, PAD, hd), BF16),
            dma((2 * ring,)),
            dma((ring,)),
            dma((ring,)),
            dma((4, 2)),
            dma((4, 2)),
            dma((4, 2)),
            dma((4, 2)),
            dma((owners,)),
            dma((owners,)),
            dma((1,)),
            dma((1,)),
        ],
        compiler_params=pltpu.CompilerParams(collective_id=1, has_side_effects=True, vmem_limit_bytes=48 << 20),
        name="project_out",
    )(slot_r, pick, context, out_blocks, fresh.reshape(2, stretches, PAD, hd))

    new_store = pl.pallas_call(
        write_back,
        grid=(stretches,),
        out_shape=jax.ShapeDtypeStruct(kv_store.shape, BF16),
        in_specs=[
            pl.BlockSpec((1, 1, length, kv_width), lambda s: (s, 0, 0, 0)),
            pl.BlockSpec((2, 1, PAD, hd), lambda s: (0, s, 0, 0)),
            pl.BlockSpec((1, 1, PAD), lambda s: (s, 0, 0)),
        ],
        out_specs=pl.BlockSpec((1, 1, length, kv_width), lambda s: (s, 0, 0, 0)),
        name="write_back",
    )(kv_store, back, slot_rows.reshape(stretches, 1, PAD))
    return (attn_out, new_store)


def solution(mesh):
    placed = (
        P("cache", None),
        P(),
        P("cache", "heads"),
        P("heads"),
        P("cache", None),
        P(),
        P("heads", "cache"),
        P("cache", "heads", None, None),
        P(),
        P(),
        P(),
    )
    return jax.shard_map(
        shards,
        mesh=mesh,
        in_specs=placed,
        out_specs=(P("cache", "heads"), P("cache", "heads", None, None)),
        check_vma=False,
    )
```

time: 515 us -> 206 us (0.40)
  waiting for transfers between devices: 268 us -> 0.69 us
  Pallas kernels: 0 us -> 181 us
  local copies, waits for them, and re-layouts: 137 us -> 6.88 us
  other arithmetic: 37.2 us -> 1.4 us
  matrix products: 30.3 us -> 0 us
  starting transfers between devices: 22.8 us -> 0.04 us
    pallas_call x0 -> x4, Pallas kernels: none -> 181 us  [the longest x1 140 us: shards(): pl.pallas_call(gather_project, out_shape=(jax.ShapeDtypeStruct((rows * he...]
    all_to_all x3 -> x0, waiting for transfers between devices: 163 us -> none  [the longest x1 115 us: shards(): lax.all_to_all(outgoing, 'cache', split_axis=0, concat_axis=0, tiled=True)]
    scatter x3 -> x0, local copies, waits for them, and re-layouts: 105 us -> none  [the longest x1 81.7 us: shards(): store_local.at[target_slot[:, :, None], send_rows].set(inbound, mode='drop')]
    reduce_scatter x2 -> x0, waiting for transfers between devices: 74.3 us -> none  [the longest x1 74.2 us: shards(): lax.psum_scatter(jnp.concatenate([jnp.dot(slices, q_weight, preferred_ele...]
    dot_general x5 -> x0, matrix products: 30.3 us -> none  [the longest x1 7.54 us: shards(): jnp.einsum('qjd,kd->jqk', query_heads, keyvals[:, :head_dim], preferred_e...]
    all_gather x1, waiting for transfers between devices: 30.2 us -> 0.01 us  [shards(): out_blocks = lax.all_gather(out_weight, 'cache', axis=0, tiled=False)]
    all_to_all x3 -> x0, starting transfers between devices: 22.5 us -> none  [the longest x1 9.34 us: shards(): lax.all_to_all(outgoing, 'cache', split_axis=0, concat_axis=0, tiled=True)]
    sub x1 -> x0, other arithmetic: 17.3 us -> none  [shards(): expon = jnp.exp(scores - highest)]
  transfers between devices with their start and end apart: 6 -> 1, of which waited for: 5 -> 0; matrix products, arithmetic and copies ran while one was open for 32% -> 3% of each run, Pallas kernels for 0% -> 71%
where the time goes in v1:
time: 206 us; the launch traced here: 204 us
  Pallas kernels  181 us (88%)
  between operations  14.2 us (7%)
  local copies, waits for them, and re-layouts  6.88 us (3%)
    pallas_call x1, Pallas kernels, shards(): pl.pallas_call(gather_project, out_shape=(jax.ShapeDtypeStruct((rows * he...  140 us
    pallas_call x1, Pallas kernels, shards(): pl.pallas_call(project_out, out_shape=(jax.ShapeDtypeStruct((rows, q_cols...  30.3 us
    pallas_call x1, Pallas kernels, shards(): pl.pallas_call(write_back, grid=(stretches,), out_shape=jax.ShapeDtypeStr...  6.46 us
  transfers between devices with their start and end apart: 1, of which 0 were waited for; matrix products, arithmetic and copies ran while one was open for 3% of the time, Pallas kernels for 71%

profile of v1, /device:TPU:34, one launch (start us, length us, event | category | flops | bytes accessed | tf_op | source)
XLA Modules:
  0.0 204.4 jit_solution(3165438394887312213)
XLA Ops:
  7.2 0.0 copy-start
  7.2 0.0 all-gather.3.cloned.1.call-start
  7.2 0.7 all-gather.3.cloned.1.call-update
  7.9 0.7 dynamic-slice_bitcast_fusion
  8.6 0.2 reshape.152.pos_ref
  8.8 0.7 compare_select_fusion
  9.5 0.1 copy.28
  9.6 0.1 reshape.142
  9.7 0.7 reshape.132.gain_ref
  10.4 0.7 reshape.134.kvb_ref
  11.1 0.7 reshape.133.qb_ref
  11.8 0.0 copy-start.1
  11.8 1.2 gather_fusion
  13.1 0.1 reshape.141
  13.2 0.1 copy.29
  13.3 0.1 convert_reduce_fusion
  13.4 0.2 dynamic-slice_reduce_fusion
  13.6 0.1 copy.33
  13.6 0.1 add.61
  13.7 0.1 copy.35
  13.8 0.1 compare_convert_fusion
  13.9 0.2 multiply_reduce_fusion
  14.1 0.6 pad.8
  14.7 140.4 %gather_project.1 = (bf16[768,128]{1,0:T(8,128)(2,1)S(1)}, bf16[2,256,128]{2,1,0:T(8,128)(2,1)S(1)}, bf16[8,16,2,16,256]{4,3,2,1,0:T(8,128)(2,1)S(1)}) custom-call(s32[128]{0:T(128)S(1)} %gather_fusion, bf16[192,8192]{1,0:T(8,128)(2,1)} %hid_hbm.1, bf16[1,8192]{1,0:T(2,128)(2,1)S(1)} %reshape.132.gain_ref, bf16[512,512]{1,0:T(8,128)(2,1)S(1)} %copy-done.2, ...), custom_call_target="tpu_custom_call" | custom-call | tf_op jit(solution)/shard_map/gather_project/pallas_call | solution.py:512
  155.1 4.1 %attend.1.ctx_ref = bf16[192,512]{1,0:T(8,128)(2,1)S(1)} custom-call(bf16[768,128]{1,0:T(8,128)(2,1)S(1)} %get-tuple-element.7.q_ref, bf16[2,256,128]{2,1,0:T(8,128)(2,1)S(1)} %get-tuple-element.8.fresh_ref, bf16[8,512,256]{2,1,0:T(8,128)(2,1)S(1)} %bitcast.8, s32[8,32]{1,0:T(8,128)S(1)} %pad.7.row_ref, s32[768,1]{1,0:T(8,128)S(1)} %reshape.152.pos_ref), custom_call_target="tpu_custom_call" | custom-call | tf_op jit(solution)/shard_map/attend/pallas_call | solution.py:548
  159.2 0.1 select_reduce_fusion.slot_ref
  159.3 0.2 fusion.pick_ref
  159.4 0.0 all-gather.3.cloned.1.call-done
  159.5 30.3 %project_out.1 = (bf16[192,512]{1,0:T(8,128)(2,1)S(1)}, bf16[2,8,32,128]{3,2,1,0:T(8,128)(2,1)S(1)}) custom-call(s32[32]{0:T(128)S(1)} %select_reduce_fusion.slot_ref, s32[8]{0:T(128)S(1)} %fusion.pick_ref, bf16[192,512]{1,0:T(8,128)(2,1)S(1)} %attend.1.ctx_ref, bf16[16,512,512]{2,1,0:T(8,128)(2,1)} %bitcast.10, bf16[2,8,32,128]{3,2,1,0:T(8,128)(2,1)S(1)} %bitcast.9), custom_call_target="tpu_custom_call" | custom-call | tf_op jit(solution)/shard_map/project_out/pallas_call | solution.py:567
  189.7 0.6 copy-done.3
  190.4 6.5 %write_back.1 = bf16[8,1,512,256]{3,2,1,0:T(8,128)(2,1)} custom-call(bf16[8,1,512,256]{3,2,1,0:T(8,128)(2,1)} %store_ref.1, bf16[2,8,32,128]{3,2,1,0:T(8,128)(2,1)} %copy-done.3, s32[8,1,32]{2,1,0:T(1,128)} %bitcast.13), custom_call_target="tpu_custom_call" | custom-call | tf_op jit(solution)/shard_map/write_back/pallas_call | solution.py:602
  196.8 0.7 copy.37
  (15 shorter events, 0.1 us)
Async XLA Ops:
  7.2 4.6 %copy-start = (s32[128]{0:T(128)S(1)}, s32[128]{0:T(128)}, u32[]{:S(2)}) copy-start(s32[128]{0:T(128)} %param.19) | copy-start | bytes 1540
  7.2 152.3 %all-gather.3.cloned.1.call-start = ((), (), s32[]{:S(2)}) async-start(), calls=%async_computation | async-start | bytes 8912896 | tf_op jit(solution)/shard_map/all_gather | solution.py:489
  11.8 1.9 copy-start.4
  11.8 2.9 %copy-start.1 = (bf16[512,2048]{1,0:T(8,128)(2,1)S(1)}, bf16[512,2048]{1,0:T(8,128)(2,1)}, u32[]{:S(2)}) copy-start(bf16[512,2048]{1,0:T(8,128)(2,1)} %kvw_hbm.1) | copy-start | bytes 6291460
  11.8 2.9 %copy-start.2 = (bf16[512,512]{1,0:T(8,128)(2,1)S(1)}, bf16[512,512]{1,0:T(8,128)(2,1)}, u32[]{:S(2)}) copy-start(bf16[512,512]{1,0:T(8,128)(2,1)} %qw_hbm.1) | copy-start | bytes 1572868
  189.7 0.7 copy-start.3
Sparse Core Ops, SparseCore 0:
  10.4 121.2 all-gather.2

commit v2 on v1

--- a/solution.py
+++ b/solution.py
@@ -12,6 +12,7 @@
 SIDE = 4
 BF16 = jnp.bfloat16
 F32 = jnp.float32
+RIGHT, OPPOSITE, LEFT = 1, 2, 3
 PAD = 32
 
 
@@ -19,6 +20,78 @@
     return pltpu.make_async_remote_copy(
         src_ref=src, dst_ref=dst, send_sem=send_sem, recv_sem=recv_sem, device_id=device, device_id_type=MESH
     )
+
+
+class Spread:
+    def __init__(self, piece, send_sem, recv_sem, me, head):
+        self.piece, self.send_sem, self.recv_sem, self.head = piece, send_sem, recv_sem, head
+        self.me, self.x, self.y = me, me // SIDE, lax.rem(me, SIDE)
+        self.sends = []
+
+    def at(self, dx, dy):
+        return lax.rem(self.x + dx, SIDE) * SIDE + lax.rem(self.y + dy, SIDE)
+
+    def along(self, axis, d, s=0):
+        return self.at(d, s) if axis == 0 else self.at(s, d)
+
+    def go(self, c, u, axis, d):
+        piece = self.piece(c, u)
+        copy = remote(
+            piece, piece, self.send_sem.at[len(self.sends)], self.recv_sem.at[c, u], (self.along(axis, d), self.head)
+        )
+        copy.start()
+        self.sends.append(copy)
+
+    def arrived(self, c, u):
+        piece = self.piece(c, u)
+        remote(piece, piece, self.send_sem.at[0], self.recv_sem.at[c, u], (self.at(1, 0), self.head)).wait_recv()
+
+    def both(self, c, axis, direction):
+        for u in (0, 1):
+            for d in (RIGHT, LEFT):
+                self.go(c, 2 * axis + u, direction, d)
+
+    def start(self):
+        for u in (0, 1):
+            for axis in (0, 1):
+                for d in (RIGHT, LEFT):
+                    self.go(self.me, 2 * axis + u, axis, d)
+
+    def first(self):
+        for axis in (0, 1):
+            self.arrived(self.along(axis, LEFT), 2 * axis)
+            self.go(self.along(axis, LEFT), 2 * axis, axis, RIGHT)
+            self.arrived(self.along(axis, RIGHT), 2 * axis + 1)
+            self.go(self.along(axis, RIGHT), 2 * axis + 1, axis, LEFT)
+        for axis in (0, 1):
+            self.both(self.me, axis, 1 - axis)
+
+    def turn(self):
+        for axis in (0, 1):
+            self.arrived(self.along(axis, LEFT), 2 * axis + 1)
+            self.arrived(self.along(axis, RIGHT), 2 * axis)
+            for s in (LEFT, RIGHT):
+                self.both(self.along(axis, s), axis, 1 - axis)
+        for axis in (0, 1):
+            self.arrived(self.along(axis, OPPOSITE), 2 * axis)
+            self.arrived(self.along(axis, OPPOSITE), 2 * axis + 1)
+            self.both(self.along(axis, OPPOSITE), axis, 1 - axis)
+
+    def second(self, s):
+        for axis in (0, 1):
+            self.arrived(self.along(axis, s, LEFT), 2 * axis)
+            self.go(self.along(axis, s, LEFT), 2 * axis, 1 - axis, RIGHT)
+            self.arrived(self.along(axis, s, RIGHT), 2 * axis + 1)
+            self.go(self.along(axis, s, RIGHT), 2 * axis + 1, 1 - axis, LEFT)
+        for axis in (0, 1):
+            self.arrived(self.along(axis, s, LEFT), 2 * axis + 1)
+            self.arrived(self.along(axis, s, RIGHT), 2 * axis)
+            self.arrived(self.along(axis, s, OPPOSITE), 2 * axis)
+            self.arrived(self.along(axis, s, OPPOSITE), 2 * axis + 1)
+
+    def finish(self):
+        for copy in self.sends:
+            copy.wait_send()
 
 
 def gather_project(
@@ -31,16 +104,12 @@
     head = lax.axis_index("heads")
     core = lax.rem(head, 2)
     partner = (me, head + 1 - 2 * core)
-    x, y = me // SIDE, lax.rem(me, SIDE)
     owners = SIDE * SIDE
     rows = hid.shape[0]
     depth, width = w.shape[1], w.shape[2]
     unit, half = depth // 4, depth // 2
     q_cols = qw_hbm.shape[1]
     hd = width - q_cols
-
-    def at(dx, dy):
-        return lax.rem(x + dx, SIDE) * SIDE + lax.rem(y + dy, SIDE)
 
     own_q = pltpu.make_async_copy(qw_hbm, w.at[me, :, 0:q_cols], loc.at[0])
     own_kv = pltpu.make_async_copy(
@@ -89,31 +158,8 @@
     own_q.wait()
     own_kv.wait()
 
-    sends = []
-
-    def piece(c, u):
-        return w.at[c, pl.ds(u * unit, unit)]
-
-    def send(c, u, dx, dy):
-        copy = remote(piece(c, u), piece(c, u), w_send.at[len(sends)], w_recv.at[c, u], (at(dx, dy), head))
-        copy.start()
-        sends.append(copy)
-
-    def arrived(c, u):
-        remote(piece(c, u), piece(c, u), w_send.at[0], w_recv.at[c, u], (at(1, 0), head)).wait_recv()
-
-    L, O, R = SIDE - 1, 2, 1
-
-    def first(axis, d):
-        return at(d, 0) if axis == 0 else at(0, d)
-
-    def go(c, u, axis, d):
-        send(c, u, d if axis == 0 else 0, d if axis == 1 else 0)
-
-    for u in (0, 1):
-        for axis in (0, 1):
-            for d in (R, L):
-                go(me, 2 * axis + u, axis, d)
+    spread = Spread(lambda c, u: w.at[c, pl.ds(u * unit, unit)], w_send, w_recv, me, head)
+    spread.start()
 
     own_hid.wait()
     tall = 16
@@ -137,15 +183,7 @@
         lo = axis * half
         acc[...] += jnp.dot(nrm[c, :, lo : lo + half], w[c, lo : lo + half, :], preferred_element_type=F32)
 
-    for axis in (0, 1):
-        arrived(first(axis, L), 2 * axis)
-        go(first(axis, L), 2 * axis, axis, R)
-        arrived(first(axis, R), 2 * axis + 1)
-        go(first(axis, R), 2 * axis + 1, axis, L)
-    for axis in (0, 1):
-        for u in (0, 1):
-            for d in (R, L):
-                go(me, 2 * axis + u, 1 - axis, d)
+    spread.first()
 
     own_hop.wait()
 
@@ -165,49 +203,25 @@
     own_out = pltpu.make_async_copy(hop_out.at[me], blocks_hbm.at[:, me, core], loc.at[4])
     own_out.start()
 
-    for axis in (0, 1):
-        arrived(first(axis, L), 2 * axis + 1)
-        arrived(first(axis, R), 2 * axis)
-        for s in (L, R):
-            for u in (0, 1):
-                for d in (R, L):
-                    go(first(axis, s), 2 * axis + u, 1 - axis, d)
-    for axis in (0, 1):
-        arrived(first(axis, O), 2 * axis)
-        arrived(first(axis, O), 2 * axis + 1)
-        for u in (0, 1):
-            for d in (R, L):
-                go(first(axis, O), 2 * axis + u, 1 - axis, d)
+    spread.turn()
 
     @pl.loop(0, SIDE)
     def _(i):
-        multiply(at(i, 0), 0)
-        multiply(at(0, i), 1)
-
-    def second(axis, s, d):
-        return at(s, d) if axis == 0 else at(d, s)
+        multiply(spread.along(0, i), 0)
+        multiply(spread.along(1, i), 1)
 
     def core_swap(which):
         return remote(
             blocks_hbm.at[:, :, which], blocks_hbm.at[:, :, which], x_send.at[0], x_recv.at[0], partner
         )
 
-    for n, s in enumerate((0, L, R, O)):
-        for axis in (0, 1):
-            arrived(second(axis, s, L), 2 * axis)
-            go(second(axis, s, L), 2 * axis, 1 - axis, R)
-            arrived(second(axis, s, R), 2 * axis + 1)
-            go(second(axis, s, R), 2 * axis + 1, 1 - axis, L)
-        for axis in (0, 1):
-            arrived(second(axis, s, L), 2 * axis + 1)
-            arrived(second(axis, s, R), 2 * axis)
-            arrived(second(axis, s, O), 2 * axis)
-            arrived(second(axis, s, O), 2 * axis + 1)
+    for n, s in enumerate((0, LEFT, RIGHT, OPPOSITE)):
+        spread.second(s)
 
         @pl.loop(1, SIDE)
         def _(i):
-            multiply(second(0, s, i), 0)
-            multiply(second(1, s, i), 1)
+            multiply(spread.along(0, s, i), 0)
+            multiply(spread.along(1, s, i), 1)
 
         if n == 2:
             own_out.wait()
@@ -238,8 +252,7 @@
     remote(fresh_ref.at[1 - core], fresh_ref.at[1 - core], x_send.at[1], x_recv.at[1], partner).wait_recv()
     swap.wait_send()
     core_swap(core).wait_send()
-    for copy in sends:
-        copy.wait_send()
+    spread.finish()
 
     @pl.loop(1, owners)
     def _(o):
@@ -305,10 +318,10 @@
 
 
 def project_out(
-    slot_ref, pick_ref, ctx_ref, w_hbm, fresh_ref,
+    slot_ref, pick_ref, ctx_ref, w_ref, fresh_ref,
     out_ref, back_ref,
-    w, pair_out, pair_in, own, r_out, l_out, r_in, l_in, f_out, f_in,
-    w_sem, p_send, p_recv, r_send, r_recv, l_send, l_recv, f_send, f_recv, b_send, b_recv,
+    ctxs, pair_out, pair_in, own, r_out, l_out, r_in, l_in, f_out, f_in, total_out,
+    c_send, c_recv, p_send, p_recv, r_send, r_recv, l_send, l_recv, f_send, f_recv, b_send, b_recv,
 ):
     me = lax.axis_index("cache")
     head = lax.axis_index("heads")
@@ -319,20 +332,13 @@
     partner = (me, head + 1 - 2 * core)
     right = (me, lax.rem(z + 1, ring) * 2 + core)
     left = (me, lax.rem(z + ring - 1, ring) * 2 + core)
+    mirror = (head, me)
     rows = ctx_ref.shape[0]
     hrow = rows // 2
     order = (4, 3, -3, 2, -2, 1, -1, 0)
 
-    def column(n, parity):
+    def request(n, parity):
         return lax.rem(z + order[n] + ring, ring) * 2 + parity
-
-    def fetch(n, which):
-        block = column(n, 1 - core if which == 0 else core)
-        return pltpu.make_async_copy(w_hbm.at[block], w.at[2 * n + which], w_sem.at[2 * n + which])
-
-    for n in range(len(order)):
-        for which in (0, 1):
-            fetch(n, which).start()
 
     barrier = pltpu.get_barrier_semaphore()
 
@@ -342,7 +348,24 @@
 
     for peer in (partner, left, right):
         pl.semaphore_signal(barrier, inc=1, device_id=peer, device_id_type=MESH)
-    pl.semaphore_wait(barrier, owners + 2)
+
+    @pl.when(me != head)
+    def _():
+        pl.semaphore_signal(barrier, inc=1, device_id=mirror, device_id_type=MESH)
+
+    ctxs[me] = ctx_ref[...]
+
+    @pl.when(me != head)
+    def _():
+        pl.semaphore_wait(barrier, owners + 3)
+
+    @pl.when(me == head)
+    def _():
+        pl.semaphore_wait(barrier, owners + 2)
+
+    quarter = rows // 4
+    spread = Spread(lambda c, u: ctxs.at[c, pl.ds(u * quarter, quarter)], c_send, c_recv, me, head)
+    spread.start()
 
     @pl.loop(0, owners)
     def _(o):
@@ -361,22 +384,26 @@
             f_out.at[pl.ds(2 * src, 2)], f_in.at[pl.ds(2 * src, 2)], f_send.at[o], f_recv.at[src], (src, head)
         )
 
-    @pl.loop(1, owners)
-    def _(o):
-        give(o).start()
-
     for m in range(2):
         f_in[2 * me + m] = f_out[2 * me + m]
 
+    spread.first()
+    spread.turn()
+
+    @pl.loop(1, owners)
+    def _(o):
+        give(o).start()
+
+    for s in (0, LEFT, RIGHT, OPPOSITE):
+        spread.second(s)
+
     def pair(n):
         return remote(pair_out.at[n], pair_in.at[n], p_send.at[n], p_recv.at[n], partner)
 
     for n in range(len(order)):
-        fetch(n, 0).wait()
-        pair_out[n] = jnp.dot(ctx_ref[...], w[2 * n], preferred_element_type=F32).astype(BF16)
+        pair_out[n] = jnp.dot(ctxs[request(n, 1 - core)], w_ref[...], preferred_element_type=F32).astype(BF16)
         pair(n).start()
-        fetch(n, 1).wait()
-        own[n] = jnp.dot(ctx_ref[...], w[2 * n + 1], preferred_element_type=F32).astype(BF16)
+        own[n] = jnp.dot(ctxs[request(n, core)], w_ref[...], preferred_element_type=F32).astype(BF16)
 
     def lines(part):
         return slice(part * hrow, (part + 1) * hrow)
@@ -437,7 +464,17 @@
         rightward(3, part).wait_recv()
         leftward(3, part).wait_recv()
         value = total(7, part) + r_in[3, lines(part), :].astype(F32) + l_in[3, lines(part), :].astype(F32)
-        out_ref[lines(part), :] = value.astype(BF16)
+        total_out[lines(part), :] = value.astype(BF16)
+
+    flip = remote(total_out, out_ref, b_send.at[1], b_recv.at[1], mirror)
+
+    @pl.when(me != head)
+    def _():
+        flip.start()
+
+    @pl.when(me == head)
+    def _():
+        out_ref[...] = total_out[...]
 
     remote(back_ref.at[1 - core], back_ref.at[1 - core], b_send.at[0], b_recv.at[0], partner).wait_recv()
     swap.wait_send()
@@ -453,6 +490,12 @@
     @pl.loop(1, owners)
     def _(o):
         give(o).wait_send()
+
+    spread.finish()
+
+    @pl.when(me != head)
+    def _():
+        flip.wait()
 
 
 def write_back(store_ref, back_ref, row_ref, new_ref):
@@ -485,8 +528,6 @@
     smem = pl.BlockSpec(memory_space=pltpu.SMEM)
     hbm = pl.BlockSpec(memory_space=pl.ANY)
     dma = pltpu.SemaphoreType.DMA
-
-    out_blocks = lax.all_gather(out_weight, "cache", axis=0, tiled=False)
 
     places = stretch_place[req_stretches]
     owner_of = places // stretches
@@ -570,10 +611,10 @@
             jax.ShapeDtypeStruct((rows, q_cols), BF16),
             jax.ShapeDtypeStruct((2, stretches, PAD, hd), BF16),
         ),
-        in_specs=[smem, smem, vmem, hbm, vmem],
+        in_specs=[smem, smem, vmem, vmem, vmem],
         out_specs=(vmem, vmem),
         scratch_shapes=[
-            pltpu.VMEM((2 * ring, depth, q_cols), BF16),
+            pltpu.VMEM((owners, rows, q_cols), BF16),
             pltpu.VMEM((ring, rows, q_cols), BF16),
             pltpu.VMEM((ring, rows, q_cols), BF16),
             pltpu.VMEM((ring, rows, q_cols), BF16),
@@ -583,7 +624,9 @@
             pltpu.VMEM((4, rows, q_cols), BF16),
             pltpu.VMEM((2 * owners, PAD, hd), BF16),
             pltpu.VMEM((2 * owners, PAD, hd), BF16),
-            dma((2 * ring,)),
+            pltpu.VMEM((rows, q_cols), BF16),
+            dma((60,)),
+            dma((owners, 4)),
             dma((ring,)),
             dma((ring,)),
             dma((4, 2)),
@@ -592,12 +635,12 @@
             dma((4, 2)),
             dma((owners,)),
             dma((owners,)),
-            dma((1,)),
-            dma((1,)),
+            dma((2,)),
+            dma((2,)),
         ],
         compiler_params=pltpu.CompilerParams(collective_id=1, has_side_effects=True, vmem_limit_bytes=48 << 20),
         name="project_out",
-    )(slot_r, pick, context, out_blocks, fresh.reshape(2, stretches, PAD, hd))
+    )(slot_r, pick, context, out_weight, fresh.reshape(2, stretches, PAD, hd))
 
     new_store = pl.pallas_call(
         write_back,

time: 206 us -> 201 us (0.976)
  between operations: 14.2 us -> 0.87 us
  Pallas kernels: 181 us -> 193 us
    pallas_call x1, Pallas kernels: 30.3 us -> 83.8 us  [shards(): pl.pallas_call(project_out, out_shape=(jax.ShapeDtypeStruct((rows, q_cols...]
    pallas_call x1, Pallas kernels: 140 us -> 99 us  [shards(): pl.pallas_call(gather_project, out_shape=(jax.ShapeDtypeStruct((rows * he...]
  transfers between devices with their start and end apart: 1 -> 0, of which waited for: 0 -> 0; matrix products, arithmetic and copies ran while one was open for 3% -> 0% of each run, Pallas kernels for 71% -> 0%
where the time goes in v2:
time: 201 us
  Pallas kernels  193 us (96%)
  local copies, waits for them, and re-layouts  5.17 us (3%)
    pallas_call x1, Pallas kernels, shards(): pl.pallas_call(gather_project, out_shape=(jax.ShapeDtypeStruct((rows * he...  99 us
    pallas_call x1, Pallas kernels, shards(): pl.pallas_call(project_out, out_shape=(jax.ShapeDtypeStruct((rows, q_cols...  83.8 us
    pallas_call x1, Pallas kernels, shards(): pl.pallas_call(write_back, grid=(stretches,), out_shape=jax.ShapeDtypeStr...  6.45 us
    pallas_call x1, Pallas kernels, shards(): pl.pallas_call(attend, out_shape=jax.ShapeDtypeStruct((rows, q_cols), BF1...  4.1 us

profile of v2, /device:TPU:34, one launch (start us, length us, event | category | flops | bytes accessed | tf_op | source)
XLA Modules:
  0.0 200.7 jit_solution(3642035647631797911)
XLA Ops:
  0.6 0.0 copy-start
  0.6 0.7 dynamic-slice_bitcast_fusion
  1.3 0.2 reshape.151.pos_ref
  1.5 0.7 compare_select_fusion
  2.2 0.1 copy.28
  2.3 0.1 reshape.142
  2.4 0.0 copy-start.6
  2.4 0.0 copy-start.8
  2.5 0.0 copy-start.1
  2.5 1.2 gather_fusion
  3.8 0.3 copy-done.1
  4.1 0.1 copy-done.3
  4.1 99.0 %gather_project.1 = (bf16[768,128]{1,0:T(8,128)(2,1)S(1)}, bf16[2,256,128]{2,1,0:T(8,128)(2,1)S(1)}, bf16[8,16,2,16,256]{4,3,2,1,0:T(8,128)(2,1)S(1)}) custom-call(s32[128]{0:T(128)S(1)} %gather_fusion, bf16[192,8192]{1,0:T(8,128)(2,1)} %hid_hbm.1, bf16[1,8192]{1,0:T(2,128)(2,1)S(1)} %reshape.132.gain_ref, bf16[512,512]{1,0:T(8,128)(2,1)S(1)} %copy-done.3, ...), custom_call_target="tpu_custom_call" | custom-call | tf_op jit(solution)/shard_map/gather_project/pallas_call | solution.py:553
  103.1 0.0 copy-start.5
  103.2 4.1 %attend.1.ctx_ref = bf16[192,512]{1,0:T(8,128)(2,1)S(1)} custom-call(bf16[768,128]{1,0:T(8,128)(2,1)S(1)} %get-tuple-element.7.q_ref, bf16[2,256,128]{2,1,0:T(8,128)(2,1)S(1)} %get-tuple-element.8.fresh_ref, bf16[8,512,256]{2,1,0:T(8,128)(2,1)S(1)} %bitcast.7, s32[8,32]{1,0:T(8,128)S(1)} %pad.7.row_ref, s32[768,1]{1,0:T(8,128)S(1)} %reshape.151.pos_ref), custom_call_target="tpu_custom_call" | custom-call | tf_op jit(solution)/shard_map/attend/pallas_call | solution.py:589
  107.3 0.1 reshape.141
  107.3 0.1 copy.29
  107.4 0.1 convert_reduce_fusion
  107.6 0.2 dynamic-slice_reduce_fusion
  107.8 0.1 select_reduce_fusion.slot_ref
  107.8 0.1 copy.33
  107.9 0.1 add.61
  108.0 0.2 fusion.pick_ref
  108.2 83.8 %project_out.1 = (bf16[192,512]{1,0:T(8,128)(2,1)S(1)}, bf16[2,8,32,128]{3,2,1,0:T(8,128)(2,1)S(1)}) custom-call(s32[32]{0:T(128)S(1)} %select_reduce_fusion.slot_ref, s32[8]{0:T(128)S(1)} %fusion.pick_ref, bf16[192,512]{1,0:T(8,128)(2,1)S(1)} %attend.1.ctx_ref, bf16[512,512]{1,0:T(8,128)(2,1)S(1)} %copy-done.2, bf16[2,8,32,128]{3,2,1,0:T(8,128)(2,1)S(1)} %bitcast.8), custom_call_target="tpu_custom_call" | custom-call | tf_op jit(solution)/shard_map/project_out/pallas_call | solution.py:608
  192.0 0.0 copy-start.4
  192.0 0.6 copy-done.4
  192.6 0.1 compare_convert_fusion
  192.7 0.1 copy.35
  192.8 0.2 multiply_reduce_fusion
  193.0 0.6 pad.8
  193.6 6.5 %write_back.1 = bf16[8,1,512,256]{3,2,1,0:T(8,128)(2,1)} custom-call(bf16[8,1,512,256]{3,2,1,0:T(8,128)(2,1)} %store_ref.1, bf16[2,8,32,128]{3,2,1,0:T(8,128)(2,1)} %copy-done.4, s32[8,1,32]{2,1,0:T(1,128)} %bitcast.11), custom_call_target="tpu_custom_call" | custom-call | tf_op jit(solution)/shard_map/write_back/pallas_call | solution.py:645
  200.1 0.7 copy.37
  (20 shorter events, 0.1 us)
Async XLA Ops:
  0.6 1.8 copy-start
  2.4 1.3 copy-start.6
  2.4 1.3 copy-start.7
  2.4 1.3 copy-start.8
  2.5 1.6 copy-start.1
  2.5 1.7 copy-start.3
  103.1 5.1 %copy-start.2 = (bf16[512,512]{1,0:T(8,128)(2,1)S(1)}, bf16[512,512]{1,0:T(8,128)(2,1)}, u32[]{:S(2)}) copy-start(bf16[512,512]{1,0:T(8,128)(2,1)} %w_ref.1) | copy-start | bytes 1572868
  103.1 89.6 %copy-start.5 = (s32[16,8,24]{2,1,0:T(8,128)S(1)}, s32[16,8,24]{2,1,0:T(8,128)}, u32[]{:S(2)}) copy-start(s32[16,8,24]{2,1,0:T(8,128)} %param.21) | copy-start | bytes 36868
  192.0 0.7 copy-start.4

commit v3 on v2

--- a/solution.py
+++ b/solution.py
@@ -97,30 +97,34 @@
 def gather_project(
     place_ref, hid_hbm, gain_ref, qw_hbm, kvw_hbm, qb_ref, kvb_ref, store_hbm,
     q_ref, fresh_ref, blocks_hbm,
-    hid, nrm, w, acc, hop_in, hop_out, qs, fpad,
-    loc, w_send, w_recv, h1_send, h1_recv, h2_send, h2_recv, x_send, x_recv,
+    hid, nrm, acts, w, acc, part, sums, hop_in, hop_out, qs, fpad,
+    loc, w_send, w_recv, a_send, a_recv, c_send, c_recv, s_send, s_recv,
+    h1_send, h1_recv, h2_send, h2_recv, x_send, x_recv,
 ):
     me = lax.axis_index("cache")
     head = lax.axis_index("heads")
     core = lax.rem(head, 2)
     partner = (me, head + 1 - 2 * core)
+    x, y = me // SIDE, lax.rem(me, SIDE)
     owners = SIDE * SIDE
     rows = hid.shape[0]
     depth, width = w.shape[1], w.shape[2]
-    unit, half = depth // 4, depth // 2
     q_cols = qw_hbm.shape[1]
     hd = width - q_cols
 
-    own_q = pltpu.make_async_copy(qw_hbm, w.at[me, :, 0:q_cols], loc.at[0])
+    def ring(i, d):
+        return lax.rem(i + d, SIDE)
+
+    own_hid = pltpu.make_async_copy(hid_hbm, hid, loc.at[2])
+    own_q = pltpu.make_async_copy(qw_hbm, w.at[x, :, 0:q_cols], loc.at[0])
     own_kv = pltpu.make_async_copy(
-        kvw_hbm.at[:, pl.ds(pl.multiple_of(head * hd, hd), hd)], w.at[me, :, q_cols:width], loc.at[1]
+        kvw_hbm.at[:, pl.ds(pl.multiple_of(head * hd, hd), hd)], w.at[x, :, q_cols:width], loc.at[1]
     )
-    own_hid = pltpu.make_async_copy(hid_hbm, hid, loc.at[2])
     own_hop = pltpu.make_async_copy(store_hbm.at[:, me, core], hop_in.at[pl.ds(me * 8, 8)], loc.at[3])
+    own_hid.start()
     own_q.start()
     own_kv.start()
     own_hop.start()
-    own_hid.start()
 
     barrier = pltpu.get_barrier_semaphore()
 
@@ -129,37 +133,6 @@
         pl.semaphore_signal(barrier, inc=1, device_id=(lax.rem(me + o, owners), head), device_id_type=MESH)
 
     pl.semaphore_signal(barrier, inc=1, device_id=partner, device_id_type=MESH)
-    pl.semaphore_wait(barrier, owners)
-
-    def hop1(o):
-        to = lax.rem(me + o, owners)
-        return remote(
-            store_hbm.at[:, to, core], hop_in.at[pl.ds(me * 8, 8)], h1_send.at[o], h1_recv.at[me], (to, head)
-        )
-
-    def hop1_from(o):
-        src = lax.rem(me + owners - o, owners)
-        return remote(
-            store_hbm.at[:, src, core], hop_in.at[pl.ds(src * 8, 8)], h1_send.at[o], h1_recv.at[src], (src, head)
-        )
-
-    def hop2(o):
-        to = lax.rem(me + o, owners)
-        return remote(hop_out.at[to], blocks_hbm.at[:, me, core], h2_send.at[o], h2_recv.at[me], (to, head))
-
-    def hop2_from(o):
-        src = lax.rem(me + owners - o, owners)
-        return remote(hop_out.at[src], blocks_hbm.at[:, src, core], h2_send.at[o], h2_recv.at[src], (src, head))
-
-    @pl.loop(1, owners)
-    def _(o):
-        hop1(o).start()
-
-    own_q.wait()
-    own_kv.wait()
-
-    spread = Spread(lambda c, u: w.at[c, pl.ds(u * unit, unit)], w_send, w_recv, me, head)
-    spread.start()
 
     own_hid.wait()
     tall = 16
@@ -177,13 +150,73 @@
             g = gain_ref[:, c * depth : (c + 1) * depth].astype(F32)
             nrm[c, lines, :] = (v * factor * g).astype(BF16)
 
-    acc[...] = jnp.zeros_like(acc)
-
-    def multiply(c, axis):
-        lo = axis * half
-        acc[...] += jnp.dot(nrm[c, :, lo : lo + half], w[c, lo : lo + half, :], preferred_element_type=F32)
-
-    spread.first()
+    pl.semaphore_wait(barrier, owners)
+
+    def rows_to(d, i):
+        to = ring(y, d)
+        return remote(
+            nrm.at[(2 * core + i) * SIDE + to], acts.at[2 * core + i, y], a_send.at[d, i], a_recv.at[d, i],
+            (x * SIDE + to, head),
+        )
+
+    def hop1(o):
+        to = lax.rem(me + o, owners)
+        return remote(
+            store_hbm.at[:, to, core], hop_in.at[pl.ds(me * 8, 8)], h1_send.at[o], h1_recv.at[me], (to, head)
+        )
+
+    def hop1_from(o):
+        src = lax.rem(me + owners - o, owners)
+        return remote(
+            store_hbm.at[:, src, core], hop_in.at[pl.ds(src * 8, 8)], h1_send.at[o], h1_recv.at[src], (src, head)
+        )
+
+    def hop2(o):
+        to = lax.rem(me + o, owners)
+        return remote(hop_out.at[to], blocks_hbm.at[:, me, core], h2_send.at[o], h2_recv.at[me], (to, head))
+
+    def hop2_from(o):
+        src = lax.rem(me + owners - o, owners)
+        return remote(hop_out.at[src], blocks_hbm.at[:, src, core], h2_send.at[o], h2_recv.at[src], (src, head))
+
+    def weights_to(d):
+        to = ring(x, d)
+        return remote(w.at[x], w.at[x], w_send.at[d], w_recv.at[d], (to * SIDE + y, head))
+
+    def weights_from(d):
+        src = ring(x, SIDE - d)
+        return remote(w.at[src], w.at[src], w_send.at[d], w_recv.at[d], (src * SIDE + y, head))
+
+    steps = (RIGHT, LEFT, OPPOSITE)
+    for i in (0, 1):
+        for d in steps:
+            rows_to(d, i).start()
+
+    @pl.loop(1, owners)
+    def _(o):
+        hop1(o).start()
+
+    own_q.wait()
+    own_kv.wait()
+    for d in steps:
+        weights_to(d).start()
+
+    for i in range(SIDE):
+        pltpu.make_async_copy(nrm.at[i * SIDE + y], acts.at[i, y], loc.at[5 + i]).start()
+
+    def rows_from(d, i, which):
+        src = ring(y, SIDE - d)
+        place = acts.at[2 * which + i, src]
+        return remote(place, place, a_send.at[d, i], a_recv.at[d, i], (x * SIDE + src, head))
+
+    def rows_over(d, i, which):
+        place = acts.at[2 * which + i, ring(y, SIDE - d)]
+        return remote(place, place, c_send.at[d, i], c_recv.at[d, i], partner)
+
+    for i in (0, 1):
+        for d in steps:
+            rows_from(d, i, core).wait_recv()
+            rows_over(d, i, core).start()
 
     own_hop.wait()
 
@@ -203,34 +236,51 @@
     own_out = pltpu.make_async_copy(hop_out.at[me], blocks_hbm.at[:, me, core], loc.at[4])
     own_out.start()
 
-    spread.turn()
+    for i in range(SIDE):
+        pltpu.make_async_copy(nrm.at[i * SIDE + y], acts.at[i, y], loc.at[5 + i]).wait()
+    for d in steps:
+        weights_from(d).wait_recv()
+
+    def product(i, j):
+        return jnp.dot(acts[i, j], w[i], preferred_element_type=F32)
 
     @pl.loop(0, SIDE)
-    def _(i):
-        multiply(spread.along(0, i), 0)
-        multiply(spread.along(1, i), 1)
+    def _(j):
+        acc[j] = product(2 * core, j)
+        acc[j] += product(2 * core + 1, j)
+
+    for i in (0, 1):
+        for d in steps:
+            rows_over(d, i, 1 - core).wait_recv()
+
+    def sums_to(d):
+        to = ring(y, d)
+        return remote(part.at[d], sums.at[d], s_send.at[d], s_recv.at[d], (x * SIDE + to, head))
+
+    for d in (OPPOSITE, RIGHT, LEFT):
+        j = ring(y, d)
+        acc[j] += product(2 - 2 * core, j)
+        part[d] = (acc[j] + product(3 - 2 * core, j)).astype(BF16)
+        sums_to(d).start()
+    acc[y] += product(2 - 2 * core, y)
+    acc[y] += product(3 - 2 * core, y)
 
     def core_swap(which):
         return remote(
             blocks_hbm.at[:, :, which], blocks_hbm.at[:, :, which], x_send.at[0], x_recv.at[0], partner
         )
 
-    for n, s in enumerate((0, LEFT, RIGHT, OPPOSITE)):
-        spread.second(s)
-
-        @pl.loop(1, SIDE)
-        def _(i):
-            multiply(spread.along(0, s, i), 0)
-            multiply(spread.along(1, s, i), 1)
-
-        if n == 2:
-            own_out.wait()
-
-            @pl.loop(1, owners)
-            def _(o):
-                hop2_from(o).wait_recv()
-
-            core_swap(core).start()
+    own_out.wait()
+
+    @pl.loop(1, owners)
+    def _(o):
+        hop2_from(o).wait_recv()
+
+    core_swap(core).start()
+
+    for d in steps:
+        sums_to(d).wait_recv()
+        acc[y] += sums[d].astype(F32)
 
     per = rows // 8
     heads = q_cols // hd
@@ -240,24 +290,31 @@
         lines = slice(per * r, per * (r + 1))
         for j in range(heads):
             at_row = (r * heads + j) * per
-            qs[at_row : at_row + per, :] = acc[lines, j * hd : (j + 1) * hd] + bias[:, j * hd : (j + 1) * hd]
-        fpad[r * PAD : r * PAD + per, :] = acc[lines, q_cols:width] + kv_bias
+            qs[at_row : at_row + per, :] = acc[y, lines, j * hd : (j + 1) * hd] + bias[:, j * hd : (j + 1) * hd]
+        fpad[r * PAD : r * PAD + per, :] = acc[y, lines, q_cols:width] + kv_bias
         fpad[r * PAD + per : (r + 1) * PAD, :] = jnp.zeros((PAD - per, hd), F32)
     fresh_ref[core] = fpad[...].astype(BF16)
     swap = remote(fresh_ref.at[core], fresh_ref.at[core], x_send.at[1], x_recv.at[1], partner)
     swap.start()
     q_ref[...] = qs[...].astype(BF16)
 
+    for i in (0, 1):
+        for d in steps:
+            rows_to(d, i).wait_send()
+            rows_over(d, i, core).wait_send()
+    for d in steps:
+        weights_to(d).wait_send()
+        sums_to(d).wait_send()
+
+    @pl.loop(1, owners)
+    def _(o):
+        hop1(o).wait_send()
+        hop2(o).wait_send()
+
     core_swap(1 - core).wait_recv()
     remote(fresh_ref.at[1 - core], fresh_ref.at[1 - core], x_send.at[1], x_recv.at[1], partner).wait_recv()
     swap.wait_send()
     core_swap(core).wait_send()
-    spread.finish()
-
-    @pl.loop(1, owners)
-    def _(o):
-        hop1(o).wait_send()
-        hop2(o).wait_send()
 
 
 def attend(q_ref, fresh_ref, blocks_ref, row_ref, pos_ref, ctx_ref, ks, vs, sc, top, low, out, flat):
@@ -562,15 +619,24 @@
         scratch_shapes=[
             pltpu.VMEM((rows, width), BF16),
             pltpu.VMEM((owners, rows, depth), BF16),
-            pltpu.VMEM((owners, depth, q_cols + hd), BF16),
-            pltpu.VMEM((rows, q_cols + hd), F32),
+            pltpu.VMEM((SIDE, SIDE, rows, depth), BF16),
+            pltpu.VMEM((SIDE, depth, q_cols + hd), BF16),
+            pltpu.VMEM((SIDE, rows, q_cols + hd), F32),
+            pltpu.VMEM((SIDE, rows, q_cols + hd), BF16),
+            pltpu.VMEM((SIDE, rows, q_cols + hd), BF16),
             pltpu.VMEM((owners * stretches, piece, kv_width), BF16),
             pltpu.VMEM((owners, stretches, piece, kv_width), BF16),
             pltpu.VMEM((rows * heads, hd), F32),
             pltpu.VMEM((stretches * PAD, hd), F32),
-            dma((5,)),
-            dma((60,)),
-            dma((owners, 4)),
+            dma((5 + SIDE,)),
+            dma((SIDE,)),
+            dma((SIDE,)),
+            dma((SIDE, 2)),
+            dma((SIDE, 2)),
+            dma((SIDE, 2)),
+            dma((SIDE, 2)),
+            dma((SIDE,)),
+            dma((SIDE,)),
             dma((owners,)),
             dma((owners,)),
             dma((owners,)),

time: 201 us -> 175 us (0.87)
  Pallas kernels: 193 us -> 167 us
    pallas_call x1, Pallas kernels: 99 us -> 71.2 us  [shards(): pl.pallas_call(gather_project, out_shape=(jax.ShapeDtypeStruct((rows * he...]
where the time goes in v3:
time: 175 us; the launch traced here: 174 us
  Pallas kernels  167 us (95%)
  local copies, waits for them, and re-layouts  5.17 us (3%)
    pallas_call x1, Pallas kernels, shards(): pl.pallas_call(project_out, out_shape=(jax.ShapeDtypeStruct((rows, q_cols...  85.2 us
    pallas_call x1, Pallas kernels, shards(): pl.pallas_call(gather_project, out_shape=(jax.ShapeDtypeStruct((rows * he...  71.2 us
    pallas_call x1, Pallas kernels, shards(): pl.pallas_call(write_back, grid=(stretches,), out_shape=jax.ShapeDtypeStr...  6.45 us
    pallas_call x1, Pallas kernels, shards(): pl.pallas_call(attend, out_shape=jax.ShapeDtypeStruct((rows, q_cols), BF1...  4.1 us

profile of v3, /device:TPU:34, one launch (start us, length us, event | category | flops | bytes accessed | tf_op | source)
XLA Modules:
  0.0 174.5 jit_solution(2569139354781668481)
XLA Ops:
  0.6 0.0 copy-start
  0.6 0.7 dynamic-slice_bitcast_fusion
  1.3 0.2 reshape.151.pos_ref
  1.5 0.7 compare_select_fusion
  2.2 0.1 copy.28
  2.3 0.1 reshape.142
  2.4 0.0 copy-start.6
  2.4 0.0 copy-start.7
  2.4 0.0 copy-start.8
  2.5 0.0 copy-start.1
  2.5 1.2 gather_fusion
  3.8 0.3 copy-done.1
  4.1 0.1 copy-done.3
  4.1 71.2 %gather_project.1 = (bf16[768,128]{1,0:T(8,128)(2,1)S(1)}, bf16[2,256,128]{2,1,0:T(8,128)(2,1)S(1)}, bf16[8,16,2,16,256]{4,3,2,1,0:T(8,128)(2,1)S(1)}) custom-call(s32[128]{0:T(128)S(1)} %gather_fusion, bf16[192,8192]{1,0:T(8,128)(2,1)} %hid_hbm.1, bf16[1,8192]{1,0:T(2,128)(2,1)S(1)} %reshape.132.gain_ref, bf16[512,512]{1,0:T(8,128)(2,1)S(1)} %copy-done.3, ...), custom_call_target="tpu_custom_call" | custom-call | tf_op jit(solution)/shard_map/gather_project/pallas_call | solution.py:610
  75.4 0.0 copy-start.5
  75.4 4.1 %attend.1.ctx_ref = bf16[192,512]{1,0:T(8,128)(2,1)S(1)} custom-call(bf16[768,128]{1,0:T(8,128)(2,1)S(1)} %get-tuple-element.7.q_ref, bf16[2,256,128]{2,1,0:T(8,128)(2,1)S(1)} %get-tuple-element.8.fresh_ref, bf16[8,512,256]{2,1,0:T(8,128)(2,1)S(1)} %bitcast.7, s32[8,32]{1,0:T(8,128)S(1)} %pad.7.row_ref, s32[768,1]{1,0:T(8,128)S(1)} %reshape.151.pos_ref), custom_call_target="tpu_custom_call" | custom-call | tf_op jit(solution)/shard_map/attend/pallas_call | solution.py:655
  79.5 0.1 reshape.141
  79.6 0.1 copy.29
  79.7 0.1 convert_reduce_fusion
  79.8 0.2 dynamic-slice_reduce_fusion
  80.0 0.1 select_reduce_fusion.slot_ref
  80.1 0.1 copy.33
  80.2 0.1 add.61
  80.3 0.2 fusion.pick_ref
  80.5 85.2 %project_out.1 = (bf16[192,512]{1,0:T(8,128)(2,1)S(1)}, bf16[2,8,32,128]{3,2,1,0:T(8,128)(2,1)S(1)}) custom-call(s32[32]{0:T(128)S(1)} %select_reduce_fusion.slot_ref, s32[8]{0:T(128)S(1)} %fusion.pick_ref, bf16[192,512]{1,0:T(8,128)(2,1)S(1)} %attend.1.ctx_ref, bf16[512,512]{1,0:T(8,128)(2,1)S(1)} %copy-done.2, bf16[2,8,32,128]{3,2,1,0:T(8,128)(2,1)S(1)} %bitcast.8), custom_call_target="tpu_custom_call" | custom-call | tf_op jit(solution)/shard_map/project_out/pallas_call | solution.py:674
  165.7 0.6 copy-done.4
  166.4 0.1 compare_convert_fusion
  166.4 0.1 copy.35
  166.5 0.2 multiply_reduce_fusion
  166.7 0.6 pad.8
  167.3 6.5 %write_back.1 = bf16[8,1,512,256]{3,2,1,0:T(8,128)(2,1)} custom-call(bf16[8,1,512,256]{3,2,1,0:T(8,128)(2,1)} %store_ref.1, bf16[2,8,32,128]{3,2,1,0:T(8,128)(2,1)} %copy-done.4, s32[8,1,32]{2,1,0:T(1,128)} %bitcast.11), custom_call_target="tpu_custom_call" | custom-call | tf_op jit(solution)/shard_map/write_back/pallas_call | solution.py:711
  173.8 0.7 copy.37
  (20 shorter events, 0.1 us)
Async XLA Ops:
  0.6 1.8 %copy-start = (s32[128]{0:T(128)S(1)}, s32[128]{0:T(128)}, u32[]{:S(2)}) copy-start(s32[128]{0:T(128)} %param.19) | copy-start | bytes 1540
  2.4 1.3 copy-start.6
  2.4 1.3 copy-start.7
  2.4 1.3 copy-start.8
  2.5 1.6 copy-start.1
  2.5 1.7 copy-start.3
  75.4 5.1 %copy-start.2 = (bf16[512,512]{1,0:T(8,128)(2,1)S(1)}, bf16[512,512]{1,0:T(8,128)(2,1)}, u32[]{:S(2)}) copy-start(bf16[512,512]{1,0:T(8,128)(2,1)} %w_ref.1) | copy-start | bytes 1572868
  75.4 91.0 %copy-start.5 = (s32[16,8,24]{2,1,0:T(8,128)S(1)}, s32[16,8,24]{2,1,0:T(8,128)}, u32[]{:S(2)}) copy-start(s32[16,8,24]{2,1,0:T(8,128)} %param.21) | copy-start | bytes 36868
  165.7 0.7 copy-start.4

commit v4 on v0

v4 whole, which is shorter than its diff:
```python
import functools
import math

import jax
import jax.numpy as jnp
from jax import lax
from jax.experimental import pallas as pl
from jax.experimental.pallas import tpu as pltpu
from jax.sharding import PartitionSpec as P

MESH = pl.DeviceIdType.MESH
SIDE = 4
BF16 = jnp.bfloat16
F32 = jnp.float32
RIGHT, OPPOSITE, LEFT = 1, 2, 3
PAD = 32


def remote(src, dst, send_sem, recv_sem, device):
    return pltpu.make_async_remote_copy(
        src_ref=src, dst_ref=dst, send_sem=send_sem, recv_sem=recv_sem, device_id=device, device_id_type=MESH
    )


def blend(old, keys, values, rows):
    hd = keys.shape[1]
    hit = lax.broadcasted_iota(jnp.int32, (old.shape[0], PAD), 0) == rows
    table = jnp.concatenate([keys, values, jnp.ones((PAD, hd), BF16)], axis=1)
    new = jnp.dot(hit.astype(F32).astype(BF16), table, preferred_element_type=F32)
    there = new[:, 2 * hd :] > 0.5
    parts = [
        jnp.where(there, new[:, i * hd : (i + 1) * hd], old[:, i * hd : (i + 1) * hd].astype(F32)).astype(BF16)
        for i in (0, 1)
    ]
    return parts[0], parts[1]


def attend(q_ref, fresh_ref, blocks_ref, row_ref, pos_ref, ctx_ref, ks, vs, sc, top, low, out, flat):
    stretches, length = ks.shape[0], ks.shape[1]
    hd = q_ref.shape[1]
    total = q_ref.shape[0]
    group = total // stretches
    heads = ctx_ref.shape[1] // hd
    per = group // heads
    scale = math.log2(math.e) / math.sqrt(hd)
    for r in range(stretches):
        old = blocks_ref[r].reshape(length, 2 * hd)
        ks[r], vs[r] = blend(old, fresh_ref[0, r], fresh_ref[1, r], row_ref[r : r + 1, :])
    top[...] = jnp.full_like(top, -jnp.inf)
    low[...] = jnp.zeros_like(low)
    out[...] = jnp.zeros_like(out)

    def fold(a, op):
        parts = [a[:, i * hd : (i + 1) * hd] for i in range(length // hd)]
        while len(parts) > 1:
            parts = [op(parts[i], parts[i + 1]) for i in range(0, len(parts), 2)]
        return parts[0]

    base = [sum(total - t * group for t in range(s)) for s in range(stretches)]
    for s in range(stretches):
        scores = lax.dot_general(
            q_ref[s * group :, :], ks[s], (((1,), (1,)), ((), ())), preferred_element_type=F32
        )
        key = lax.broadcasted_iota(jnp.int32, (group, length), 1)
        first = jnp.where(key <= pos_ref[s * group : (s + 1) * group, :], scores[:group], -jnp.inf)
        sc[base[s] : base[s] + group, :] = first
        top[s * group : (s + 1) * group, :] = jnp.maximum(
            top[s * group : (s + 1) * group, :], fold(first, jnp.maximum)
        )
        if s + 1 < stretches:
            sc[base[s] + group : base[s] + total - s * group, :] = scores[group:]
            top[(s + 1) * group :, :] = jnp.maximum(top[(s + 1) * group :, :], fold(scores[group:], jnp.maximum))
    top[...] = jnp.broadcast_to(jnp.max(top[...], axis=1, keepdims=True), top.shape)
    for s in range(stretches):
        here = slice(s * group, total)
        held = slice(base[s], base[s] + total - s * group)
        peak = top[here, :]
        expon = jnp.concatenate(
            [jnp.exp2((sc[held, i * hd : (i + 1) * hd] - peak) * scale) for i in range(length // hd)], axis=1
        )
        low[here, :] += fold(expon, jnp.add)
        out[here, :] += jnp.dot(expon.astype(BF16), vs[s], preferred_element_type=F32)
    out[...] = out[...] / jnp.sum(low[...], axis=1, keepdims=True)
    for r in range(stretches):
        for j in range(heads):
            at_row = (r * heads + j) * per
            flat[r * per : (r + 1) * per, j * hd : (j + 1) * hd] = out[at_row : at_row + per, :]
    ctx_ref[...] = flat[...].astype(BF16)


def prefill(
    place_ref, slot_ref, pick_ref, hid_hbm, gain_ref, qw_hbm, kvw_hbm, qb_ref, kvb_ref, ow_hbm, store_hbm,
    row_ref, pos_ref, slot_row_ref,
    out_ref, new_hbm,
    hid, acts, w, acc, part, sums, hop_in, hop_out, qs, fpad,
    queries, own_fresh, fresh, blocks, ks, vs, sc, top, low, res, flat, ctx,
    ow, ctxs, chunk, r_out, l_out, r_in, l_in, done, f_out, f_in, back, old, new,
    loc, w_send, w_recv, a_send, a_recv, c_send, c_recv, s_send, s_recv,
    h1_send, h1_recv, h2_send, h2_recv, x_send, x_recv,
    o_send, o_recv, oo_send, oo_recv, t_send, t_recv,
    r_send, r_recv, l_send, l_recv, f_send, f_recv, n_sem,
):
    me = lax.axis_index("cache")
    head = lax.axis_index("heads")
    core = lax.rem(head, 2)
    partner = (me, head + 1 - 2 * core)
    x, y = me // SIDE, lax.rem(me, SIDE)
    z = head // 2
    owners = SIDE * SIDE
    levels = lax.axis_size("heads") // 2
    right = (me, lax.rem(z + 1, levels) * 2 + core)
    left = (me, lax.rem(z + levels - 1, levels) * 2 + core)
    turn = lax.rem(head, SIDE)
    mirror = (x * SIDE + turn, head - turn + y)
    rows = hid.shape[0]
    depth, width = w.shape[1], w.shape[2]
    q_cols = qw_hbm.shape[1]
    hd = width - q_cols

    def ring(i, d):
        return lax.rem(i + d, SIDE)

    own_hid = pltpu.make_async_copy(hid_hbm, hid, loc.at[2])
    own_q = pltpu.make_async_copy(qw_hbm, w.at[x, :, 0:q_cols], loc.at[0])
    own_kv = pltpu.make_async_copy(
        kvw_hbm.at[:, pl.ds(pl.multiple_of(head * hd, hd), hd)], w.at[x, :, q_cols:width], loc.at[1]
    )
    own_hop = pltpu.make_async_copy(store_hbm.at[:, me, core], hop_in.at[pl.ds(me * 8, 8)], loc.at[3])
    own_hid.start()
    own_q.start()
    own_kv.start()
    own_hop.start()
    own_ow = pltpu.make_async_copy(ow_hbm, ow.at[core, x], loc.at[5 + SIDE])
    own_ow.start()
    old_in = pltpu.make_async_copy(store_hbm, old, loc.at[6 + SIDE])
    old_in.start()

    barrier = pltpu.get_barrier_semaphore()

    @pl.loop(1, owners)
    def _(o):
        pl.semaphore_signal(barrier, inc=1, device_id=(lax.rem(me + o, owners), head), device_id_type=MESH)

    for peer in (partner, left, right):
        pl.semaphore_signal(barrier, inc=1, device_id=peer, device_id_type=MESH)
    for d in (RIGHT, OPPOSITE, LEFT):
        across = (x * SIDE + ring(y, d), head + 1 - 2 * core)
        pl.semaphore_signal(barrier, inc=1, device_id=across, device_id_type=MESH)

    @pl.when(turn != y)
    def _():
        pl.semaphore_signal(barrier, inc=1, device_id=mirror, device_id_type=MESH)

    @pl.when(turn != y)
    def _():
        pl.semaphore_wait(barrier, owners + 6)

    @pl.when(turn == y)
    def _():
        pl.semaphore_wait(barrier, owners + 5)

    def slice_of(c):
        return hid.at[:, pl.ds(pl.multiple_of(c * depth, depth), depth)]

    def rows_to(d, i):
        to = ring(y, d)
        return remote(
            slice_of((2 * core + i) * SIDE + to), acts.at[2 * core + i, y], a_send.at[d, i], a_recv.at[d, i],
            (x * SIDE + to, head),
        )

    def hop1(o):
        to = lax.rem(me + o, owners)
        return remote(
            store_hbm.at[:, to, core], hop_in.at[pl.ds(me * 8, 8)], h1_send.at[o], h1_recv.at[me], (to, head)
        )

    def hop1_from(o):
        src = lax.rem(me + owners - o, owners)
        return remote(
            store_hbm.at[:, src, core], hop_in.at[pl.ds(src * 8, 8)], h1_send.at[o], h1_recv.at[src], (src, head)
        )

    def hop2(o):
        to = lax.rem(me + o, owners)
        return remote(hop_out.at[to], blocks.at[:, me, core], h2_send.at[o], h2_recv.at[me], (to, head))

    def hop2_from(o):
        src = lax.rem(me + owners - o, owners)
        return remote(hop_out.at[src], blocks.at[:, src, core], h2_send.at[o], h2_recv.at[src], (src, head))

    def weights_to(d):
        to = ring(x, d)
        return remote(w.at[x], w.at[x], w_send.at[d], w_recv.at[d], (to * SIDE + y, head))

    def weights_from(d):
        src = ring(x, SIDE - d)
        return remote(w.at[src], w.at[src], w_send.at[d], w_recv.at[d], (src * SIDE + y, head))

    steps = (RIGHT, LEFT, OPPOSITE)
    own_q.wait()
    own_kv.wait()
    for d in steps:
        weights_to(d).start()

    @pl.loop(1, owners)
    def _(o):
        hop1(o).start()

    own_hid.wait()
    tall = 16

    @pl.loop(0, rows // tall)
    def _(i):
        lines = pl.ds(pl.multiple_of(i * tall, tall), tall)
        total = jnp.zeros((tall, 1), F32)
        for c in range(owners):
            v = hid[lines, c * depth : (c + 1) * depth].astype(F32)
            total += jnp.sum(v * v, axis=-1, keepdims=True)
        factor = lax.rsqrt(total / (owners * depth) + 1e-06)
        for c in range(owners):
            v = hid[lines, c * depth : (c + 1) * depth].astype(F32)
            g = gain_ref[:, c * depth : (c + 1) * depth].astype(F32)
            hid[lines, c * depth : (c + 1) * depth] = (v * factor * g).astype(BF16)

    for i in (0, 1):
        for d in steps:
            rows_to(d, i).start()

    for i in range(SIDE):
        pltpu.make_async_copy(slice_of(i * SIDE + y), acts.at[i, y], loc.at[5 + i]).start()

    def rows_from(d, i, which):
        src = ring(y, SIDE - d)
        place = acts.at[2 * which + i, src]
        return remote(place, place, a_send.at[d, i], a_recv.at[d, i], (x * SIDE + src, head))

    def rows_over(d, i, which):
        place = acts.at[2 * which + i, ring(y, SIDE - d)]
        return remote(place, place, c_send.at[d, i], c_recv.at[d, i], partner)

    for i in (0, 1):
        for d in steps:
            rows_from(d, i, core).wait_recv()
            rows_over(d, i, core).start()

    own_hop.wait()

    @pl.loop(1, owners)
    def _(o):
        hop1_from(o).wait_recv()

    @pl.loop(0, owners)
    def _(i):
        for r in range(8):
            hop_out[i, r] = hop_in[place_ref[i * 8 + r]]

    @pl.loop(1, owners)
    def _(o):
        hop2(o).start()

    own_out = pltpu.make_async_copy(hop_out.at[me], blocks.at[:, me, core], loc.at[4])
    own_out.start()

    for i in range(SIDE):
        pltpu.make_async_copy(slice_of(i * SIDE + y), acts.at[i, y], loc.at[5 + i]).wait()
    for d in steps:
        weights_from(d).wait_recv()

    def product(i, j):
        return jnp.dot(acts[i, j], w[i], preferred_element_type=F32)

    @pl.loop(0, SIDE)
    def _(j):
        acc[j] = product(2 * core, j)
        acc[j] += product(2 * core + 1, j)

    for i in (0, 1):
        for d in steps:
            rows_over(d, i, 1 - core).wait_recv()

    def sums_to(d):
        to = ring(y, d)
        return remote(part.at[d], sums.at[d], s_send.at[d], s_recv.at[d], (x * SIDE + to, head))

    for d in (OPPOSITE, RIGHT, LEFT):
        j = ring(y, d)
        acc[j] += product(2 - 2 * core, j)
        part[d] = (acc[j] + product(3 - 2 * core, j)).astype(BF16)
        sums_to(d).start()

    def block_to(d):
        to = ring(x, d)
        return remote(ow_hbm, ow.at[core, x], o_send.at[d], o_recv.at[d], (to * SIDE + y, head))

    def block_from(d, which):
        place = ow.at[which, ring(x, SIDE - d)]
        return remote(place, place, oo_send.at[d], oo_recv.at[d], partner)

    for d in steps:
        block_to(d).start()
    own_ow.wait()
    block_from(0, core).start()
    acc[y] += product(2 - 2 * core, y)
    acc[y] += product(3 - 2 * core, y)

    def core_swap(which):
        return remote(
            blocks.at[:, :, which], blocks.at[:, :, which], x_send.at[0], x_recv.at[0], partner
        )

    own_out.wait()

    @pl.loop(1, owners)
    def _(o):
        hop2_from(o).wait_recv()

    core_swap(core).start()

    for d in steps:
        remote(part.at[d], sums.at[d], s_send.at[d], s_recv.at[d], (x * SIDE + ring(y, SIDE - d), head)).wait_recv()
        acc[y] += sums[d].astype(F32)

    per = rows // 8
    heads = q_cols // hd
    bias = qb_ref[...].astype(F32)
    kv_bias = kvb_ref[:, pl.ds(pl.multiple_of(head * hd, hd), hd)].astype(F32)
    for r in range(8):
        lines = slice(per * r, per * (r + 1))
        for j in range(heads):
            at_row = (r * heads + j) * per
            qs[at_row : at_row + per, :] = acc[y, lines, j * hd : (j + 1) * hd] + bias[:, j * hd : (j + 1) * hd]
        fpad[r * PAD : r * PAD + per, :] = acc[y, lines, q_cols:width] + kv_bias
        fpad[r * PAD + per : (r + 1) * PAD, :] = jnp.zeros((PAD - per, hd), F32)
    own_fresh[...] = fpad[...].astype(BF16).reshape(own_fresh.shape)
    fresh[core] = own_fresh[...]
    swap = remote(own_fresh, fresh.at[core], x_send.at[1], x_recv.at[1], partner)
    swap.start()
    queries[...] = qs[...].astype(BF16)

    @pl.loop(0, owners)
    def _(o):
        for m in range(2):
            f_out[2 * o + m] = own_fresh[slot_ref[2 * o + m]]

    def give(o):
        to = lax.rem(me + o, owners)
        return remote(
            f_out.at[pl.ds(2 * to, 2)], f_in.at[pl.ds(2 * me, 2)], f_send.at[o], f_recv.at[me], (to, head)
        )

    def take(o):
        src = lax.rem(me + owners - o, owners)
        return remote(
            f_out.at[pl.ds(2 * src, 2)], f_in.at[pl.ds(2 * src, 2)], f_send.at[o], f_recv.at[src], (src, head)
        )

    @pl.loop(1, owners)
    def _(o):
        give(o).start()

    for m in range(2):
        f_in[2 * me + m] = f_out[2 * me + m]

    core_swap(1 - core).wait_recv()
    remote(fresh.at[1 - core], fresh.at[1 - core], x_send.at[1], x_recv.at[1], partner).wait_recv()

    attend(queries, fresh, blocks, row_ref, pos_ref, ctx, ks, vs, sc, top, low, res, flat)

    def ctx_to(d):
        to = ring(y, d)
        return remote(
            ctx, ctxs.at[y // 2, core], t_send.at[d], t_recv.at[d, core], (x * SIDE + to, 2 * z + lax.rem(y, 2))
        )

    def ctx_from(d, which):
        src = ring(y, SIDE - d)
        place = ctxs.at[src // 2, which]
        return remote(place, place, t_send.at[d], t_recv.at[d, which], (x * SIDE + src, 2 * z + which))

    for d in (RIGHT, LEFT, OPPOSITE):
        ctx_to(d).start()

    mine = lax.rem(y, 2) == core

    @pl.when(mine)
    def _():
        ctxs[y // 2, core] = ctx[...]

    @pl.when(jnp.logical_not(mine))
    def _():
        ctx_to(0).start()

    for d in steps:
        place = ow.at[core, ring(x, SIDE - d)]
        remote(place, place, o_send.at[d], o_recv.at[d], (ring(x, SIDE - d) * SIDE + y, head)).wait_recv()
        block_from(d, core).start()

    @pl.loop(1, owners)
    def _(o):
        take(o).wait_recv()

    for s in range(8):
        back[core, s] = f_in[pick_ref[s]]
    swap_back = remote(back.at[core], back.at[core], x_send.at[2], x_recv.at[2], partner)
    swap_back.start()

    @pl.when(mine)
    def _():
        ctx_from(0, 1 - core).wait_recv()
        for which in (0, 1):
            ctx_from(OPPOSITE, which).wait_recv()

    @pl.when(jnp.logical_not(mine))
    def _():
        for d in (RIGHT, LEFT):
            for which in (0, 1):
                ctx_from(d, which).wait_recv()

    for d in (0,) + steps:
        block_from(d, 1 - core).wait_recv()

    hrow = rows // 2
    order = (4, 3, -3, 2, -2, 1, -1, 0)

    def compute(n):
        target = lax.rem(z + order[n] + levels, levels)
        column, request = target // 2, lax.rem(target, 2)
        chunk[n] = jnp.dot(ctxs[request, 0], ow[0, column], preferred_element_type=F32)
        chunk[n] += jnp.dot(ctxs[request, 1], ow[1, column], preferred_element_type=F32)

    def lines_of(half):
        return slice(half * hrow, (half + 1) * hrow)

    def ring_copy(step, half, out, into, send_sem, recv_sem, to):
        return remote(
            out.at[step, pl.ds(half * hrow, hrow)],
            into.at[step, pl.ds(half * hrow, hrow)],
            send_sem.at[step, half],
            recv_sem.at[step, half],
            to,
        )

    def rightward(step, half):
        return ring_copy(step, half, r_out, r_in, r_send, r_recv, right)

    def leftward(step, half):
        return ring_copy(step, half, l_out, l_in, l_send, l_recv, left)

    compute(0)
    r_out[0, lines_of(0), :] = chunk[0, lines_of(0), :].astype(BF16)
    rightward(0, 0).start()
    l_out[0, lines_of(1), :] = chunk[0, lines_of(1), :].astype(BF16)
    leftward(0, 1).start()
    compute(1)
    compute(2)
    for step in (1, 2, 3):
        n_right, n_left = 2 * step - 1, 2 * step
        halves = ((1, 0), (0, 1)) if step == 1 else ((0, 1), (1, 0))
        for right_half, left_half in halves:
            value = chunk[n_right, lines_of(right_half), :]
            if step > 1 or right_half == 0:
                rightward(step - 1, right_half).wait_recv()
                value += r_in[step - 1, lines_of(right_half), :].astype(F32)
            r_out[step, lines_of(right_half), :] = value.astype(BF16)
            rightward(step, right_half).start()
            value = chunk[n_left, lines_of(left_half), :]
            if step > 1 or left_half == 1:
                leftward(step - 1, left_half).wait_recv()
                value += l_in[step - 1, lines_of(left_half), :].astype(F32)
            l_out[step, lines_of(left_half), :] = value.astype(BF16)
            leftward(step, left_half).start()
        if step < 3:
            compute(2 * step + 1)
            compute(2 * step + 2)
        else:
            compute(7)

    remote(back.at[1 - core], back.at[1 - core], x_send.at[2], x_recv.at[2], partner).wait_recv()
    old_in.wait()
    for s in range(8):
        keys, values = blend(old[s].reshape(new.shape[1], 2 * hd), back[0, s], back[1, s], slot_row_ref[s : s + 1, :])
        new[s, :, 0:hd] = keys
        new[s, :, hd : 2 * hd] = values
    new_out = pltpu.make_async_copy(new, new_hbm, n_sem.at[0])
    new_out.start()

    def flip(half):
        return remote(
            done.at[pl.ds(half * hrow, hrow)], out_ref.at[pl.ds(half * hrow, hrow)],
            x_send.at[3 + half], x_recv.at[3 + half], mirror,
        )

    for half in (0, 1):
        rightward(3, half).wait_recv()
        leftward(3, half).wait_recv()
        value = chunk[7, lines_of(half), :] + r_in[3, lines_of(half), :].astype(F32)
        value += l_in[3, lines_of(half), :].astype(F32)
        done[lines_of(half), :] = value.astype(BF16)

        @pl.when(turn != y)
        def _():
            flip(half).start()

    @pl.when(turn == y)
    def _():
        out_ref[...] = done[...]

    for i in (0, 1):
        for d in steps:
            rows_to(d, i).wait_send()
            rows_over(d, i, core).wait_send()
    for d in steps:
        weights_to(d).wait_send()
        sums_to(d).wait_send()
        block_to(d).wait_send()
        ctx_to(d).wait_send()
    for d in (0,) + steps:
        block_from(d, core).wait_send()

    @pl.when(jnp.logical_not(mine))
    def _():
        ctx_to(0).wait_send()

    @pl.loop(1, owners)
    def _(o):
        hop1(o).wait_send()
        hop2(o).wait_send()
        give(o).wait_send()

    core_swap(core).wait_send()
    swap.wait_send()
    swap_back.wait_send()
    rightward(0, 0).wait_send()
    leftward(0, 1).wait_send()
    for step in (1, 2, 3):
        for half in (0, 1):
            rightward(step, half).wait_send()
            leftward(step, half).wait_send()
    new_out.wait()

    @pl.when(turn != y)
    def _():
        for half in (0, 1):
            flip(half).wait()


def shards(
    hidden, norm_gain, q_weight, q_bias, kv_weight, kv_bias, out_weight, kv_store, stretch_place, req_stretches, rec_rows
):
    owners = lax.axis_size("cache")
    me = lax.axis_index("cache")
    rows, width = hidden.shape
    stretches, _, length, kv_width = kv_store.shape
    hd = kv_width // 2
    per = rec_rows.shape[2]
    depth, q_cols = q_weight.shape
    levels = lax.axis_size("heads") // 2
    heads = q_cols // hd
    vmem = pl.BlockSpec(memory_space=pltpu.VMEM)
    smem = pl.BlockSpec(memory_space=pltpu.SMEM)
    hbm = pl.BlockSpec(memory_space=pl.ANY)
    dma = pltpu.SemaphoreType.DMA

    places = stretch_place[req_stretches]
    owner_of = places // stretches
    earlier = jnp.arange(stretches)[None, :] < jnp.arange(stretches)[:, None]
    rank_of = jnp.sum((owner_of[:, :, None] == owner_of[:, None, :]) & earlier[None], axis=2).astype(jnp.int32)
    pair_of = owner_of * 2 + rank_of
    my_pair = lax.dynamic_index_in_dim(pair_of, me, 0, keepdims=False)
    order = jnp.arange(stretches, dtype=jnp.int32)
    slot_r = jnp.sum((my_pair[None, :] == jnp.arange(2 * owners)[:, None]) * order[None, :], axis=1).astype(jnp.int32)
    flat_places = places.reshape(-1)
    mine = flat_places[None, :] == (me * stretches + order)[:, None]
    source = jnp.arange(owners)[:, None] * 2 + rank_of
    pick = jnp.sum(mine * source.reshape(1, -1), axis=1).astype(jnp.int32)
    slot_rows = jnp.sum(mine[:, :, None] * rec_rows.reshape(1, -1, per), axis=1).astype(jnp.int32)
    slot_rows = jnp.pad(slot_rows, ((0, 0), (0, PAD - per)), constant_values=-1)
    my_rows = lax.dynamic_index_in_dim(rec_rows, me, 0, keepdims=False)
    pad_rows = jnp.pad(my_rows, ((0, 0), (0, PAD - per)), constant_values=-1)
    row_pos = jnp.broadcast_to(my_rows[:, None, :], (stretches, heads, per)).reshape(rows * heads, 1)

    store = kv_store.reshape(stretches, owners, 2, length // (2 * owners), kv_width)
    piece = length // (2 * owners)

    attn_out, new_store = pl.pallas_call(
        prefill,
        out_shape=(
            jax.ShapeDtypeStruct((rows, q_cols), BF16),
            jax.ShapeDtypeStruct((stretches, length, kv_width), BF16),
        ),
        in_specs=[smem, smem, smem, hbm, vmem, hbm, hbm, vmem, vmem, hbm, hbm, vmem, vmem, vmem],
        out_specs=(vmem, hbm),
        scratch_shapes=[
            pltpu.VMEM((rows, width), BF16),
            pltpu.VMEM((SIDE, SIDE, rows, depth), BF16),
            pltpu.VMEM((SIDE, depth, q_cols + hd), BF16),
            pltpu.VMEM((SIDE, rows, q_cols + hd), F32),
            pltpu.VMEM((SIDE, rows, q_cols + hd), BF16),
            pltpu.VMEM((SIDE, rows, q_cols + hd), BF16),
            pltpu.VMEM((owners * stretches, piece, kv_width), BF16),
            pltpu.VMEM((owners, stretches, piece, kv_width), BF16),
            pltpu.VMEM((rows * heads, hd), F32),
            pltpu.VMEM((stretches * PAD, hd), F32),
            pltpu.VMEM((rows * heads, hd), BF16),
            pltpu.VMEM((stretches, PAD, hd), BF16),
            pltpu.VMEM((2, stretches, PAD, hd), BF16),
            pltpu.VMEM((stretches, owners, 2, piece, kv_width), BF16),
            pltpu.VMEM((stretches, length, hd), BF16),
            pltpu.VMEM((stretches, length, hd), BF16),
            pltpu.VMEM((rows * heads * (stretches + 1) // 2, length), F32),
            pltpu.VMEM((rows * heads, hd), F32),
            pltpu.VMEM((rows * heads, hd), F32),
            pltpu.VMEM((rows * heads, hd), F32),
            pltpu.VMEM((rows, q_cols), F32),
            pltpu.VMEM((rows, q_cols), BF16),
            pltpu.VMEM((2, SIDE, depth, q_cols), BF16),
            pltpu.VMEM((2, 2, rows, q_cols), BF16),
            pltpu.VMEM((levels, rows, q_cols), F32),
            pltpu.VMEM((4, rows, q_cols), BF16),
            pltpu.VMEM((4, rows, q_cols), BF16),
            pltpu.VMEM((4, rows, q_cols), BF16),
            pltpu.VMEM((4, rows, q_cols), BF16),
            pltpu.VMEM((rows, q_cols), BF16),
            pltpu.VMEM((2 * owners, PAD, hd), BF16),
            pltpu.VMEM((2 * owners, PAD, hd), BF16),
            pltpu.VMEM((2, stretches, PAD, hd), BF16),
            pltpu.VMEM((stretches, owners, 2, piece, kv_width), BF16),
            pltpu.VMEM((stretches, length, kv_width), BF16),
            dma((7 + SIDE,)),
            dma((SIDE,)),
            dma((SIDE,)),
            dma((SIDE, 2)),
            dma((SIDE, 2)),
            dma((SIDE, 2)),
            dma((SIDE, 2)),
            dma((SIDE,)),
            dma((SIDE,)),
            dma((owners,)),
            dma((owners,)),
            dma((owners,)),
            dma((owners,)),
            dma((5,)),
            dma((5,)),
            dma((SIDE,)),
            dma((SIDE,)),
            dma((SIDE,)),
            dma((SIDE,)),
            dma((SIDE,)),
            dma((SIDE, 2)),
            dma((4, 2)),
            dma((4, 2)),
            dma((4, 2)),
            dma((4, 2)),
            dma((owners,)),
            dma((owners,)),
            dma((1,)),
        ],
        compiler_params=pltpu.CompilerParams(collective_id=0, has_side_effects=True, vmem_limit_bytes=58 << 20),
        name="prefill",
    )(
        flat_places, slot_r, pick, hidden, norm_gain.reshape(1, -1), q_weight, kv_weight,
        q_bias.reshape(1, -1), kv_bias.reshape(1, -1), out_weight, store, pad_rows, row_pos, slot_rows,
    )
    return (attn_out, new_store.reshape(kv_store.shape))


def solution(mesh):
    placed = (
        P("cache", None),
        P(),
        P("cache", "heads"),
        P("heads"),
        P("cache", None),
        P(),
        P("heads", "cache"),
        P("cache", "heads", None, None),
        P(),
        P(),
        P(),
    )
    return jax.shard_map(
        shards,
        mesh=mesh,
        in_specs=placed,
        out_specs=(P("cache", "heads"), P("cache", "heads", None, None)),
        check_vma=False,
    )
```

time: 515 us -> 140 us (0.27)
  waiting for transfers between devices: 268 us -> 0 us
  local copies, waits for them, and re-layouts: 137 us -> 11.9 us
  Pallas kernels: 0 us -> 122 us
  other arithmetic: 37.2 us -> 2.52 us
  matrix products: 30.3 us -> 0 us
  starting transfers between devices: 22.8 us -> 0 us
  between operations: 14 us -> 0.76 us
    all_to_all x3 -> x0, waiting for transfers between devices: 163 us -> none  [the longest x1 115 us: shards(): lax.all_to_all(outgoing, 'cache', split_axis=0, concat_axis=0, tiled=True)]
    pallas_call x0 -> x1, Pallas kernels: none -> 122 us  [shards(): pl.pallas_call(prefill, out_shape=(jax.ShapeDtypeStruct((rows, q_cols), B...]
    scatter x3 -> x0, local copies, waits for them, and re-layouts: 105 us -> none  [the longest x1 81.7 us: shards(): store_local.at[target_slot[:, :, None], send_rows].set(inbound, mode='drop')]
    reduce_scatter x2 -> x0, waiting for transfers between devices: 74.3 us -> none  [the longest x1 74.2 us: shards(): lax.psum_scatter(jnp.concatenate([jnp.dot(slices, q_weight, preferred_ele...]
    dot_general x5 -> x0, matrix products: 30.3 us -> none  [the longest x1 7.54 us: shards(): jnp.einsum('qjd,kd->jqk', query_heads, keyvals[:, :head_dim], preferred_e...]
    all_gather x1 -> x0, waiting for transfers between devices: 30.2 us -> none  [shards(): lax.all_gather(out_weight, 'cache', axis=1, tiled=True)]
    all_to_all x3 -> x0, starting transfers between devices: 22.5 us -> none  [the longest x1 9.34 us: shards(): lax.all_to_all(outgoing, 'cache', split_axis=0, concat_axis=0, tiled=True)]
    sub x1 -> x0, other arithmetic: 17.3 us -> none  [shards(): expon = jnp.exp(scores - highest)]
  transfers between devices with their start and end apart: 6 -> 0, of which waited for: 5 -> 0; matrix products, arithmetic and copies ran while one was open for 32% -> 0% of each run, Pallas kernels for 0% -> 0%
where the time goes in v4:
time: 140 us; the launch traced here: 137 us
  Pallas kernels  122 us (87%)
  local copies, waits for them, and re-layouts  11.9 us (8%)
  other arithmetic  2.52 us (2%)
    pallas_call x1, Pallas kernels, shards(): pl.pallas_call(prefill, out_shape=(jax.ShapeDtypeStruct((rows, q_cols), B...  122 us
    unnamed x12, local copies, waits for them, and re-layouts  4.69 us

profile of v4, /device:TPU:34, one launch (start us, length us, event | category | flops | bytes accessed | tf_op | source)
XLA Modules:
  0.0 137.1 jit_solution(6734840398434752667)
XLA Ops:
  0.6 0.0 copy-start
  0.7 1.3 reshape.130.qb_ref
  2.0 0.7 dynamic-slice_bitcast_fusion
  2.6 0.6 pad.7.row_ref
  3.2 0.7 compare_select_fusion
  3.9 0.1 copy.31
  4.0 0.1 reshape.137
  4.1 0.0 copy-done
  4.1 0.0 copy-start.4
  4.1 0.0 copy-start.2
  4.1 0.0 copy-start.3
  4.2 1.2 gather_fusion
  5.4 0.0 copy-start.1
  5.4 0.1 compare_convert_fusion
  5.5 0.1 reshape.136
  5.5 0.1 copy.32
  5.6 0.1 convert_reduce_fusion
  5.8 0.2 dynamic-slice_reduce_fusion
  5.9 0.6 select_reduce_fusion.slot_ref
  6.6 0.1 copy.36
  6.6 0.1 add.61
  6.7 0.8 fusion.pick_ref
  7.5 0.0 copy-done.4
  7.5 0.6 reshape.131.kvb_ref
  8.1 0.1 copy.37
  8.1 0.2 multiply_reduce_fusion
  8.4 0.6 pad.8.slot_row_ref
  9.0 0.6 reshape.129.gain_ref
  9.6 0.9 reshape.146.pos_ref
  10.5 121.9 %prefill.1 = (bf16[192,512]{1,0:T(8,128)(2,1)}, bf16[8,512,256]{2,1,0:T(8,128)(2,1)}) custom-call(s32[128]{0:T(128)} %copy-done.1, s32[32]{0:T(128)} %select_reduce_fusion.slot_ref, s32[8]{0:T(128)} %fusion.pick_ref, bf16[192,8192]{1,0:T(8,128)(2,1)} %hid_hbm.1, bf16[1,8192]{1,0:T(2,128)(2,1)} %reshape.129.gain_ref, bf16[512,512]{1,0:T(8,128)(2,1)} %qw_hbm.1, ...), custom_call_target="tpu_custom_call" | custom-call | tf_op jit(solution)/shard_map/prefill/pallas_call | solution.py:586
  132.4 1.6 %copy.42 = bf16[192,512]{1,0:T(8,128)(2,1)} copy(bf16[192,512]{1,0:T(8,128)(2,1)} %get-tuple-element.18) | data formatting | bytes 393216
  134.0 3.0 %copy.43 = bf16[8,1,512,256]{3,2,1,0:T(8,128)(2,1)} copy(bf16[8,1,512,256]{3,2,1,0:T(8,128)(2,1)} %bitcast.7) | data formatting | bytes 4194304
  (10 shorter events, 0.1 us)
Async XLA Ops:
  0.6 3.5 %copy-start = (s32[128]{0:T(128)S(1)}, s32[128]{0:T(128)}, u32[]{:S(2)}) copy-start(s32[128]{0:T(128)} %param.19) | copy-start | bytes 1540
  4.1 3.4 %copy-start.4 = (bf16[2048]{0:T(1024)(128)(2,1)S(1)}, bf16[2048]{0:T(1024)(128)(2,1)}, u32[]{:S(2)}) copy-start(bf16[2048]{0:T(1024)(128)(2,1)} %param.16) | copy-start | bytes 12292
  4.1 4.0 %copy-start.2 = (s32[16,8,24]{2,1,0:T(8,128)S(1)}, s32[16,8,24]{2,1,0:T(8,128)}, u32[]{:S(2)}) copy-start(s32[16,8,24]{2,1,0:T(8,128)} %param.21) | copy-start | bytes 36868
  4.1 4.8 %copy-start.3 = (bf16[8192]{0:T(1024)(128)(2,1)S(1)}, bf16[8192]{0:T(1024)(128)(2,1)}, u32[]{:S(2)}) copy-start(bf16[8192]{0:T(1024)(128)(2,1)} %param.12) | copy-start | bytes 49156
  5.4 5.2 %copy-start.1 = (s32[128]{0:T(128)}, s32[128]{0:T(128)S(1)}, u32[]{:S(2)}) copy-start(s32[128]{0:T(128)S(1)} %gather_fusion) | copy-start | bytes 1540

commit v5 on v4

--- a/solution.py
+++ b/solution.py
@@ -35,7 +35,7 @@
     return parts[0], parts[1]
 
 
-def attend(q_ref, fresh_ref, blocks_ref, row_ref, pos_ref, ctx_ref, ks, vs, sc, top, low, out, flat):
+def attend(q_ref, fresh_ref, blocks_ref, row_ref, ctx_ref, ks, vs, sc, top, low, out, flat):
     stretches, length = ks.shape[0], ks.shape[1]
     hd = q_ref.shape[1]
     total = q_ref.shape[0]
@@ -45,7 +45,7 @@
     scale = math.log2(math.e) / math.sqrt(hd)
     for r in range(stretches):
         old = blocks_ref[r].reshape(length, 2 * hd)
-        ks[r], vs[r] = blend(old, fresh_ref[0, r], fresh_ref[1, r], row_ref[r : r + 1, :])
+        ks[r], vs[r] = blend(old, fresh_ref[0, r], fresh_ref[1, r], row_ref[r : r + 1, 0:PAD])
     top[...] = jnp.full_like(top, -jnp.inf)
     low[...] = jnp.zeros_like(low)
     out[...] = jnp.zeros_like(out)
@@ -56,13 +56,15 @@
             parts = [op(parts[i], parts[i + 1]) for i in range(0, len(parts), 2)]
         return parts[0]
 
+    columns = jnp.transpose(row_ref[...].astype(F32))
     base = [sum(total - t * group for t in range(s)) for s in range(stretches)]
     for s in range(stretches):
         scores = lax.dot_general(
             q_ref[s * group :, :], ks[s], (((1,), (1,)), ((), ())), preferred_element_type=F32
         )
-        key = lax.broadcasted_iota(jnp.int32, (group, length), 1)
-        first = jnp.where(key <= pos_ref[s * group : (s + 1) * group, :], scores[:group], -jnp.inf)
+        key = lax.broadcasted_iota(jnp.int32, (group, length), 1).astype(F32)
+        last = jnp.concatenate([columns[0:per, s : s + 1]] * heads, axis=0)
+        first = jnp.where(key <= last, scores[:group], -jnp.inf)
         sc[base[s] : base[s] + group, :] = first
         top[s * group : (s + 1) * group, :] = jnp.maximum(
             top[s * group : (s + 1) * group, :], fold(first, jnp.maximum)
@@ -89,10 +91,9 @@
 
 
 def prefill(
-    place_ref, slot_ref, pick_ref, hid_hbm, gain_ref, qw_hbm, kvw_hbm, qb_ref, kvb_ref, ow_hbm, store_hbm,
-    row_ref, pos_ref, slot_row_ref,
+    table_ref, req_ref, hid_hbm, gain_ref, qw_hbm, kvw_hbm, qb_ref, kvb_ref, ow_hbm, store_hbm, rec_ref,
     out_ref, new_hbm,
-    hid, acts, w, acc, part, sums, hop_in, hop_out, qs, fpad,
+    hid, acts, w, acc, part, sums, hop_in, hop_out, qs, fpad, my_rows, slot_rows,
     queries, own_fresh, fresh, blocks, ks, vs, sc, top, low, res, flat, ctx,
     ow, ctxs, chunk, r_out, l_out, r_in, l_in, done, f_out, f_in, back, old, new,
     loc, w_send, w_recv, a_send, a_recv, c_send, c_recv, s_send, s_recv,
@@ -116,6 +117,7 @@
     depth, width = w.shape[1], w.shape[2]
     q_cols = qw_hbm.shape[1]
     hd = width - q_cols
+    per = rows // 8
 
     def ring(i, d):
         return lax.rem(i + d, SIDE)
@@ -189,19 +191,64 @@
         src = lax.rem(me + owners - o, owners)
         return remote(hop_out.at[src], blocks.at[:, src, core], h2_send.at[o], h2_recv.at[src], (src, head))
 
-    def weights_to(d):
-        to = ring(x, d)
-        return remote(w.at[x], w.at[x], w_send.at[d], w_recv.at[d], (to * SIDE + y, head))
-
-    def weights_from(d):
-        src = ring(x, SIDE - d)
-        return remote(w.at[src], w.at[src], w_send.at[d], w_recv.at[d], (src * SIDE + y, head))
+    class Ring4:
+        def __init__(self, source, place, send_sem, recv_sem):
+            self.source, self.place, self.send_sem, self.recv_sem = source, place, send_sem, recv_sem
+            self.deep = place(0).shape[0] // 2
+
+        def part(self, ref, half):
+            return ref.at[pl.ds(half * self.deep, self.deep)]
+
+        def copy(self, d, half, passed=False):
+            to = (ring(x, d) * SIDE + y, head)
+            src = self.part(self.place(ring(x, SIDE - d)) if passed else self.source, half)
+            dst = self.part(self.place(ring(x, SIDE - d) if passed else x), half)
+            k = OPPOSITE if passed else d
+            return remote(src, dst, self.send_sem.at[k, half], self.recv_sem.at[k, half], to)
+
+        def wait(self, d, half):
+            place = self.part(self.place(ring(x, SIDE - d)), half)
+            remote(
+                place, place, self.send_sem.at[d, half], self.recv_sem.at[d, half],
+                (ring(x, SIDE - d) * SIDE + y, head),
+            ).wait_recv()
+
+        def start(self):
+            self.copy(RIGHT, 0).start()
+            self.copy(LEFT, 1).start()
+
+        def rest(self):
+            self.copy(RIGHT, 1).start()
+            self.copy(LEFT, 0).start()
+
+        def forward(self):
+            self.wait(RIGHT, 0)
+            self.copy(RIGHT, 0, True).start()
+            self.wait(LEFT, 1)
+            self.copy(LEFT, 1, True).start()
+
+        def wait_rest(self):
+            self.wait(RIGHT, 1)
+            self.wait(LEFT, 0)
+
+        def wait_opposite(self):
+            self.wait(OPPOSITE, 0)
+            self.wait(OPPOSITE, 1)
+
+        def finish(self):
+            for half in (0, 1):
+                self.copy(RIGHT, half).wait_send()
+                self.copy(LEFT, half).wait_send()
+            self.copy(RIGHT, 0, True).wait_send()
+            self.copy(LEFT, 1, True).wait_send()
+
+    weights = Ring4(w.at[x], lambda i: w.at[i], w_send, w_recv)
+    ow_blocks = Ring4(ow_hbm, lambda i: ow.at[core, i], o_send, o_recv)
 
     steps = (RIGHT, LEFT, OPPOSITE)
     own_q.wait()
     own_kv.wait()
-    for d in steps:
-        weights_to(d).start()
+    weights.start()
 
     @pl.loop(1, owners)
     def _(o):
@@ -220,15 +267,39 @@
         factor = lax.rsqrt(total / (owners * depth) + 1e-06)
         for c in range(owners):
             v = hid[lines, c * depth : (c + 1) * depth].astype(F32)
-            g = gain_ref[:, c * depth : (c + 1) * depth].astype(F32)
+            g = gain_ref[c * depth : (c + 1) * depth].astype(F32).reshape(1, depth)
             hid[lines, c * depth : (c + 1) * depth] = (v * factor * g).astype(BF16)
 
     for i in (0, 1):
         for d in steps:
             rows_to(d, i).start()
+    weights.rest()
 
     for i in range(SIDE):
         pltpu.make_async_copy(slice_of(i * SIDE + y), acts.at[i, y], loc.at[5 + i]).start()
+
+    def place_of(i, r):
+        return table_ref[req_ref[i, r]]
+
+    my_owner = [place_of(me, r) // 8 for r in range(8)]
+    my_rank = [sum([(my_owner[q] == my_owner[r]).astype(jnp.int32) for q in range(r)], 0) for r in range(8)]
+
+    def find(n, found):
+        here = place_of(n // 8, lax.rem(n, 8)) - me * 8
+        return tuple(jnp.where(here == s, n, found[s]) for s in range(8))
+
+    found = lax.fori_loop(0, owners * 8, find, (jnp.int32(0),) * 8)
+    my_rows[...] = jnp.full_like(my_rows, -1)
+    slot_rows[...] = jnp.full_like(slot_rows, -1)
+    my_rows[:, 0:per] = rec_ref[me]
+    picks = []
+    for s in range(8):
+        i, r = found[s] // 8, lax.rem(found[s], 8)
+        slot_rows[s : s + 1, 0:per] = rec_ref[i, pl.ds(r, 1), :]
+        rank = sum([((q < r) & (place_of(i, q) // 8 == me)).astype(jnp.int32) for q in range(8)], 0)
+        picks.append(2 * i + jnp.minimum(rank, 1))
+
+    weights.forward()
 
     def rows_from(d, i, which):
         src = ring(y, SIDE - d)
@@ -253,7 +324,7 @@
     @pl.loop(0, owners)
     def _(i):
         for r in range(8):
-            hop_out[i, r] = hop_in[place_ref[i * 8 + r]]
+            hop_out[i, r] = hop_in[place_of(i, r)]
 
     @pl.loop(1, owners)
     def _(o):
@@ -264,8 +335,8 @@
 
     for i in range(SIDE):
         pltpu.make_async_copy(slice_of(i * SIDE + y), acts.at[i, y], loc.at[5 + i]).wait()
-    for d in steps:
-        weights_from(d).wait_recv()
+    weights.wait_rest()
+    weights.wait_opposite()
 
     def product(i, j):
         return jnp.dot(acts[i, j], w[i], preferred_element_type=F32)
@@ -289,16 +360,12 @@
         part[d] = (acc[j] + product(3 - 2 * core, j)).astype(BF16)
         sums_to(d).start()
 
-    def block_to(d):
-        to = ring(x, d)
-        return remote(ow_hbm, ow.at[core, x], o_send.at[d], o_recv.at[d], (to * SIDE + y, head))
-
     def block_from(d, which):
         place = ow.at[which, ring(x, SIDE - d)]
         return remote(place, place, oo_send.at[d], oo_recv.at[d], partner)
 
-    for d in steps:
-        block_to(d).start()
+    ow_blocks.start()
+    ow_blocks.rest()
     own_ow.wait()
     block_from(0, core).start()
     acc[y] += product(2 - 2 * core, y)
@@ -321,10 +388,10 @@
         remote(part.at[d], sums.at[d], s_send.at[d], s_recv.at[d], (x * SIDE + ring(y, SIDE - d), head)).wait_recv()
         acc[y] += sums[d].astype(F32)
 
-    per = rows // 8
     heads = q_cols // hd
-    bias = qb_ref[...].astype(F32)
-    kv_bias = kvb_ref[:, pl.ds(pl.multiple_of(head * hd, hd), hd)].astype(F32)
+    bias = qb_ref[...].astype(F32).reshape(1, q_cols)
+    both = kvb_ref[pl.ds(pl.multiple_of(z * 2 * hd, 2 * hd), 2 * hd)].astype(F32).reshape(1, 2 * hd)
+    kv_bias = jnp.where(core == 0, both[:, 0:hd], both[:, hd:])
     for r in range(8):
         lines = slice(per * r, per * (r + 1))
         for j in range(heads):
@@ -341,7 +408,8 @@
     @pl.loop(0, owners)
     def _(o):
         for m in range(2):
-            f_out[2 * o + m] = own_fresh[slot_ref[2 * o + m]]
+            row = sum([jnp.where((my_owner[r] == o) & (my_rank[r] == m), r, 0) for r in range(8)], 0)
+            f_out[2 * o + m] = own_fresh[row]
 
     def give(o):
         to = lax.rem(me + o, owners)
@@ -365,7 +433,7 @@
     core_swap(1 - core).wait_recv()
     remote(fresh.at[1 - core], fresh.at[1 - core], x_send.at[1], x_recv.at[1], partner).wait_recv()
 
-    attend(queries, fresh, blocks, row_ref, pos_ref, ctx, ks, vs, sc, top, low, res, flat)
+    attend(queries, fresh, blocks, my_rows, ctx, ks, vs, sc, top, low, res, flat)
 
     def ctx_to(d):
         to = ring(y, d)
@@ -391,17 +459,17 @@
     def _():
         ctx_to(0).start()
 
-    for d in steps:
-        place = ow.at[core, ring(x, SIDE - d)]
-        remote(place, place, o_send.at[d], o_recv.at[d], (ring(x, SIDE - d) * SIDE + y, head)).wait_recv()
-        block_from(d, core).start()
+    ow_blocks.forward()
+    ow_blocks.wait_rest()
+    block_from(RIGHT, core).start()
+    block_from(LEFT, core).start()
 
     @pl.loop(1, owners)
     def _(o):
         take(o).wait_recv()
 
     for s in range(8):
-        back[core, s] = f_in[pick_ref[s]]
+        back[core, s] = f_in[picks[s]]
     swap_back = remote(back.at[core], back.at[core], x_send.at[2], x_recv.at[2], partner)
     swap_back.start()
 
@@ -417,6 +485,8 @@
             for which in (0, 1):
                 ctx_from(d, which).wait_recv()
 
+    ow_blocks.wait_opposite()
+    block_from(OPPOSITE, core).start()
     for d in (0,) + steps:
         block_from(d, 1 - core).wait_recv()
 
@@ -446,6 +516,12 @@
 
     def leftward(step, half):
         return ring_copy(step, half, l_out, l_in, l_send, l_recv, left)
+
+    def renew(s):
+        keys, values = blend(old[s].reshape(new.shape[1], 2 * hd), back[0, s], back[1, s], slot_rows[s : s + 1, 0:PAD])
+        new[s, :, 0:hd] = keys
+        new[s, :, hd : 2 * hd] = values
+        pltpu.make_async_copy(new.at[s], new_hbm.at[s], n_sem.at[s]).start()
 
     compute(0)
     r_out[0, lines_of(0), :] = chunk[0, lines_of(0), :].astype(BF16)
@@ -470,20 +546,16 @@
                 value += l_in[step - 1, lines_of(left_half), :].astype(F32)
             l_out[step, lines_of(left_half), :] = value.astype(BF16)
             leftward(step, left_half).start()
+        if step == 1:
+            old_in.wait()
+            remote(back.at[1 - core], back.at[1 - core], x_send.at[2], x_recv.at[2], partner).wait_recv()
         if step < 3:
             compute(2 * step + 1)
             compute(2 * step + 2)
+            for s in range(4 * step - 4, 4 * step):
+                renew(s)
         else:
             compute(7)
-
-    remote(back.at[1 - core], back.at[1 - core], x_send.at[2], x_recv.at[2], partner).wait_recv()
-    old_in.wait()
-    for s in range(8):
-        keys, values = blend(old[s].reshape(new.shape[1], 2 * hd), back[0, s], back[1, s], slot_row_ref[s : s + 1, :])
-        new[s, :, 0:hd] = keys
-        new[s, :, hd : 2 * hd] = values
-    new_out = pltpu.make_async_copy(new, new_hbm, n_sem.at[0])
-    new_out.start()
 
     def flip(half):
         return remote(
@@ -511,10 +583,10 @@
             rows_to(d, i).wait_send()
             rows_over(d, i, core).wait_send()
     for d in steps:
-        weights_to(d).wait_send()
         sums_to(d).wait_send()
-        block_to(d).wait_send()
         ctx_to(d).wait_send()
+    weights.finish()
+    ow_blocks.finish()
     for d in (0,) + steps:
         block_from(d, core).wait_send()
 
@@ -537,12 +609,23 @@
         for half in (0, 1):
             rightward(step, half).wait_send()
             leftward(step, half).wait_send()
-    new_out.wait()
+    for s in range(8):
+        pltpu.make_async_copy(new.at[s], new_hbm.at[s], n_sem.at[s]).wait()
 
     @pl.when(turn != y)
     def _():
         for half in (0, 1):
             flip(half).wait()
+
+
+def hand_over(out_ref, store_ref, out_copy, store_copy, sem):
+    copies = [pltpu.make_async_copy(out_ref, out_copy, sem.at[0])]
+    for s in range(store_ref.shape[0]):
+        copies.append(pltpu.make_async_copy(store_ref.at[s], store_copy.at[s, 0], sem.at[s + 1]))
+    for copy in copies:
+        copy.start()
+    for copy in copies:
+        copy.wait()
 
 
 def shards(
@@ -562,24 +645,6 @@
     hbm = pl.BlockSpec(memory_space=pl.ANY)
     dma = pltpu.SemaphoreType.DMA
 
-    places = stretch_place[req_stretches]
-    owner_of = places // stretches
-    earlier = jnp.arange(stretches)[None, :] < jnp.arange(stretches)[:, None]
-    rank_of = jnp.sum((owner_of[:, :, None] == owner_of[:, None, :]) & earlier[None], axis=2).astype(jnp.int32)
-    pair_of = owner_of * 2 + rank_of
-    my_pair = lax.dynamic_index_in_dim(pair_of, me, 0, keepdims=False)
-    order = jnp.arange(stretches, dtype=jnp.int32)
-    slot_r = jnp.sum((my_pair[None, :] == jnp.arange(2 * owners)[:, None]) * order[None, :], axis=1).astype(jnp.int32)
-    flat_places = places.reshape(-1)
-    mine = flat_places[None, :] == (me * stretches + order)[:, None]
-    source = jnp.arange(owners)[:, None] * 2 + rank_of
-    pick = jnp.sum(mine * source.reshape(1, -1), axis=1).astype(jnp.int32)
-    slot_rows = jnp.sum(mine[:, :, None] * rec_rows.reshape(1, -1, per), axis=1).astype(jnp.int32)
-    slot_rows = jnp.pad(slot_rows, ((0, 0), (0, PAD - per)), constant_values=-1)
-    my_rows = lax.dynamic_index_in_dim(rec_rows, me, 0, keepdims=False)
-    pad_rows = jnp.pad(my_rows, ((0, 0), (0, PAD - per)), constant_values=-1)
-    row_pos = jnp.broadcast_to(my_rows[:, None, :], (stretches, heads, per)).reshape(rows * heads, 1)
-
     store = kv_store.reshape(stretches, owners, 2, length // (2 * owners), kv_width)
     piece = length // (2 * owners)
 
@@ -589,7 +654,7 @@
             jax.ShapeDtypeStruct((rows, q_cols), BF16),
             jax.ShapeDtypeStruct((stretches, length, kv_width), BF16),
         ),
-        in_specs=[smem, smem, smem, hbm, vmem, hbm, hbm, vmem, vmem, hbm, hbm, vmem, vmem, vmem],
+        in_specs=[smem, smem, hbm, vmem, hbm, hbm, vmem, vmem, hbm, hbm, vmem],
         out_specs=(vmem, hbm),
         scratch_shapes=[
             pltpu.VMEM((rows, width), BF16),
@@ -602,6 +667,8 @@
             pltpu.VMEM((owners, stretches, piece, kv_width), BF16),
             pltpu.VMEM((rows * heads, hd), F32),
             pltpu.VMEM((stretches * PAD, hd), F32),
+            pltpu.VMEM((stretches, hd), jnp.int32),
+            pltpu.VMEM((stretches, hd), jnp.int32),
             pltpu.VMEM((rows * heads, hd), BF16),
             pltpu.VMEM((stretches, PAD, hd), BF16),
             pltpu.VMEM((2, stretches, PAD, hd), BF16),
@@ -628,8 +695,8 @@
             pltpu.VMEM((stretches, owners, 2, piece, kv_width), BF16),
             pltpu.VMEM((stretches, length, kv_width), BF16),
             dma((7 + SIDE,)),
-            dma((SIDE,)),
-            dma((SIDE,)),
+            dma((SIDE, 2)),
+            dma((SIDE, 2)),
             dma((SIDE, 2)),
             dma((SIDE, 2)),
             dma((SIDE, 2)),
@@ -642,8 +709,8 @@
             dma((owners,)),
             dma((5,)),
             dma((5,)),
-            dma((SIDE,)),
-            dma((SIDE,)),
+            dma((SIDE, 2)),
+            dma((SIDE, 2)),
             dma((SIDE,)),
             dma((SIDE,)),
             dma((SIDE,)),
@@ -654,15 +721,24 @@
             dma((4, 2)),
             dma((owners,)),
             dma((owners,)),
-            dma((1,)),
+            dma((8,)),
         ],
         compiler_params=pltpu.CompilerParams(collective_id=0, has_side_effects=True, vmem_limit_bytes=58 << 20),
         name="prefill",
     )(
-        flat_places, slot_r, pick, hidden, norm_gain.reshape(1, -1), q_weight, kv_weight,
-        q_bias.reshape(1, -1), kv_bias.reshape(1, -1), out_weight, store, pad_rows, row_pos, slot_rows,
+        stretch_place, req_stretches, hidden, norm_gain, q_weight, kv_weight, q_bias, kv_bias, out_weight, store, rec_rows
     )
-    return (attn_out, new_store.reshape(kv_store.shape))
+    return pl.pallas_call(
+        hand_over,
+        out_shape=(
+            jax.ShapeDtypeStruct((rows, q_cols), BF16),
+            jax.ShapeDtypeStruct((stretches, 1, length, kv_width), BF16),
+        ),
+        in_specs=[hbm, hbm],
+        out_specs=(hbm, hbm),
+        scratch_shapes=[dma((stretches + 1,))],
+        name="hand_over",
+    )(attn_out, new_store)
 
 
 def solution(mesh):

time: 140 us -> 188 us (1.34)
  Pallas kernels: 122 us -> 184 us
  local copies, waits for them, and re-layouts: 11.9 us -> 1.36 us
  other arithmetic: 2.52 us -> 0 us
    pallas_call x0 -> x1, Pallas kernels: none -> 70.7 us  [shards(): pl.pallas_call(hand_over, out_shape=(jax.ShapeDtypeStruct((rows, q_cols),...]
    pallas_call x1, Pallas kernels: 122 us -> 113 us  [shards(): pl.pallas_call(prefill, out_shape=(jax.ShapeDtypeStruct((rows, q_cols), B...]
    reshape x4 -> x0, local copies, waits for them, and re-layouts: 3.42 us -> none  [the longest x1 1.27 us: shards(): q_bias.reshape(1, -1)]
    unnamed x12 -> x1, local copies, waits for them, and re-layouts: 4.69 us -> 1.36 us
where the time goes in v5:
time: 188 us; the launch traced here: 186 us
  Pallas kernels  184 us (98%)
    pallas_call x1, Pallas kernels, shards(): pl.pallas_call(prefill, out_shape=(jax.ShapeDtypeStruct((rows, q_cols), B...  113 us
    pallas_call x1, Pallas kernels, shards(): pl.pallas_call(hand_over, out_shape=(jax.ShapeDtypeStruct((rows, q_cols),...  70.7 us

profile of v5, /device:TPU:34, one launch (start us, length us, event | category | flops | bytes accessed | tf_op | source)
XLA Modules:
  0.0 186.1 jit_solution(15847260586561698770)
XLA Ops:
  0.6 1.4 copy.13.req_ref
  2.0 113.4 %prefill.1 = (bf16[192,512]{1,0:T(8,128)(2,1)}, bf16[8,512,256]{2,1,0:T(8,128)(2,1)}) custom-call(s32[128]{0:T(128)} %table_ref.1, s32[16,8]{1,0:T(8,128)} %copy.13.req_ref, bf16[192,8192]{1,0:T(8,128)(2,1)} %hid_hbm.1, bf16[8192]{0:T(1024)(128)(2,1)} %gain_ref.1, bf16[512,512]{1,0:T(8,128)(2,1)} %qw_hbm.1, bf16[512,2048]{1,0:T(8,128)(2,1)} %kvw_hbm.1, ...), custom_call_target="tpu_custom_call" | custom-call | tf_op jit(solution)/shard_map/prefill/pallas_call | solution.py:651
  115.4 70.7 %hand_over.1 = (bf16[192,512]{1,0:T(8,128)(2,1)}, bf16[8,1,512,256]{3,2,1,0:T(8,128)(2,1)}) custom-call(bf16[192,512]{1,0:T(8,128)(2,1)} %get-tuple-element.4.out_ref, bf16[8,512,256]{2,1,0:T(8,128)(2,1)} %get-tuple-element.5.store_ref), custom_call_target="tpu_custom_call" | custom-call | tf_op jit(solution)/shard_map/hand_over/pallas_call | solution.py:731

commit v6 on v5

--- a/solution.py
+++ b/solution.py
@@ -618,13 +618,18 @@
             flip(half).wait()
 
 
-def hand_over(out_ref, store_ref, out_copy, store_copy, sem):
-    copies = [pltpu.make_async_copy(out_ref, out_copy, sem.at[0])]
-    for s in range(store_ref.shape[0]):
-        copies.append(pltpu.make_async_copy(store_ref.at[s], store_copy.at[s, 0], sem.at[s + 1]))
-    for copy in copies:
+def hand_over(out_ref, store_ref, out_copy, store_copy, out_held, held, sem_in, sem_out):
+    count = store_ref.shape[0]
+    ins = [pltpu.make_async_copy(store_ref.at[s], held.at[s], sem_in.at[s]) for s in range(count)]
+    ins.append(pltpu.make_async_copy(out_ref, out_held, sem_in.at[count]))
+    outs = [pltpu.make_async_copy(held.at[s], store_copy.at[s, 0], sem_out.at[s]) for s in range(count)]
+    outs.append(pltpu.make_async_copy(out_held, out_copy, sem_out.at[count]))
+    for copy in ins:
         copy.start()
-    for copy in copies:
+    for copy_in, copy_out in zip(ins, outs):
+        copy_in.wait()
+        copy_out.start()
+    for copy in outs:
         copy.wait()
 
 
@@ -736,7 +741,12 @@
         ),
         in_specs=[hbm, hbm],
         out_specs=(hbm, hbm),
-        scratch_shapes=[dma((stretches + 1,))],
+        scratch_shapes=[
+            pltpu.VMEM((rows, q_cols), BF16),
+            pltpu.VMEM((stretches, length, kv_width), BF16),
+            dma((stretches + 1,)),
+            dma((stretches + 1,)),
+        ],
         name="hand_over",
     )(attn_out, new_store)
 

time: 188 us -> 119 us (0.63)
  Pallas kernels: 184 us -> 116 us
    pallas_call x1, Pallas kernels: 70.7 us -> 2.47 us  [shards(): pl.pallas_call(hand_over, out_shape=(jax.ShapeDtypeStruct((rows, q_cols),...]
where the time goes in v6:
time: 119 us; the launch traced here: 118 us
  Pallas kernels  116 us (97%)
  local copies, waits for them, and re-layouts  1.36 us (1%)
    pallas_call x1, Pallas kernels, shards(): pl.pallas_call(prefill, out_shape=(jax.ShapeDtypeStruct((rows, q_cols), B...  113 us
    pallas_call x1, Pallas kernels, shards(): pl.pallas_call(hand_over, out_shape=(jax.ShapeDtypeStruct((rows, q_cols),...  2.47 us

profile of v6, /device:TPU:34, one launch (start us, length us, event | category | flops | bytes accessed | tf_op | source)
XLA Modules:
  0.0 117.9 jit_solution(4250414262133668082)
XLA Ops:
  0.6 1.4 %copy.13.req_ref = s32[16,8]{1,0:T(8,128)} copy(s32[16,8]{0,1:T(8,128)} %param.20) | data formatting | bytes 1024 | tf_op args[9]
  2.0 113.4 %prefill.1 = (bf16[192,512]{1,0:T(8,128)(2,1)}, bf16[8,512,256]{2,1,0:T(8,128)(2,1)}) custom-call(s32[128]{0:T(128)} %table_ref.1, s32[16,8]{1,0:T(8,128)} %copy.13.req_ref, bf16[192,8192]{1,0:T(8,128)(2,1)} %hid_hbm.1, bf16[8192]{0:T(1024)(128)(2,1)} %gain_ref.1, bf16[512,512]{1,0:T(8,128)(2,1)} %qw_hbm.1, bf16[512,2048]{1,0:T(8,128)(2,1)} %kvw_hbm.1, ...), custom_call_target="tpu_custom_call" | custom-call | tf_op jit(solution)/shard_map/prefill/pallas_call | solution.py:656
  115.4 2.5 %hand_over.1 = (bf16[192,512]{1,0:T(8,128)(2,1)}, bf16[8,1,512,256]{3,2,1,0:T(8,128)(2,1)}) custom-call(bf16[192,512]{1,0:T(8,128)(2,1)} %get-tuple-element.4.out_ref, bf16[8,512,256]{2,1,0:T(8,128)(2,1)} %get-tuple-element.5.store_ref), custom_call_target="tpu_custom_call" | custom-call | tf_op jit(solution)/shard_map/hand_over/pallas_call | solution.py:736

commit v7 on v6

--- a/solution.py
+++ b/solution.py
@@ -96,7 +96,7 @@
     hid, acts, w, acc, part, sums, hop_in, hop_out, qs, fpad, my_rows, slot_rows,
     queries, own_fresh, fresh, blocks, ks, vs, sc, top, low, res, flat, ctx,
     ow, ctxs, chunk, r_out, l_out, r_in, l_in, done, f_out, f_in, back, old, new,
-    loc, w_send, w_recv, a_send, a_recv, c_send, c_recv, s_send, s_recv,
+    loc, w_send, w_recv, a_send, a_recv, zr_send, zr_recv, zl_send, zl_recv, c_send, c_recv, s_send, s_recv,
     h1_send, h1_recv, h2_send, h2_recv, x_send, x_recv,
     o_send, o_recv, oo_send, oo_recv, t_send, t_recv,
     r_send, r_recv, l_send, l_recv, f_send, f_recv, n_sem,
@@ -164,12 +164,51 @@
     def slice_of(c):
         return hid.at[:, pl.ds(pl.multiple_of(c * depth, depth), depth)]
 
-    def rows_to(d, i):
+    few = rows // 4
+
+    def eighth(level, d):
+        lines = pl.ds(pl.multiple_of(level // 2 * few, few), few)
+        return acts.at[2 * core + lax.rem(level, 2), ring(y, SIDE - d), lines]
+
+    def rows_to(d):
         to = ring(y, d)
+        lines = pl.ds(pl.multiple_of(z // 2 * few, few), few)
+        column = ((2 * core + lax.rem(z, 2)) * SIDE + to) * depth
         return remote(
-            slice_of((2 * core + i) * SIDE + to), acts.at[2 * core + i, y], a_send.at[d, i], a_recv.at[d, i],
-            (x * SIDE + to, head),
-        )
+            hid.at[lines, pl.ds(pl.multiple_of(column, depth), depth)], acts.at[2 * core + lax.rem(z, 2), y, lines],
+            a_send.at[d], a_recv.at[d], (x * SIDE + to, head),
+        )
+
+    def rows_from(d):
+        place = eighth(z, d)
+        return remote(place, place, a_send.at[d], a_recv.at[d], (x * SIDE + ring(y, SIDE - d), head))
+
+    def upward(step, d, arriving=False):
+        place = eighth(lax.rem(z + levels + 1 - step - (1 if arriving else 0), levels), d)
+        return remote(place, place, zr_send.at[step, d], zr_recv.at[step, d], right)
+
+    def downward(step, d, arriving=False):
+        place = eighth(lax.rem(z - 1 + step + (1 if arriving else 0), levels), d)
+        return remote(place, place, zl_send.at[step, d], zl_recv.at[step, d], left)
+
+    def goes_up(step, d):
+        return step < 4 or d != LEFT
+
+    def goes_down(step, d):
+        return step < 4 or d == LEFT
+
+    def level_step(step):
+        for d in steps:
+            if step == 1:
+                rows_from(d).wait_recv()
+            else:
+                upward(step - 1, d, True).wait_recv()
+            if goes_up(step, d):
+                upward(step, d).start()
+            if step > 1:
+                downward(step - 1, d, True).wait_recv()
+            if goes_down(step, d):
+                downward(step, d).start()
 
     def hop1(o):
         to = lax.rem(me + o, owners)
@@ -270,9 +309,8 @@
             g = gain_ref[c * depth : (c + 1) * depth].astype(F32).reshape(1, depth)
             hid[lines, c * depth : (c + 1) * depth] = (v * factor * g).astype(BF16)
 
-    for i in (0, 1):
-        for d in steps:
-            rows_to(d, i).start()
+    for d in steps:
+        rows_to(d).start()
     weights.rest()
 
     for i in range(SIDE):
@@ -299,21 +337,10 @@
         rank = sum([((q < r) & (place_of(i, q) // 8 == me)).astype(jnp.int32) for q in range(8)], 0)
         picks.append(2 * i + jnp.minimum(rank, 1))
 
+    level_step(1)
     weights.forward()
 
-    def rows_from(d, i, which):
-        src = ring(y, SIDE - d)
-        place = acts.at[2 * which + i, src]
-        return remote(place, place, a_send.at[d, i], a_recv.at[d, i], (x * SIDE + src, head))
-
-    def rows_over(d, i, which):
-        place = acts.at[2 * which + i, ring(y, SIDE - d)]
-        return remote(place, place, c_send.at[d, i], c_recv.at[d, i], partner)
-
-    for i in (0, 1):
-        for d in steps:
-            rows_from(d, i, core).wait_recv()
-            rows_over(d, i, core).start()
+    level_step(2)
 
     own_hop.wait()
 
@@ -332,6 +359,22 @@
 
     own_out = pltpu.make_async_copy(hop_out.at[me], blocks.at[:, me, core], loc.at[4])
     own_out.start()
+
+    level_step(3)
+    level_step(4)
+    for d in steps:
+        if goes_up(4, d):
+            upward(4, d, True).wait_recv()
+        if goes_down(4, d):
+            downward(4, d, True).wait_recv()
+
+    def rows_over(d, i, which):
+        place = acts.at[2 * which + i, ring(y, SIDE - d)]
+        return remote(place, place, c_send.at[d, i], c_recv.at[d, i], partner)
+
+    for i in (0, 1):
+        for d in steps:
+            rows_over(d, i, core).start()
 
     for i in range(SIDE):
         pltpu.make_async_copy(slice_of(i * SIDE + y), acts.at[i, y], loc.at[5 + i]).wait()
@@ -580,8 +623,14 @@
 
     for i in (0, 1):
         for d in steps:
-            rows_to(d, i).wait_send()
             rows_over(d, i, core).wait_send()
+    for d in steps:
+        rows_to(d).wait_send()
+        for step in (1, 2, 3, 4):
+            if goes_up(step, d):
+                upward(step, d).wait_send()
+            if goes_down(step, d):
+                downward(step, d).wait_send()
     for d in steps:
         sums_to(d).wait_send()
         ctx_to(d).wait_send()
@@ -702,8 +751,12 @@
             dma((7 + SIDE,)),
             dma((SIDE, 2)),
             dma((SIDE, 2)),
-            dma((SIDE, 2)),
-            dma((SIDE, 2)),
+            dma((SIDE,)),
+            dma((SIDE,)),
+            dma((SIDE + 1, SIDE)),
+            dma((SIDE + 1, SIDE)),
+            dma((SIDE + 1, SIDE)),
+            dma((SIDE + 1, SIDE)),
             dma((SIDE, 2)),
             dma((SIDE, 2)),
             dma((SIDE,)),

time: 119 us -> 120 us (level)
  no operation moved by 1% of the time
where the time goes in v7:
time: 120 us; the launch traced here: 118 us
  Pallas kernels  116 us (97%)
  local copies, waits for them, and re-layouts  1.36 us (1%)
    pallas_call x1, Pallas kernels, shards(): pl.pallas_call(prefill, out_shape=(jax.ShapeDtypeStruct((rows, q_cols), B...  114 us
    pallas_call x1, Pallas kernels, shards(): pl.pallas_call(hand_over, out_shape=(jax.ShapeDtypeStruct((rows, q_cols),...  2.47 us

profile of v7, /device:TPU:34, one launch (start us, length us, event | category | flops | bytes accessed | tf_op | source)
XLA Modules:
  0.0 118.1 jit_solution(17046815207715572470)
XLA Ops:
  0.6 1.4 %copy.13.req_ref = s32[16,8]{1,0:T(8,128)} copy(s32[16,8]{0,1:T(8,128)} %param.20) | data formatting | bytes 1024 | tf_op args[9]
  2.0 113.7 %prefill.1 = (bf16[192,512]{1,0:T(8,128)(2,1)}, bf16[8,512,256]{2,1,0:T(8,128)(2,1)}) custom-call(s32[128]{0:T(128)} %table_ref.1, s32[16,8]{1,0:T(8,128)} %copy.13.req_ref, bf16[192,8192]{1,0:T(8,128)(2,1)} %hid_hbm.1, bf16[8192]{0:T(1024)(128)(2,1)} %gain_ref.1, bf16[512,512]{1,0:T(8,128)(2,1)} %qw_hbm.1, bf16[512,2048]{1,0:T(8,128)(2,1)} %kvw_hbm.1, ...), custom_call_target="tpu_custom_call" | custom-call | tf_op jit(solution)/shard_map/prefill/pallas_call | solution.py:705
  115.6 2.5 %hand_over.1 = (bf16[192,512]{1,0:T(8,128)(2,1)}, bf16[8,1,512,256]{3,2,1,0:T(8,128)(2,1)}) custom-call(bf16[192,512]{1,0:T(8,128)(2,1)} %get-tuple-element.4.out_ref, bf16[8,512,256]{2,1,0:T(8,128)(2,1)} %get-tuple-element.5.store_ref), custom_call_target="tpu_custom_call" | custom-call | tf_op jit(solution)/shard_map/hand_over/pallas_call | solution.py:789

commit v8 on v7

--- a/solution.py
+++ b/solution.py
@@ -97,7 +97,7 @@
     queries, own_fresh, fresh, blocks, ks, vs, sc, top, low, res, flat, ctx,
     ow, ctxs, chunk, r_out, l_out, r_in, l_in, done, f_out, f_in, back, old, new,
     loc, w_send, w_recv, a_send, a_recv, zr_send, zr_recv, zl_send, zl_recv, c_send, c_recv, s_send, s_recv,
-    h1_send, h1_recv, h2_send, h2_recv, x_send, x_recv,
+    h1_send, h1_recv, h2_send, h2_recv, k_send, k_recv, x_send, x_recv,
     o_send, o_recv, oo_send, oo_recv, t_send, t_recv,
     r_send, r_recv, l_send, l_recv, f_send, f_recv, n_sem,
 ):
@@ -111,8 +111,9 @@
     levels = lax.axis_size("heads") // 2
     right = (me, lax.rem(z + 1, levels) * 2 + core)
     left = (me, lax.rem(z + levels - 1, levels) * 2 + core)
-    turn = lax.rem(head, SIDE)
-    mirror = (x * SIDE + turn, head - turn + y)
+    goal = (lax.rem(head, SIDE) * SIDE + y, x * SIDE + head // SIDE)
+    origin = (head // SIDE * SIDE + y, lax.rem(head, SIDE) * SIDE + x)
+    stays = (goal[0] == me) & (goal[1] == head)
     rows = hid.shape[0]
     depth, width = w.shape[1], w.shape[2]
     q_cols = qw_hbm.shape[1]
@@ -132,7 +133,7 @@
     own_q.start()
     own_kv.start()
     own_hop.start()
-    own_ow = pltpu.make_async_copy(ow_hbm, ow.at[core, x], loc.at[5 + SIDE])
+    own_ow = pltpu.make_async_copy(ow_hbm, ow.at[core, y], loc.at[5 + SIDE])
     own_ow.start()
     old_in = pltpu.make_async_copy(store_hbm, old, loc.at[6 + SIDE])
     old_in.start()
@@ -146,18 +147,15 @@
     for peer in (partner, left, right):
         pl.semaphore_signal(barrier, inc=1, device_id=peer, device_id_type=MESH)
     for d in (RIGHT, OPPOSITE, LEFT):
-        across = (x * SIDE + ring(y, d), head + 1 - 2 * core)
+        across = (ring(x, d) * SIDE + y, head + 1 - 2 * core)
         pl.semaphore_signal(barrier, inc=1, device_id=across, device_id_type=MESH)
 
-    @pl.when(turn != y)
+    @pl.when(jnp.logical_not(stays))
     def _():
-        pl.semaphore_signal(barrier, inc=1, device_id=mirror, device_id_type=MESH)
-
-    @pl.when(turn != y)
-    def _():
+        pl.semaphore_signal(barrier, inc=1, device_id=origin, device_id_type=MESH)
         pl.semaphore_wait(barrier, owners + 6)
 
-    @pl.when(turn == y)
+    @pl.when(stays)
     def _():
         pl.semaphore_wait(barrier, owners + 5)
 
@@ -231,25 +229,28 @@
         return remote(hop_out.at[src], blocks.at[:, src, core], h2_send.at[o], h2_recv.at[src], (src, head))
 
     class Ring4:
-        def __init__(self, source, place, send_sem, recv_sem):
+        def __init__(self, source, place, send_sem, recv_sem, axis):
             self.source, self.place, self.send_sem, self.recv_sem = source, place, send_sem, recv_sem
+            self.axis, self.here = axis, (x, y)[axis]
             self.deep = place(0).shape[0] // 2
+
+        def device(self, d):
+            return ((ring(x, d) * SIDE + y, x * SIDE + ring(y, d))[self.axis], head)
 
         def part(self, ref, half):
             return ref.at[pl.ds(half * self.deep, self.deep)]
 
         def copy(self, d, half, passed=False):
-            to = (ring(x, d) * SIDE + y, head)
-            src = self.part(self.place(ring(x, SIDE - d)) if passed else self.source, half)
-            dst = self.part(self.place(ring(x, SIDE - d) if passed else x), half)
+            before = ring(self.here, SIDE - d)
+            src = self.part(self.place(before) if passed else self.source, half)
+            dst = self.part(self.place(before if passed else self.here), half)
             k = OPPOSITE if passed else d
-            return remote(src, dst, self.send_sem.at[k, half], self.recv_sem.at[k, half], to)
+            return remote(src, dst, self.send_sem.at[k, half], self.recv_sem.at[k, half], self.device(d))
 
         def wait(self, d, half):
-            place = self.part(self.place(ring(x, SIDE - d)), half)
+            place = self.part(self.place(ring(self.here, SIDE - d)), half)
             remote(
-                place, place, self.send_sem.at[d, half], self.recv_sem.at[d, half],
-                (ring(x, SIDE - d) * SIDE + y, head),
+                place, place, self.send_sem.at[d, half], self.recv_sem.at[d, half], self.device(SIDE - d)
             ).wait_recv()
 
         def start(self):
@@ -281,13 +282,14 @@
             self.copy(RIGHT, 0, True).wait_send()
             self.copy(LEFT, 1, True).wait_send()
 
-    weights = Ring4(w.at[x], lambda i: w.at[i], w_send, w_recv)
-    ow_blocks = Ring4(ow_hbm, lambda i: ow.at[core, i], o_send, o_recv)
+    weights = Ring4(w.at[x], lambda i: w.at[i], w_send, w_recv, 0)
+    ow_blocks = Ring4(ow_hbm, lambda i: ow.at[core, i], o_send, o_recv, 1)
 
     steps = (RIGHT, LEFT, OPPOSITE)
     own_q.wait()
     own_kv.wait()
     weights.start()
+    ow_blocks.start()
 
     @pl.loop(1, owners)
     def _(o):
@@ -312,6 +314,7 @@
     for d in steps:
         rows_to(d).start()
     weights.rest()
+    ow_blocks.rest()
 
     for i in range(SIDE):
         pltpu.make_async_copy(slice_of(i * SIDE + y), acts.at[i, y], loc.at[5 + i]).start()
@@ -341,6 +344,7 @@
     weights.forward()
 
     level_step(2)
+    ow_blocks.forward()
 
     own_hop.wait()
 
@@ -404,28 +408,22 @@
         sums_to(d).start()
 
     def block_from(d, which):
-        place = ow.at[which, ring(x, SIDE - d)]
+        place = ow.at[which, ring(y, SIDE - d)]
         return remote(place, place, oo_send.at[d], oo_recv.at[d], partner)
 
-    ow_blocks.start()
-    ow_blocks.rest()
     own_ow.wait()
     block_from(0, core).start()
     acc[y] += product(2 - 2 * core, y)
     acc[y] += product(3 - 2 * core, y)
 
-    def core_swap(which):
-        return remote(
-            blocks.at[:, :, which], blocks.at[:, :, which], x_send.at[0], x_recv.at[0], partner
-        )
-
-    own_out.wait()
-
-    @pl.loop(1, owners)
-    def _(o):
-        hop2_from(o).wait_recv()
-
-    core_swap(core).start()
+    ow_blocks.wait_rest()
+    ow_blocks.wait_opposite()
+    for d in steps:
+        block_from(d, core).start()
+
+    def core_piece(c, which):
+        place = blocks.at[:, c, which]
+        return remote(place, place, k_send.at[c], k_recv.at[c], partner)
 
     for d in steps:
         remote(part.at[d], sums.at[d], s_send.at[d], s_recv.at[d], (x * SIDE + ring(y, SIDE - d), head)).wait_recv()
@@ -473,39 +471,45 @@
     for m in range(2):
         f_in[2 * me + m] = f_out[2 * me + m]
 
-    core_swap(1 - core).wait_recv()
+    own_out.wait()
+    core_piece(me, core).start()
+
+    @pl.loop(1, owners)
+    def _(o):
+        hop2_from(o).wait_recv()
+        core_piece(lax.rem(me + owners - o, owners), core).start()
+
+    @pl.loop(0, owners)
+    def _(c):
+        core_piece(c, 1 - core).wait_recv()
+
     remote(fresh.at[1 - core], fresh.at[1 - core], x_send.at[1], x_recv.at[1], partner).wait_recv()
 
     attend(queries, fresh, blocks, my_rows, ctx, ks, vs, sc, top, low, res, flat)
 
     def ctx_to(d):
-        to = ring(y, d)
         return remote(
-            ctx, ctxs.at[y // 2, core], t_send.at[d], t_recv.at[d, core], (x * SIDE + to, 2 * z + lax.rem(y, 2))
+            ctx, ctxs.at[x // 2, core], t_send.at[d], t_recv.at[d, core],
+            (ring(x, d) * SIDE + y, 2 * z + lax.rem(x, 2)),
         )
 
     def ctx_from(d, which):
-        src = ring(y, SIDE - d)
+        src = ring(x, SIDE - d)
         place = ctxs.at[src // 2, which]
-        return remote(place, place, t_send.at[d], t_recv.at[d, which], (x * SIDE + src, 2 * z + which))
+        return remote(place, place, t_send.at[d], t_recv.at[d, which], (src * SIDE + y, 2 * z + which))
 
     for d in (RIGHT, LEFT, OPPOSITE):
         ctx_to(d).start()
 
-    mine = lax.rem(y, 2) == core
+    mine = lax.rem(x, 2) == core
 
     @pl.when(mine)
     def _():
-        ctxs[y // 2, core] = ctx[...]
+        ctxs[x // 2, core] = ctx[...]
 
     @pl.when(jnp.logical_not(mine))
     def _():
         ctx_to(0).start()
-
-    ow_blocks.forward()
-    ow_blocks.wait_rest()
-    block_from(RIGHT, core).start()
-    block_from(LEFT, core).start()
 
     @pl.loop(1, owners)
     def _(o):
@@ -528,8 +532,6 @@
             for which in (0, 1):
                 ctx_from(d, which).wait_recv()
 
-    ow_blocks.wait_opposite()
-    block_from(OPPOSITE, core).start()
     for d in (0,) + steps:
         block_from(d, 1 - core).wait_recv()
 
@@ -603,7 +605,7 @@
     def flip(half):
         return remote(
             done.at[pl.ds(half * hrow, hrow)], out_ref.at[pl.ds(half * hrow, hrow)],
-            x_send.at[3 + half], x_recv.at[3 + half], mirror,
+            x_send.at[3 + half], x_recv.at[3 + half], goal,
         )
 
     for half in (0, 1):
@@ -613,11 +615,11 @@
         value += l_in[3, lines_of(half), :].astype(F32)
         done[lines_of(half), :] = value.astype(BF16)
 
-        @pl.when(turn != y)
+        @pl.when(jnp.logical_not(stays))
         def _():
             flip(half).start()
 
-    @pl.when(turn == y)
+    @pl.when(stays)
     def _():
         out_ref[...] = done[...]
 
@@ -649,7 +651,10 @@
         hop2(o).wait_send()
         give(o).wait_send()
 
-    core_swap(core).wait_send()
+    @pl.loop(0, owners)
+    def _(c):
+        core_piece(c, core).wait_send()
+
     swap.wait_send()
     swap_back.wait_send()
     rightward(0, 0).wait_send()
@@ -661,7 +666,7 @@
     for s in range(8):
         pltpu.make_async_copy(new.at[s], new_hbm.at[s], n_sem.at[s]).wait()
 
-    @pl.when(turn != y)
+    @pl.when(jnp.logical_not(stays))
     def _():
         for half in (0, 1):
             flip(half).wait()
@@ -765,6 +770,8 @@
             dma((owners,)),
             dma((owners,)),
             dma((owners,)),
+            dma((owners,)),
+            dma((owners,)),
             dma((5,)),
             dma((5,)),
             dma((SIDE, 2)),

time: 120 us -> 135 us (1.12)
  the two profiles are of different devices: /device:TPU:34 before, /device:TPU:4 now
where the time goes in v8:
time: 135 us
  Pallas kernels  133 us (99%)
  local copies, waits for them, and re-layouts  1.36 us (1%)
    pallas_call x1, Pallas kernels, shards(): pl.pallas_call(prefill, out_shape=(jax.ShapeDtypeStruct((rows, q_cols), B...  130 us

profile of v8, /device:TPU:4, one launch (start us, length us, event | category | flops | bytes accessed | tf_op | source)
XLA Modules:
  0.0 134.5 jit_solution(17892599550913727837)
XLA Ops:
  0.6 1.4 %copy.13.req_ref = s32[16,8]{1,0:T(8,128)} copy(s32[16,8]{0,1:T(8,128)} %param.20) | data formatting | bytes 1024 | tf_op args[9]
  2.0 130.0 %prefill.1 = (bf16[192,512]{1,0:T(8,128)(2,1)}, bf16[8,512,256]{2,1,0:T(8,128)(2,1)}) custom-call(s32[128]{0:T(128)} %table_ref.1, s32[16,8]{1,0:T(8,128)} %copy.13.req_ref, bf16[192,8192]{1,0:T(8,128)(2,1)} %hid_hbm.1, bf16[8192]{0:T(1024)(128)(2,1)} %gain_ref.1, bf16[512,512]{1,0:T(8,128)(2,1)} %qw_hbm.1, bf16[512,2048]{1,0:T(8,128)(2,1)} %kvw_hbm.1, ...), custom_call_target="tpu_custom_call" | custom-call | tf_op jit(solution)/shard_map/prefill/pallas_call | solution.py:710
  132.0 2.5 %hand_over.1 = (bf16[192,512]{1,0:T(8,128)(2,1)}, bf16[8,1,512,256]{3,2,1,0:T(8,128)(2,1)}) custom-call(bf16[192,512]{1,0:T(8,128)(2,1)} %get-tuple-element.4.out_ref, bf16[8,512,256]{2,1,0:T(8,128)(2,1)} %get-tuple-element.5.store_ref), custom_call_target="tpu_custom_call" | custom-call | tf_op jit(solution)/shard_map/hand_over/pallas_call | solution.py:796

commit v9 on v7

--- a/solution.py
+++ b/solution.py
@@ -35,7 +35,7 @@
     return parts[0], parts[1]
 
 
-def attend(q_ref, fresh_ref, blocks_ref, row_ref, ctx_ref, ks, vs, sc, top, low, out, flat):
+def attend(q_ref, row_ref, ctx_ref, ks, vs, sc, top, low, out, flat):
     stretches, length = ks.shape[0], ks.shape[1]
     hd = q_ref.shape[1]
     total = q_ref.shape[0]
@@ -43,9 +43,6 @@
     heads = ctx_ref.shape[1] // hd
     per = group // heads
     scale = math.log2(math.e) / math.sqrt(hd)
-    for r in range(stretches):
-        old = blocks_ref[r].reshape(length, 2 * hd)
-        ks[r], vs[r] = blend(old, fresh_ref[0, r], fresh_ref[1, r], row_ref[r : r + 1, 0:PAD])
     top[...] = jnp.full_like(top, -jnp.inf)
     low[...] = jnp.zeros_like(low)
     out[...] = jnp.zeros_like(out)
@@ -317,7 +314,7 @@
         pltpu.make_async_copy(slice_of(i * SIDE + y), acts.at[i, y], loc.at[5 + i]).start()
 
     def place_of(i, r):
-        return table_ref[req_ref[i, r]]
+        return table_ref[req_ref[r, i]]
 
     my_owner = [place_of(me, r) // 8 for r in range(8)]
     my_rank = [sum([(my_owner[q] == my_owner[r]).astype(jnp.int32) for q in range(r)], 0) for r in range(8)]
@@ -348,15 +345,16 @@
     def _(o):
         hop1_from(o).wait_recv()
 
-    @pl.loop(0, owners)
-    def _(i):
+    def sort(i):
         for r in range(8):
             hop_out[i, r] = hop_in[place_of(i, r)]
 
     @pl.loop(1, owners)
     def _(o):
+        sort(lax.rem(me + o, owners))
         hop2(o).start()
 
+    sort(me)
     own_out = pltpu.make_async_copy(hop_out.at[me], blocks.at[:, me, core], loc.at[4])
     own_out.start()
 
@@ -414,19 +412,6 @@
     acc[y] += product(2 - 2 * core, y)
     acc[y] += product(3 - 2 * core, y)
 
-    def core_swap(which):
-        return remote(
-            blocks.at[:, :, which], blocks.at[:, :, which], x_send.at[0], x_recv.at[0], partner
-        )
-
-    own_out.wait()
-
-    @pl.loop(1, owners)
-    def _(o):
-        hop2_from(o).wait_recv()
-
-    core_swap(core).start()
-
     for d in steps:
         remote(part.at[d], sums.at[d], s_send.at[d], s_recv.at[d], (x * SIDE + ring(y, SIDE - d), head)).wait_recv()
         acc[y] += sums[d].astype(F32)
@@ -438,7 +423,7 @@
     for r in range(8):
         lines = slice(per * r, per * (r + 1))
         for j in range(heads):
-            at_row = (r * heads + j) * per
+            at_row = (j // 2 * 16 + r * 2 + j % 2) * per
             qs[at_row : at_row + per, :] = acc[y, lines, j * hd : (j + 1) * hd] + bias[:, j * hd : (j + 1) * hd]
         fpad[r * PAD : r * PAD + per, :] = acc[y, lines, q_cols:width] + kv_bias
         fpad[r * PAD + per : (r + 1) * PAD, :] = jnp.zeros((PAD - per, hd), F32)
@@ -473,36 +458,57 @@
     for m in range(2):
         f_in[2 * me + m] = f_out[2 * me + m]
 
+    def core_swap(which):
+        return remote(
+            blocks.at[:, :, which], blocks.at[:, :, which], x_send.at[0], x_recv.at[0], partner
+        )
+
+    own_out.wait()
+
+    @pl.loop(1, owners)
+    def _(o):
+        hop2_from(o).wait_recv()
+
+    core_swap(core).start()
+
+    ow_blocks.forward()
     core_swap(1 - core).wait_recv()
     remote(fresh.at[1 - core], fresh.at[1 - core], x_send.at[1], x_recv.at[1], partner).wait_recv()
 
-    attend(queries, fresh, blocks, my_rows, ctx, ks, vs, sc, top, low, res, flat)
-
-    def ctx_to(d):
+    for r in range(8):
+        old_rows = blocks[r].reshape(ks.shape[1], 2 * hd)
+        ks[r], vs[r] = blend(old_rows, fresh[0, r], fresh[1, r], my_rows[r : r + 1, 0:PAD])
+
+    def ctx_to(d, pair):
         to = ring(y, d)
         return remote(
-            ctx, ctxs.at[y // 2, core], t_send.at[d], t_recv.at[d, core], (x * SIDE + to, 2 * z + lax.rem(y, 2))
-        )
-
-    def ctx_from(d, which):
+            ctx.at[pair], ctxs.at[y // 2, core, pair], t_send.at[d, pair], t_recv.at[d, core, pair],
+            (x * SIDE + to, 2 * z + lax.rem(y, 2)),
+        )
+
+    def ctx_from(d, which, pair):
         src = ring(y, SIDE - d)
-        place = ctxs.at[src // 2, which]
-        return remote(place, place, t_send.at[d], t_recv.at[d, which], (x * SIDE + src, 2 * z + which))
-
-    for d in (RIGHT, LEFT, OPPOSITE):
-        ctx_to(d).start()
+        place = ctxs.at[src // 2, which, pair]
+        return remote(
+            place, place, t_send.at[d, pair], t_recv.at[d, which, pair], (x * SIDE + src, 2 * z + which)
+        )
 
     mine = lax.rem(y, 2) == core
 
-    @pl.when(mine)
-    def _():
-        ctxs[y // 2, core] = ctx[...]
-
-    @pl.when(jnp.logical_not(mine))
-    def _():
-        ctx_to(0).start()
-
-    ow_blocks.forward()
+    for pair in (0, 1):
+        lines = pl.ds(pair * queries.shape[0] // 2, queries.shape[0] // 2)
+        attend(queries.at[lines], my_rows, ctx.at[pair], ks, vs, sc, top, low, res, flat)
+        for d in (RIGHT, LEFT, OPPOSITE):
+            ctx_to(d, pair).start()
+
+        @pl.when(mine)
+        def _():
+            ctxs[y // 2, core, pair] = ctx[pair]
+
+        @pl.when(jnp.logical_not(mine))
+        def _():
+            ctx_to(0, pair).start()
+
     ow_blocks.wait_rest()
     block_from(RIGHT, core).start()
     block_from(LEFT, core).start()
@@ -518,15 +524,17 @@
 
     @pl.when(mine)
     def _():
-        ctx_from(0, 1 - core).wait_recv()
-        for which in (0, 1):
-            ctx_from(OPPOSITE, which).wait_recv()
+        for pair in (0, 1):
+            ctx_from(0, 1 - core, pair).wait_recv()
+            for which in (0, 1):
+                ctx_from(OPPOSITE, which, pair).wait_recv()
 
     @pl.when(jnp.logical_not(mine))
     def _():
         for d in (RIGHT, LEFT):
             for which in (0, 1):
-                ctx_from(d, which).wait_recv()
+                for pair in (0, 1):
+                    ctx_from(d, which, pair).wait_recv()
 
     ow_blocks.wait_opposite()
     block_from(OPPOSITE, core).start()
@@ -539,8 +547,12 @@
     def compute(n):
         target = lax.rem(z + order[n] + levels, levels)
         column, request = target // 2, lax.rem(target, 2)
-        chunk[n] = jnp.dot(ctxs[request, 0], ow[0, column], preferred_element_type=F32)
-        chunk[n] += jnp.dot(ctxs[request, 1], ow[1, column], preferred_element_type=F32)
+        total = None
+        for which in (0, 1):
+            both = jnp.concatenate([ctxs[request, which, 0], ctxs[request, which, 1]], axis=1)
+            term = jnp.dot(both, ow[which, column], preferred_element_type=F32)
+            total = term if total is None else total + term
+        chunk[n] = total
 
     def lines_of(half):
         return slice(half * hrow, (half + 1) * hrow)
@@ -633,7 +645,8 @@
                 downward(step, d).wait_send()
     for d in steps:
         sums_to(d).wait_send()
-        ctx_to(d).wait_send()
+        for pair in (0, 1):
+            ctx_to(d, pair).wait_send()
     weights.finish()
     ow_blocks.finish()
     for d in (0,) + steps:
@@ -641,7 +654,8 @@
 
     @pl.when(jnp.logical_not(mine))
     def _():
-        ctx_to(0).wait_send()
+        for pair in (0, 1):
+            ctx_to(0, pair).wait_send()
 
     @pl.loop(1, owners)
     def _(o):
@@ -729,14 +743,14 @@
             pltpu.VMEM((stretches, owners, 2, piece, kv_width), BF16),
             pltpu.VMEM((stretches, length, hd), BF16),
             pltpu.VMEM((stretches, length, hd), BF16),
-            pltpu.VMEM((rows * heads * (stretches + 1) // 2, length), F32),
-            pltpu.VMEM((rows * heads, hd), F32),
-            pltpu.VMEM((rows * heads, hd), F32),
-            pltpu.VMEM((rows * heads, hd), F32),
-            pltpu.VMEM((rows, q_cols), F32),
-            pltpu.VMEM((rows, q_cols), BF16),
+            pltpu.VMEM((rows * heads * (stretches + 1) // 4, length), F32),
+            pltpu.VMEM((rows * heads // 2, hd), F32),
+            pltpu.VMEM((rows * heads // 2, hd), F32),
+            pltpu.VMEM((rows * heads // 2, hd), F32),
+            pltpu.VMEM((rows, q_cols // 2), F32),
+            pltpu.VMEM((2, rows, q_cols // 2), BF16),
             pltpu.VMEM((2, SIDE, depth, q_cols), BF16),
-            pltpu.VMEM((2, 2, rows, q_cols), BF16),
+            pltpu.VMEM((2, 2, 2, rows, q_cols // 2), BF16),
             pltpu.VMEM((levels, rows, q_cols), F32),
             pltpu.VMEM((4, rows, q_cols), BF16),
             pltpu.VMEM((4, rows, q_cols), BF16),
@@ -771,8 +785,8 @@
             dma((SIDE, 2)),
             dma((SIDE,)),
             dma((SIDE,)),
-            dma((SIDE,)),
             dma((SIDE, 2)),
+            dma((SIDE, 2, 2)),
             dma((4, 2)),
             dma((4, 2)),
             dma((4, 2)),
@@ -784,7 +798,7 @@
         compiler_params=pltpu.CompilerParams(collective_id=0, has_side_effects=True, vmem_limit_bytes=58 << 20),
         name="prefill",
     )(
-        stretch_place, req_stretches, hidden, norm_gain, q_weight, kv_weight, q_bias, kv_bias, out_weight, store, rec_rows
+        stretch_place, req_stretches.T, hidden, norm_gain, q_weight, kv_weight, q_bias, kv_bias, out_weight, store, rec_rows
     )
     return pl.pallas_call(
         hand_over,

time: 120 us -> 120 us (level)
  local copies, waits for them, and re-layouts: 1.36 us -> 0 us
    unnamed x1 -> x0, local copies, waits for them, and re-layouts: 1.36 us -> none
where the time goes in v9:
time: 120 us; the launch traced here: 118 us
  Pallas kernels  117 us (98%)
    pallas_call x1, Pallas kernels, shards(): pl.pallas_call(prefill, out_shape=(jax.ShapeDtypeStruct((rows, q_cols), B...  114 us
    pallas_call x1, Pallas kernels, shards(): pl.pallas_call(hand_over, out_shape=(jax.ShapeDtypeStruct((rows, q_cols),...  2.47 us

profile of v9, /device:TPU:34, one launch (start us, length us, event | category | flops | bytes accessed | tf_op | source)
XLA Modules:
  0.0 117.6 jit_solution(563724396669435693)
XLA Ops:
  0.6 114.4 %prefill.1 = (bf16[192,512]{1,0:T(8,128)(2,1)}, bf16[8,512,256]{2,1,0:T(8,128)(2,1)}) custom-call(s32[128]{0:T(128)} %table_ref.1, s32[8,16]{1,0:T(8,128)} %bitcast.3, bf16[192,8192]{1,0:T(8,128)(2,1)} %hid_hbm.1, bf16[8192]{0:T(1024)(128)(2,1)} %gain_ref.1, bf16[512,512]{1,0:T(8,128)(2,1)} %qw_hbm.1, bf16[512,2048]{1,0:T(8,128)(2,1)} %kvw_hbm.1, ...), custom_call_target="tpu_custom_call" | custom-call | tf_op jit(solution)/shard_map/prefill/pallas_call | solution.py:719
  115.1 2.5 %hand_over.1 = (bf16[192,512]{1,0:T(8,128)(2,1)}, bf16[8,1,512,256]{3,2,1,0:T(8,128)(2,1)}) custom-call(bf16[192,512]{1,0:T(8,128)(2,1)} %get-tuple-element.4.out_ref, bf16[8,512,256]{2,1,0:T(8,128)(2,1)} %get-tuple-element.5.store_ref), custom_call_target="tpu_custom_call" | custom-call | tf_op jit(solution)/shard_map/hand_over/pallas_call | solution.py:803

commit v10 on v9

--- a/solution.py
+++ b/solution.py
@@ -93,7 +93,7 @@
     hid, acts, w, acc, part, sums, hop_in, hop_out, qs, fpad, my_rows, slot_rows,
     queries, own_fresh, fresh, blocks, ks, vs, sc, top, low, res, flat, ctx,
     ow, ctxs, chunk, r_out, l_out, r_in, l_in, done, f_out, f_in, back, old, new,
-    loc, w_send, w_recv, a_send, a_recv, zr_send, zr_recv, zl_send, zl_recv, c_send, c_recv, s_send, s_recv,
+    loc, w_send, w_recv, a_send, a_recv, c_send, c_recv, s_send, s_recv,
     h1_send, h1_recv, h2_send, h2_recv, x_send, x_recv,
     o_send, o_recv, oo_send, oo_recv, t_send, t_recv,
     r_send, r_recv, l_send, l_recv, f_send, f_recv, n_sem,
@@ -161,51 +161,12 @@
     def slice_of(c):
         return hid.at[:, pl.ds(pl.multiple_of(c * depth, depth), depth)]
 
-    few = rows // 4
-
-    def eighth(level, d):
-        lines = pl.ds(pl.multiple_of(level // 2 * few, few), few)
-        return acts.at[2 * core + lax.rem(level, 2), ring(y, SIDE - d), lines]
-
-    def rows_to(d):
+    def rows_to(d, i):
         to = ring(y, d)
-        lines = pl.ds(pl.multiple_of(z // 2 * few, few), few)
-        column = ((2 * core + lax.rem(z, 2)) * SIDE + to) * depth
-        return remote(
-            hid.at[lines, pl.ds(pl.multiple_of(column, depth), depth)], acts.at[2 * core + lax.rem(z, 2), y, lines],
-            a_send.at[d], a_recv.at[d], (x * SIDE + to, head),
-        )
-
-    def rows_from(d):
-        place = eighth(z, d)
-        return remote(place, place, a_send.at[d], a_recv.at[d], (x * SIDE + ring(y, SIDE - d), head))
-
-    def upward(step, d, arriving=False):
-        place = eighth(lax.rem(z + levels + 1 - step - (1 if arriving else 0), levels), d)
-        return remote(place, place, zr_send.at[step, d], zr_recv.at[step, d], right)
-
-    def downward(step, d, arriving=False):
-        place = eighth(lax.rem(z - 1 + step + (1 if arriving else 0), levels), d)
-        return remote(place, place, zl_send.at[step, d], zl_recv.at[step, d], left)
-
-    def goes_up(step, d):
-        return step < 4 or d != LEFT
-
-    def goes_down(step, d):
-        return step < 4 or d == LEFT
-
-    def level_step(step):
-        for d in steps:
-            if step == 1:
-                rows_from(d).wait_recv()
-            else:
-                upward(step - 1, d, True).wait_recv()
-            if goes_up(step, d):
-                upward(step, d).start()
-            if step > 1:
-                downward(step - 1, d, True).wait_recv()
-            if goes_down(step, d):
-                downward(step, d).start()
+        return remote(
+            slice_of((2 * core + i) * SIDE + to), acts.at[2 * core + i, y], a_send.at[d, i], a_recv.at[d, i],
+            (x * SIDE + to, head),
+        )
 
     def hop1(o):
         to = lax.rem(me + o, owners)
@@ -306,8 +267,9 @@
             g = gain_ref[c * depth : (c + 1) * depth].astype(F32).reshape(1, depth)
             hid[lines, c * depth : (c + 1) * depth] = (v * factor * g).astype(BF16)
 
-    for d in steps:
-        rows_to(d).start()
+    for i in (0, 1):
+        for d in steps:
+            rows_to(d, i).start()
     weights.rest()
 
     for i in range(SIDE):
@@ -334,10 +296,21 @@
         rank = sum([((q < r) & (place_of(i, q) // 8 == me)).astype(jnp.int32) for q in range(8)], 0)
         picks.append(2 * i + jnp.minimum(rank, 1))
 
-    level_step(1)
     weights.forward()
 
-    level_step(2)
+    def rows_from(d, i, which):
+        src = ring(y, SIDE - d)
+        place = acts.at[2 * which + i, src]
+        return remote(place, place, a_send.at[d, i], a_recv.at[d, i], (x * SIDE + src, head))
+
+    def rows_over(d, i, which):
+        place = acts.at[2 * which + i, ring(y, SIDE - d)]
+        return remote(place, place, c_send.at[d, i], c_recv.at[d, i], partner)
+
+    for i in (0, 1):
+        for d in steps:
+            rows_from(d, i, core).wait_recv()
+            rows_over(d, i, core).start()
 
     own_hop.wait()
 
@@ -357,22 +330,6 @@
     sort(me)
     own_out = pltpu.make_async_copy(hop_out.at[me], blocks.at[:, me, core], loc.at[4])
     own_out.start()
-
-    level_step(3)
-    level_step(4)
-    for d in steps:
-        if goes_up(4, d):
-            upward(4, d, True).wait_recv()
-        if goes_down(4, d):
-            downward(4, d, True).wait_recv()
-
-    def rows_over(d, i, which):
-        place = acts.at[2 * which + i, ring(y, SIDE - d)]
-        return remote(place, place, c_send.at[d, i], c_recv.at[d, i], partner)
-
-    for i in (0, 1):
-        for d in steps:
-            rows_over(d, i, core).start()
 
     for i in range(SIDE):
         pltpu.make_async_copy(slice_of(i * SIDE + y), acts.at[i, y], loc.at[5 + i]).wait()
@@ -522,6 +479,17 @@
     swap_back = remote(back.at[core], back.at[core], x_send.at[2], x_recv.at[2], partner)
     swap_back.start()
 
+    def renew(s):
+        keys, values = blend(old[s].reshape(new.shape[1], 2 * hd), back[0, s], back[1, s], slot_rows[s : s + 1, 0:PAD])
+        new[s, :, 0:hd] = keys
+        new[s, :, hd : 2 * hd] = values
+        pltpu.make_async_copy(new.at[s], new_hbm.at[s], n_sem.at[s]).start()
+
+    old_in.wait()
+    remote(back.at[1 - core], back.at[1 - core], x_send.at[2], x_recv.at[2], partner).wait_recv()
+    for s in range(8):
+        renew(s)
+
     @pl.when(mine)
     def _():
         for pair in (0, 1):
@@ -571,12 +539,6 @@
 
     def leftward(step, half):
         return ring_copy(step, half, l_out, l_in, l_send, l_recv, left)
-
-    def renew(s):
-        keys, values = blend(old[s].reshape(new.shape[1], 2 * hd), back[0, s], back[1, s], slot_rows[s : s + 1, 0:PAD])
-        new[s, :, 0:hd] = keys
-        new[s, :, hd : 2 * hd] = values
-        pltpu.make_async_copy(new.at[s], new_hbm.at[s], n_sem.at[s]).start()
 
     compute(0)
     r_out[0, lines_of(0), :] = chunk[0, lines_of(0), :].astype(BF16)
@@ -601,14 +563,9 @@
                 value += l_in[step - 1, lines_of(left_half), :].astype(F32)
             l_out[step, lines_of(left_half), :] = value.astype(BF16)
             leftward(step, left_half).start()
-        if step == 1:
-            old_in.wait()
-            remote(back.at[1 - core], back.at[1 - core], x_send.at[2], x_recv.at[2], partner).wait_recv()
         if step < 3:
             compute(2 * step + 1)
             compute(2 * step + 2)
-            for s in range(4 * step - 4, 4 * step):
-                renew(s)
         else:
             compute(7)
 
@@ -635,14 +592,8 @@
 
     for i in (0, 1):
         for d in steps:
+            rows_to(d, i).wait_send()
             rows_over(d, i, core).wait_send()
-    for d in steps:
-        rows_to(d).wait_send()
-        for step in (1, 2, 3, 4):
-            if goes_up(step, d):
-                upward(step, d).wait_send()
-            if goes_down(step, d):
-                downward(step, d).wait_send()
     for d in steps:
         sums_to(d).wait_send()
         for pair in (0, 1):
@@ -765,12 +716,8 @@
             dma((7 + SIDE,)),
             dma((SIDE, 2)),
             dma((SIDE, 2)),
-            dma((SIDE,)),
-            dma((SIDE,)),
-            dma((SIDE + 1, SIDE)),
-            dma((SIDE + 1, SIDE)),
-            dma((SIDE + 1, SIDE)),
-            dma((SIDE + 1, SIDE)),
+            dma((SIDE, 2)),
+            dma((SIDE, 2)),
             dma((SIDE, 2)),
             dma((SIDE, 2)),
             dma((SIDE,)),

time: 120 us -> 118 us (0.983); the launches traced: 118 us -> 117 us
  no operation moved by 1% of the time
where the time goes in v10:
time: 118 us; the launch traced here: 117 us
  Pallas kernels  117 us (99%)
    pallas_call x1, Pallas kernels, shards(): pl.pallas_call(prefill, out_shape=(jax.ShapeDtypeStruct((rows, q_cols), B...  114 us
    pallas_call x1, Pallas kernels, shards(): pl.pallas_call(hand_over, out_shape=(jax.ShapeDtypeStruct((rows, q_cols),...  2.47 us

profile of v10, /device:TPU:34, one launch (start us, length us, event | category | flops | bytes accessed | tf_op | source)
XLA Modules:
  0.0 117.5 jit_solution(1978828371219644381)
XLA Ops:
  0.6 114.4 %prefill.1 = (bf16[192,512]{1,0:T(8,128)(2,1)}, bf16[8,512,256]{2,1,0:T(8,128)(2,1)}) custom-call(s32[128]{0:T(128)} %table_ref.1, s32[8,16]{1,0:T(8,128)} %bitcast.3, bf16[192,8192]{1,0:T(8,128)(2,1)} %hid_hbm.1, bf16[8192]{0:T(1024)(128)(2,1)} %gain_ref.1, bf16[512,512]{1,0:T(8,128)(2,1)} %qw_hbm.1, bf16[512,2048]{1,0:T(8,128)(2,1)} %kvw_hbm.1, ...), custom_call_target="tpu_custom_call" | custom-call | tf_op jit(solution)/shard_map/prefill/pallas_call | solution.py:670
  115.0 2.5 %hand_over.1 = (bf16[192,512]{1,0:T(8,128)(2,1)}, bf16[8,1,512,256]{3,2,1,0:T(8,128)(2,1)}) custom-call(bf16[192,512]{1,0:T(8,128)(2,1)} %get-tuple-element.4.out_ref, bf16[8,512,256]{2,1,0:T(8,128)(2,1)} %get-tuple-element.5.store_ref), custom_call_target="tpu_custom_call" | custom-call | tf_op jit(solution)/shard_map/hand_over/pallas_call | solution.py:750

commit v11 on v10

--- a/solution.py
+++ b/solution.py
@@ -243,13 +243,13 @@
     ow_blocks = Ring4(ow_hbm, lambda i: ow.at[core, i], o_send, o_recv)
 
     steps = (RIGHT, LEFT, OPPOSITE)
+    @pl.loop(1, owners)
+    def _(o):
+        hop1(o).start()
+
     own_q.wait()
     own_kv.wait()
     weights.start()
-
-    @pl.loop(1, owners)
-    def _(o):
-        hop1(o).start()
 
     own_hid.wait()
     tall = 16

time: 118 us -> 119 us (level)
  no operation moved by 1% of the time
where the time goes in v11:
time: 119 us; the launch traced here: 118 us
  Pallas kernels  117 us (98%)
    pallas_call x1, Pallas kernels, shards(): pl.pallas_call(prefill, out_shape=(jax.ShapeDtypeStruct((rows, q_cols), B...  115 us
    pallas_call x1, Pallas kernels, shards(): pl.pallas_call(hand_over, out_shape=(jax.ShapeDtypeStruct((rows, q_cols),...  2.47 us

profile of v11, /device:TPU:34, one launch (start us, length us, event | category | flops | bytes accessed | tf_op | source)
XLA Modules:
  0.0 118.0 jit_solution(4953983123878257279)
XLA Ops:
  0.6 114.9 %prefill.1 = (bf16[192,512]{1,0:T(8,128)(2,1)}, bf16[8,512,256]{2,1,0:T(8,128)(2,1)}) custom-call(s32[128]{0:T(128)} %table_ref.1, s32[8,16]{1,0:T(8,128)} %bitcast.3, bf16[192,8192]{1,0:T(8,128)(2,1)} %hid_hbm.1, bf16[8192]{0:T(1024)(128)(2,1)} %gain_ref.1, bf16[512,512]{1,0:T(8,128)(2,1)} %qw_hbm.1, bf16[512,2048]{1,0:T(8,128)(2,1)} %kvw_hbm.1, ...), custom_call_target="tpu_custom_call" | custom-call | tf_op jit(solution)/shard_map/prefill/pallas_call | solution.py:670
  115.5 2.5 %hand_over.1 = (bf16[192,512]{1,0:T(8,128)(2,1)}, bf16[8,1,512,256]{3,2,1,0:T(8,128)(2,1)}) custom-call(bf16[192,512]{1,0:T(8,128)(2,1)} %get-tuple-element.4.out_ref, bf16[8,512,256]{2,1,0:T(8,128)(2,1)} %get-tuple-element.5.store_ref), custom_call_target="tpu_custom_call" | custom-call | tf_op jit(solution)/shard_map/hand_over/pallas_call | solution.py:750
